TPU v7x, 512 devices: a whole 4x8x8 slice. The times are simulated.
512 devices in a mesh: lag: 64 (over y, x, core), row: 8 (over z).
Axes of the slice: x: 4, y: 8, z: 8, core: 2. Of those that a mesh axis runs over, the one named last changes fastest.
Arguments:
- blocks: bfloat16 [128, 2048, 2048], P('lag', 'row'), may hold values from -0.03125 to 0.03125
- history: bfloat16 [128, 2048, 128], P('lag'), may hold values from -6 to 6
- excitation: float32 [2, 2048, 128], P(None, 'row'), may hold values from -6 to 6
- self_inverse: float32 [2048, 2048], P('lag', 'row'), may hold values from -2 to 2
Outputs:
- currents: float32 [2, 2048, 128], P(None, 'lag')
All inputs are finite; a program needn't handle non-finite values.
Results may differ from a plain program's by a relative error of at most 0.0003.
Values may be sent and summed in bfloat16 or wider, within the bound.
No kernel may reach another device: no remote copies, remote signals or barrier semaphores. Data moves between devices by JAX's collectives and lax.ppermute only.
A program may use at most 64 MiB of HBM per device.

v0:
```python
import jax
import jax.numpy as jnp
from jax import lax
from jax.sharding import PartitionSpec as P

STEPS = 2


def shifted(block, axis, distance):
    devices = range(lax.axis_size(axis))
    route = [(i - distance, i) for i in devices if i - distance in devices]
    return lax.ppermute(block, axis, route)


def cut_along(array, dim, size):
    dims = array.shape
    pieces = array.reshape(*dims[:dim], size, dims[dim] // size, *dims[dim + 1 :])
    return jnp.moveaxis(pieces, dim, 0)


def sum_at_owner(array, axis, dim):
    size = lax.axis_size(axis)
    pieces = lax.all_to_all(cut_along(array, dim, size), axis, 0, 0, tiled=True)
    return jnp.sum(pieces, axis=0)


def laid_out(pieces, dim):
    dims = list(pieces.shape[1:])
    dims[dim] *= pieces.shape[0]
    return jnp.moveaxis(pieces, 0, dim).reshape(dims)


def from_everyone(array, axis):
    copies = jnp.broadcast_to(array, (lax.axis_size(axis), *array.shape))
    return lax.all_to_all(copies, axis, split_axis=0, concat_axis=0, tiled=True)


def gather_directly(array, axis, dim):
    return laid_out(from_everyone(array, axis), dim)


def of_everyone(array, axis):
    everything = from_everyone(array, axis)
    return jnp.sum(everything, axis=0)


def shards(blocks, history, excitation, self_inverse):
    lag_index = lax.axis_index("lag")
    lag_dev = blocks.shape[0]
    past = history
    reach = (STEPS - 2) // lag_dev + 1
    pieces = [history]
    pieces.insert(0, shifted(history, "lag", 1))
    window = jnp.concatenate(pieces, axis=0)
    fresh = []
    results = []
    for marker in range(STEPS):
        if marker > 0:
            stacked = jnp.stack(fresh[::-1])
            chosen = []
            for offset in range(lag_dev):
                lag_pos = lag_index * lag_dev + offset
                older = window[offset - marker + lag_dev * reach]
                recent = lax.dynamic_index_in_dim(
                    stacked, jnp.minimum(lag_pos, marker - 1), 0, keepdims=False
                )
                chosen.append(jnp.where(lag_pos < marker, recent, older))
            past = jnp.stack(chosen)
        partial_value = jnp.einsum("lpq,lqc->pc", blocks, past, preferred_element_type=jnp.float32)
        shares = sum_at_owner(partial_value, "lag", 0)
        count = shares.shape[0]
        local_field = lax.dynamic_slice_in_dim(excitation[marker], lag_index * count, count, 0)
        residual = gather_directly(local_field - shares, "lag", 0)
        term = jnp.dot(
            self_inverse,
            residual,
            precision=lax.Precision.HIGHEST,
            preferred_element_type=jnp.float32,
        )
        solved = of_everyone(term, "row")
        results.append(solved)
        if marker + 1 < STEPS:
            newest = gather_directly(solved.astype(jnp.bfloat16), "lag", 0)
            fresh.append(newest)
    return jnp.stack(results)


def solution(mesh):
    return jax.shard_map(
        shards,
        mesh=mesh,
        in_specs=(
            P("lag", "row", None),
            P("lag", None, None),
            P(None, "row", None),
            P("lag", "row"),
        ),
        out_specs=P(None, "lag", None),
        check_vma=False,
    )
```

profile of v0, /device:TPU:1, one launch (start us, length us, event | category | flops | bytes accessed | tf_op | source)
XLA Modules:
  0.0 138.4 jit_solution(1551905702277198034)
XLA Ops:
  0.0 1.7 %copy-done = bf16[2,256,2048]{2,1,0:T(8,128)(2,1)S(1)} copy-done((bf16[2,256,2048]{2,1,0:T(8,128)(2,1)S(1)}, bf16[2,256,2048]{2,1,0:T(8,128)(2,1)}, u32[]{:S(2)}) %copy-start) | copy-done | bytes 2097176
  1.7 2.6 %fusion.5 = f32[256,128,1]{1,0,2:T(8,128)} fusion(bf16[2,256,2048]{2,1,0:T(8,128)(2,1)S(1)} %copy-done, bf16[2,2048,128]{2,1,0:T(8,128)(2,1)} %param.5), kind=kOutput, calls=%fused_computation.13 | convolution fusion | flops 268435456 | bytes 3276800 | tf_op jit(solution)/shard_map/lpq,lqc->pc/dot_general | solution.py:69
  4.2 11.6 %all-to-all-start = ((f32[64,4,128]{2,1,0:T(4,128)}), f32[64,4,128]{2,1,0:T(4,128)S(1)}, u32[]{:S(2)}, u32[]{:S(2)}) async-start(f32[64,4,128]{2,1,0:T(4,128)} %bitcast.2), calls=%async_computation | async-start | bytes 262144 | tf_op jit(solution)/shard_map/all_to_all | solution.py:23
  15.9 0.7 fusion.4
  16.6 10.4 %all-to-all-done = f32[64,4,128]{2,1,0:T(4,128)S(1)} async-done(((f32[64,4,128]{2,1,0:T(4,128)}), f32[64,4,128]{2,1,0:T(4,128)S(1)}, u32[]{:S(2)}, u32[]{:S(2)}) %all-to-all-start) | async-done | bytes 131104 | tf_op jit(solution)/shard_map/all_to_all | solution.py:23
  27.1 0.7 bitcast_subtract_fusion.1
  27.8 14.9 %all_to_all.35 = f32[64,4,128]{2,1,0:T(4,128)S(1)} all-to-all(f32[64,4,128]{2,1,0:T(4,128)S(1)} %broadcast_in_dim.15), channel_id=1, replica_groups=mesh['lag'=64,'row'=8] {'lag'}, dimensions={0} | all-to-all | bytes 262144 | tf_op jit(solution)/shard_map/all_to_all | solution.py:35
  42.7 0.9 convolution_bitcast_fusion.2
  43.6 0.7 broadcast_in_dim.16
  44.3 10.0 %all-to-all-start.2 = ((f32[8,32,128]{2,1,0:T(8,128)}), f32[8,32,128]{2,1,0:T(8,128)S(1)}, u32[]{:S(2)}, u32[]{:S(2)}) async-start(f32[8,32,128]{2,1,0:T(8,128)} %broadcast_in_dim.16), calls=%async_computation.2 | async-start | bytes 262144 | tf_op jit(solution)/shard_map/all_to_all | solution.py:35
  54.4 1.3 copy.13
  55.7 2.8 %collective-permute-start = (bf16[2,2048,128]{1,2,0:T(8,128)(2,1)}, bf16[2,2048,128]{1,2,0:T(8,128)(2,1)}, u32[]{:S(2)}, u32[]{:S(2)}) collective-permute-start(bf16[2,2048,128]{1,2,0:T(8,128)(2,1)} %copy.13), channel_id=1, source_target_pairs={{0,8},{8,16},{16,24},{24,32},{32,40},{40,48},{48,56},{56,64},{64,7... | collective-permute-start | bytes 3145736 | tf_op jit(solution)/shard_map/ppermute | solution.py:12
  58.5 3.7 %all-to-all-done.2 = f32[8,32,128]{2,1,0:T(8,128)S(1)} async-done(((f32[8,32,128]{2,1,0:T(8,128)}), f32[8,32,128]{2,1,0:T(8,128)S(1)}, u32[]{:S(2)}, u32[]{:S(2)}) %all-to-all-start.2) | async-done | bytes 131104 | tf_op jit(solution)/shard_map/all_to_all | solution.py:35
  62.2 0.9 broadcast_in_dim.17
  63.1 7.0 %all-to-all-start.3 = ((bf16[64,32,128]{2,1,0:T(8,128)(2,1)}), bf16[64,32,128]{2,1,0:T(8,128)(2,1)}, u32[]{:S(2)}, u32[]{:S(2)}) async-start(bf16[64,32,128]{2,1,0:T(8,128)(2,1)} %broadcast_in_dim.17), calls=%async_computation.3 | async-start | bytes 1048576 | tf_op jit(solution)/shard_map/all_to_all | solution.py:35
  70.1 17.7 %all-to-all-done.3 = bf16[64,32,128]{2,1,0:T(8,128)(2,1)} async-done(((bf16[64,32,128]{2,1,0:T(8,128)(2,1)}), bf16[64,32,128]{2,1,0:T(8,128)(2,1)}, u32[]{:S(2)}, u32[]{:S(2)}) %all-to-all-start.3) | async-done | bytes 524320 | tf_op jit(solution)/shard_map/all_to_all | solution.py:35
  87.9 2.0 %copy.14 = bf16[1,2048,128]{1,2,0:T(8,128)(2,1)} copy(bf16[1,2048,128]{2,1,0:T(8,128)(2,1)} %bitcast.7) | data formatting | bytes 1048576 | tf_op jit(solution)/shard_map/jit(dynamic_index_in_dim)/squeeze | solution.py:64
  89.9 1.3 slice_select_fusion.1
  91.2 0.8 convolution_bitcast_fusion
  92.1 16.6 %all_to_all.36 = f32[64,4,128]{2,1,0:T(4,128)S(1)} all-to-all(f32[64,4,128]{2,1,0:T(4,128)S(1)} %bitcast.29), channel_id=1, replica_groups=mesh['lag'=64,'row'=8] {'lag'}, dimensions={0} | all-to-all | bytes 262144 | tf_op jit(solution)/shard_map/all_to_all | solution.py:23
  108.9 0.7 bitcast_subtract_fusion
  109.6 14.9 %all_to_all.37 = f32[64,4,128]{2,1,0:T(4,128)S(1)} all-to-all(f32[64,4,128]{2,1,0:T(4,128)S(1)} %broadcast_in_dim.18), channel_id=1, replica_groups=mesh['lag'=64,'row'=8] {'lag'}, dimensions={0} | all-to-all | bytes 262144 | tf_op jit(solution)/shard_map/all_to_all | solution.py:35
  124.7 13.1 %all_to_all.38 = f32[8,32,128]{2,1,0:T(8,128)S(1)} all-to-all(f32[8,32,128]{2,1,0:T(8,128)S(1)} %broadcast_in_dim.19), channel_id=1, replica_groups=mesh['lag'=64,'row'=8] {'row'}, dimensions={0} | all-to-all | bytes 262144 | tf_op jit(solution)/shard_map/all_to_all | solution.py:35
  137.8 0.6 pad_maximum_fusion
  (20 shorter events, 0.5 us)
Async XLA Ops:
  0.0 1.7 %copy-start = (bf16[2,256,2048]{2,1,0:T(8,128)(2,1)S(1)}, bf16[2,256,2048]{2,1,0:T(8,128)(2,1)}, u32[]{:S(2)}) copy-start(bf16[2,256,2048]{2,1,0:T(8,128)(2,1)} %param.4) | copy-start | bytes 6291460
  0.0 54.4 %copy-start.1 = (bf16[2,2048,128]{2,1,0:T(8,128)(2,1)S(1)}, bf16[2,2048,128]{2,1,0:T(8,128)(2,1)}, u32[]{:S(2)}) copy-start(bf16[2,2048,128]{2,1,0:T(8,128)(2,1)} %param.5) | copy-start | bytes 3145732
  0.0 15.9 %copy-start.3 = (f32[2,256,128]{2,1,0:T(8,128)S(1)}, f32[2,256,128]{2,1,0:T(8,128)}, u32[]{:S(2)}) copy-start(f32[2,256,128]{2,1,0:T(8,128)} %param.6) | copy-start | bytes 786436
  4.2 22.7 %all-to-all-start = ((f32[64,4,128]{2,1,0:T(4,128)}), f32[64,4,128]{2,1,0:T(4,128)S(1)}, u32[]{:S(2)}, u32[]{:S(2)}) async-start(f32[64,4,128]{2,1,0:T(4,128)} %bitcast.2), calls=%async_computation | async-start | bytes 262144 | tf_op jit(solution)/shard_map/all_to_all | solution.py:23
  44.3 17.9 %all-to-all-start.2 = ((f32[8,32,128]{2,1,0:T(8,128)}), f32[8,32,128]{2,1,0:T(8,128)S(1)}, u32[]{:S(2)}, u32[]{:S(2)}) async-start(f32[8,32,128]{2,1,0:T(8,128)} %broadcast_in_dim.16), calls=%async_computation.2 | async-start | bytes 262144 | tf_op jit(solution)/shard_map/all_to_all | solution.py:35
  55.7 34.2 %copy-start.2 = (bf16[2,2048,128]{1,2,0:T(8,128)(2,1)S(1)}, bf16[2,2048,128]{1,2,0:T(8,128)(2,1)}, u32[]{:S(2)}) copy-start(bf16[2,2048,128]{1,2,0:T(8,128)(2,1)} %copy.13) | copy-start | bytes 3145732
  55.7 34.2 %collective-permute-start = (bf16[2,2048,128]{1,2,0:T(8,128)(2,1)}, bf16[2,2048,128]{1,2,0:T(8,128)(2,1)}, u32[]{:S(2)}, u32[]{:S(2)}) collective-permute-start(bf16[2,2048,128]{1,2,0:T(8,128)(2,1)} %copy.13), channel_id=1, source_target_pairs={{0,8},{8,16},{16,24},{24,32},{32,40},{40,48},{48,56},{56,64},{64,7... | collective-permute-start | bytes 3145736 | tf_op jit(solution)/shard_map/ppermute | solution.py:12
  63.1 24.8 %all-to-all-start.3 = ((bf16[64,32,128]{2,1,0:T(8,128)(2,1)}), bf16[64,32,128]{2,1,0:T(8,128)(2,1)}, u32[]{:S(2)}, u32[]{:S(2)}) async-start(bf16[64,32,128]{2,1,0:T(8,128)(2,1)} %broadcast_in_dim.17), calls=%async_computation.3 | async-start | bytes 1048576 | tf_op jit(solution)/shard_map/all_to_all | solution.py:35
  91.2 33.3 %copy-start.4 = (f32[32,256]{1,0:T(8,128)S(1)}, f32[32,256]{1,0:T(8,128)}, u32[]{:S(2)}) copy-start(f32[32,256]{1,0:T(8,128)} %param.7) | copy-start | bytes 98308
where the time goes:
time: 139 us; the launch traced here: 138 us
  blocking collectives  59.5 us (43%)
  waiting for transfers between devices  31.9 us (23%)
  starting transfers between devices  31.5 us (23%)
  local copies, waits for them, and re-layouts  7.42 us (5%)
  matrix products  4.53 us (3%)
  other arithmetic  3.46 us (2%)
    all_to_all x3, blocking collectives, from_everyone(): return lax.all_to_all(copies, axis, split_axis=0, concat_axis=0, tiled=True)  42.9 us
    all_to_all x2, waiting for transfers between devices, from_everyone(): return lax.all_to_all(copies, axis, split_axis=0, concat_axis=0, tiled=True)  21.5 us
    all_to_all x2, starting transfers between devices, from_everyone(): return lax.all_to_all(copies, axis, split_axis=0, concat_axis=0, tiled=True)  17 us
    all_to_all x1, blocking collectives, sum_at_owner(): pieces = lax.all_to_all(cut_along(array, dim, size), axis, 0, 0, tiled=True)  16.6 us
    all_to_all x1, starting transfers between devices, sum_at_owner(): pieces = lax.all_to_all(cut_along(array, dim, size), axis, 0, 0, tiled=True)  11.6 us
    all_to_all x1, waiting for transfers between devices, sum_at_owner(): pieces = lax.all_to_all(cut_along(array, dim, size), axis, 0, 0, tiled=True)  10.4 us
    dot_general x2, matrix products, shards(): jnp.einsum('lpq,lqc->pc', blocks, past, preferred_element_type=jnp.float32)  3.4 us
    unnamed x11, local copies, waits for them, and re-layouts  2.99 us
  transfers between devices with their start and end apart: 4, of which 3 were waited for; matrix products, arithmetic and copies ran while one was open for 4% of the time, Pallas kernels for 0%

commit v1 on v0

v1 whole, which is shorter than its diff:
```python
import numpy as np
import jax
import jax.numpy as jnp
from jax import lax
from jax.sharding import Mesh, PartitionSpec as P

LAG = ("y", "x", "core")
W = ("x", "core")
F32 = jnp.float32


def exchange(array, axes):
    n = lax.axis_size(axes)
    copies = jnp.broadcast_to(array, (n, *array.shape))
    return lax.all_to_all(copies, axes, 0, 0, tiled=True)


def all_sum(array, axes):
    return jnp.sum(exchange(array, axes), axis=0)


def scatter_sum(pieces, axes):
    return jnp.sum(lax.all_to_all(pieces, axes, 0, 0, tiled=True), axis=0)


def times(left, right, precision=None):
    return lax.dot_general(
        left, right, (((1,), (1,)), ((), ())), precision=precision, preferred_element_type=F32
    )


def shards(blocks, history, excitation, self_inverse):
    ny, nw, nz = lax.axis_size("y"), lax.axis_size(W), lax.axis_size("row")
    iy, iz = lax.axis_index("y"), lax.axis_index("row")
    rows, size = blocks.shape[1:]
    columns = history.shape[2]
    cy = columns // ny
    own = self_inverse.shape[0]
    nlag = ny * nw

    first = blocks[0].reshape(rows, ny, nw, own).transpose(2, 0, 1, 3).reshape(nw, rows, ny * own)
    first = lax.all_to_all(first, W, 0, 0, tiled=True)[0]
    first = lax.all_to_all(first.reshape(ny, rows // ny, ny * own), "y", 0, 0, tiled=True)[0]
    first = exchange(first, "y").reshape(rows, ny * own)

    inverse = exchange(self_inverse, "y").reshape(ny * own, rows)

    before = lax.ppermute(history[1], LAG, [(i, i + 1) for i in range(nlag - 1)])
    field = excitation.transpose(0, 2, 1)
    field = lax.dynamic_slice_in_dim(field, iy * cy, cy, 1)

    part0 = jnp.einsum("lpq,lqc->cp", blocks, history, preferred_element_type=F32)
    part0 = scatter_sum(part0.reshape(ny, cy, rows), "y")
    past1 = jnp.stack([before, history[0]])
    part1 = jnp.einsum("lpq,lqc->cp", blocks, past1, preferred_element_type=F32)
    part1 = scatter_sum(part1.reshape(ny, cy, rows), "y")

    resid0 = field[0] - all_sum(part0, W)
    cur0 = all_sum(times(resid0, inverse, lax.Precision.HIGHEST), "row")
    part1 = part1 + times(cur0.astype(jnp.bfloat16), first)
    resid1 = field[1] - all_sum(part1, W)
    term1 = times(resid1, inverse, lax.Precision.HIGHEST)

    cz = cy // nz
    mine0 = lax.dynamic_slice_in_dim(cur0, iz * cz, cz, 0)
    both = jnp.concatenate([term1, mine0], axis=0)
    both = both.reshape(cy + cz, ny, own).transpose(1, 0, 2).reshape(ny, 1, (cy + cz) * own)
    both = jnp.broadcast_to(both, (ny, nz, (cy + cz) * own)).reshape(ny * nz, (cy + cz) * own)
    got = lax.all_to_all(both, ("y", "row"), 0, 0, tiled=True).reshape(ny, nz, cy + cz, own)
    out1 = jnp.sum(got[:, :, :cy], axis=1).reshape(columns, own)
    out0 = got[:, :, cy:].reshape(columns, own)
    return jnp.stack([out0.T, out1.T])


def solution(mesh):
    n_row = mesh.shape["row"]
    fine = Mesh(np.asarray(mesh.devices).reshape(-1, 4, 2, n_row), ("y", "x", "core", "row"))
    return jax.shard_map(
        shards,
        mesh=fine,
        in_specs=(
            P(LAG, "row", None),
            P(LAG, None, None),
            P(None, "row", None),
            P(LAG, "row"),
        ),
        out_specs=P(None, LAG, None),
        check_vma=False,
    )
```

time: 139 us -> 157 us (1.13)
  blocking collectives: 59.5 us -> 42.6 us
  waiting for transfers between devices: 31.9 us -> 47 us
  starting transfers between devices: 31.5 us -> 46.2 us
  local copies, waits for them, and re-layouts: 7.42 us -> 11.7 us
  matrix products: 4.53 us -> 6.86 us
  other arithmetic: 3.46 us -> 1.19 us
    all_to_all x4 -> x3, blocking collectives: 59.5 us -> 42.6 us  [the longest x1 15.6 us: shards(): lax.all_to_all(both, ('y', 'row'), 0, 0, tiled=True)]
    all_to_all x3 -> x7, waiting for transfers between devices: 31.9 us -> 47 us  [the longest x4 27.2 us: exchange(): return lax.all_to_all(copies, axes, 0, 0, tiled=True)]
    all_to_all x3 -> x7, starting transfers between devices: 28.7 us -> 42.7 us  [the longest x4 26.9 us: exchange(): return lax.all_to_all(copies, axes, 0, 0, tiled=True)]
    dot_general x4 -> x5, matrix products: 4.53 us -> 6.86 us  [the longest x1 2.77 us: shards(): jnp.einsum('lpq,lqc->cp', blocks, history, preferred_element_type=F32)]
    squeeze x1, local copies, waits for them, and re-layouts: 2.03 us -> 0.01 us  [shards(): lax.all_to_all(first.reshape(ny, rows // ny, ny * own), 'y', 0, 0, tiled=...]
    slice x1 -> x6, local copies, waits for them, and re-layouts: 0.72 us -> 2.57 us  [the longest x2 1.67 us: shards(): first = lax.all_to_all(first, W, 0, 0, tiled=True)[0]]
    unnamed x11 -> x14, local copies, waits for them, and re-layouts: 2.99 us -> 4.47 us
  transfers between devices with their start and end apart: 4 -> 8, of which waited for: 3 -> 7; matrix products, arithmetic and copies ran while one was open for 4% -> 8% of each run, Pallas kernels for 0% -> 0%
where the time goes in v1:
time: 157 us; the launch traced here: 156 us
  waiting for transfers between devices  47 us (30%)
  starting transfers between devices  46.2 us (29%)
  blocking collectives  42.6 us (27%)
  local copies, waits for them, and re-layouts  11.7 us (7%)
  matrix products  6.86 us (4%)
    all_to_all x4, waiting for transfers between devices, exchange(): return lax.all_to_all(copies, axes, 0, 0, tiled=True)  27.2 us
    all_to_all x4, starting transfers between devices, exchange(): return lax.all_to_all(copies, axes, 0, 0, tiled=True)  26.9 us
    all_to_all x1, blocking collectives, shards(): lax.all_to_all(both, ('y', 'row'), 0, 0, tiled=True)  15.6 us
    all_to_all x1, blocking collectives, scatter_sum(): return jnp.sum(lax.all_to_all(pieces, axes, 0, 0, tiled=True), axis=0)  15.5 us
    all_to_all x1, blocking collectives, exchange(): return lax.all_to_all(copies, axes, 0, 0, tiled=True)  11.5 us
    all_to_all x1, waiting for transfers between devices, scatter_sum(): return jnp.sum(lax.all_to_all(pieces, axes, 0, 0, tiled=True), axis=0)  7.82 us
    all_to_all x1, waiting for transfers between devices, shards(): first = lax.all_to_all(first, W, 0, 0, tiled=True)[0]  6.75 us
    all_to_all x1, starting transfers between devices, shards(): first = lax.all_to_all(first, W, 0, 0, tiled=True)[0]  6.38 us
  transfers between devices with their start and end apart: 8, of which 7 were waited for; matrix products, arithmetic and copies ran while one was open for 8% of the time, Pallas kernels for 0%

profile of v1, /device:TPU:1, one launch (start us, length us, event | category | flops | bytes accessed | tf_op | source)
XLA Modules:
  0.0 155.8 jit_solution(1895114335898515078)
XLA Ops:
  0.0 2.8 %fusion.15 = f32[128,256,1]{1,0,2:T(8,128)S(1)} fusion(bf16[2,2048,128]{2,1,0:T(8,128)(2,1)} %param.5, bf16[2,256,2048]{2,1,0:T(8,128)(2,1)} %param.4), kind=kOutput, calls=%fused_computation.23 | convolution fusion | flops 268435456 | bytes 3276800 | tf_op jit(solution)/shard_map/lpq,lqc->cp/dot_general | solution.py:52
  2.8 15.5 %all_to_all.54 = f32[8,16,256]{2,1,0:T(8,128)S(1)} all-to-all(f32[8,16,256]{2,1,0:T(8,128)S(1)} %bitcast.56), channel_id=1, replica_groups=mesh['y'=8,'x'=4,'core'=2,'row'=8] {'y'}, dimensions={0} | all-to-all | bytes 262144 | tf_op jit(solution)/shard_map/all_to_all | solution.py:23
  18.3 11.5 %all_to_all.55 = f32[8,16,256]{2,1,0:T(8,128)S(1)} all-to-all(f32[8,16,256]{2,1,0:T(8,128)S(1)} %broadcast_in_dim.22), channel_id=1, replica_groups=mesh['y'=8,'x'=4,'core'=2,'row'=8] {'x','core'}, dimensions={0} | all-to-all | bytes 262144 | tf_op jit(solution)/shard_map/all_to_all | solution.py:15
  30.5 3.4 %all-to-all-start.3 = ((f32[8,32,256]{2,1,0:T(8,128)}), f32[8,32,256]{2,1,0:T(8,128)S(1)}, u32[]{:S(2)}, u32[]{:S(2)}) async-start(f32[8,32,256]{2,1,0:T(8,128)} %broadcast_in_dim.23), calls=%async_computation.3 | async-start | bytes 524288 | tf_op jit(solution)/shard_map/all_to_all | solution.py:15
  34.5 1.1 copy.38
  35.6 8.8 %all-to-all-done.3 = f32[8,32,256]{2,1,0:T(8,128)S(1)} async-done(((f32[8,32,256]{2,1,0:T(8,128)}), f32[8,32,256]{2,1,0:T(8,128)S(1)}, u32[]{:S(2)}, u32[]{:S(2)}) %all-to-all-start.3) | async-done | bytes 262176 | tf_op jit(solution)/shard_map/all_to_all | solution.py:15
  44.4 6.4 %all-to-all-start.5 = ((bf16[8,256,256]{1,2,0:T(8,128)(2,1)}), bf16[8,256,256]{1,2,0:T(8,128)(2,1)}, u32[]{:S(2)}, u32[]{:S(2)}) async-start(bf16[8,256,256]{1,2,0:T(8,128)(2,1)} %bitcast.12), calls=%async_computation.5 | async-start | bytes 2097152 | tf_op jit(solution)/shard_map/all_to_all | solution.py:42
  51.7 2.2 %copy.45 = bf16[1,2048,128]{1,2,0:T(8,128)(2,1)} copy(bf16[1,2048,128]{2,1,0:T(8,128)(2,1)} %get-tuple-element.5) | data formatting | bytes 1048576
  53.9 3.5 %collective-permute-start = (bf16[2048,128]{0,1:T(8,128)(2,1)}, bf16[2048,128]{0,1:T(8,128)(2,1)}, u32[]{:S(2)}, u32[]{:S(2)}) collective-permute-start(bf16[2048,128]{0,1:T(8,128)(2,1)} %bitcast.57), channel_id=1, source_target_pairs={{0,8},{8,16},{16,24},{24,32},{32,40},{40,48},{48,56},{56,64},{64,7... | collective-permute-start | bytes 1572872 | tf_op jit(solution)/shard_map/ppermute | solution.py:48
  58.3 1.0 fusion.5
  59.3 6.7 %all-to-all-done.5 = bf16[8,256,256]{1,2,0:T(8,128)(2,1)} async-done(((bf16[8,256,256]{1,2,0:T(8,128)(2,1)}), bf16[8,256,256]{1,2,0:T(8,128)(2,1)}, u32[]{:S(2)}, u32[]{:S(2)}) %all-to-all-start.5) | async-done | bytes 1048608 | tf_op jit(solution)/shard_map/all_to_all | solution.py:42
  66.7 10.0 %all-to-all-start.4 = ((f32[8,16,256]{2,1,0:T(8,128)}), f32[8,16,256]{2,1,0:T(8,128)S(1)}, u32[]{:S(2)}, u32[]{:S(2)}) async-start(f32[8,16,256]{2,1,0:T(8,128)} %broadcast_in_dim.24), calls=%async_computation.4 | async-start | bytes 262144 | tf_op jit(solution)/shard_map/all_to_all | solution.py:15
  76.7 1.0 copy.46
  79.4 5.3 %all-to-all-done.4 = f32[8,16,256]{2,1,0:T(8,128)S(1)} async-done(((f32[8,16,256]{2,1,0:T(8,128)}), f32[8,16,256]{2,1,0:T(8,128)S(1)}, u32[]{:S(2)}, u32[]{:S(2)}) %all-to-all-start.4) | async-done | bytes 131104 | tf_op jit(solution)/shard_map/all_to_all | solution.py:15
  84.7 6.1 %all-to-all-start.6 = ((bf16[8,32,256]{2,1,0:T(8,128)(2,1)}), bf16[8,32,256]{2,1,0:T(8,128)(2,1)S(1)}, u32[]{:S(2)}, u32[]{:S(2)}) async-start(bf16[8,32,256]{2,1,0:T(8,128)(2,1)} %bitcast.13), calls=%async_computation.6 | async-start | bytes 262144 | tf_op jit(solution)/shard_map/all_to_all | solution.py:43
  90.8 2.7 %fusion = f32[128,256,1]{1,0,2:T(8,128)} fusion(bf16[2,256,2048]{2,1,0:T(8,128)(2,1)S(1)} %copy-done.1, bf16[1,2048,128]{1,2,0:T(8,128)(2,1)} %copy.46, bf16[1,2048,128]{1,2,0:T(8,128)(2,1)} %bitcast.2), kind=kOutput, calls=%fused_computation.1 | convolution fusion | flops 268959744 | bytes 3276800 | tf_op jit(solution)/shard_map/lpq,lqc->cp/dot_general | solution.py:55
  93.5 5.3 %all-to-all-done.6 = bf16[8,32,256]{2,1,0:T(8,128)(2,1)S(1)} async-done(((bf16[8,32,256]{2,1,0:T(8,128)(2,1)}), bf16[8,32,256]{2,1,0:T(8,128)(2,1)S(1)}, u32[]{:S(2)}, u32[]{:S(2)}) %all-to-all-start.6) | async-done | bytes 131104 | tf_op jit(solution)/shard_map/all_to_all | solution.py:43
  98.8 3.4 %all-to-all-start = ((f32[8,16,256]{2,1,0:T(8,128)}), f32[8,16,256]{2,1,0:T(8,128)S(1)}, u32[]{:S(2)}, u32[]{:S(2)}) async-start(f32[8,16,256]{2,1,0:T(8,128)} %bitcast.4), calls=%async_computation | async-start | bytes 262144 | tf_op jit(solution)/shard_map/all_to_all | solution.py:23
  102.2 7.8 %all-to-all-done = f32[8,16,256]{2,1,0:T(8,128)S(1)} async-done(((f32[8,16,256]{2,1,0:T(8,128)}), f32[8,16,256]{2,1,0:T(8,128)S(1)}, u32[]{:S(2)}, u32[]{:S(2)}) %all-to-all-start) | async-done | bytes 131104 | tf_op jit(solution)/shard_map/all_to_all | solution.py:23
  110.7 3.4 %all-to-all-start.7 = ((bf16[8,32,256]{2,1,0:T(8,128)(2,1)}), bf16[8,32,256]{2,1,0:T(8,128)(2,1)S(1)}, u32[]{:S(2)}, u32[]{:S(2)}) async-start(bf16[8,32,256]{2,1,0:T(8,128)(2,1)} %broadcast_in_dim.25), calls=%async_computation.7 | async-start | bytes 262144 | tf_op jit(solution)/shard_map/all_to_all | solution.py:15
  114.1 7.8 %all-to-all-done.7 = bf16[8,32,256]{2,1,0:T(8,128)(2,1)S(1)} async-done(((bf16[8,32,256]{2,1,0:T(8,128)(2,1)}), bf16[8,32,256]{2,1,0:T(8,128)(2,1)S(1)}, u32[]{:S(2)}, u32[]{:S(2)}) %all-to-all-start.7) | async-done | bytes 131104 | tf_op jit(solution)/shard_map/all_to_all | solution.py:15
  122.7 10.1 %all-to-all-start.8 = ((f32[8,16,256]{2,1,0:T(8,128)}), f32[8,16,256]{2,1,0:T(8,128)S(1)}, u32[]{:S(2)}, u32[]{:S(2)}) async-start(f32[8,16,256]{2,1,0:T(8,128)} %broadcast_in_dim.26), calls=%async_computation.8 | async-start | bytes 262144 | tf_op jit(solution)/shard_map/all_to_all | solution.py:15
  132.8 5.3 %all-to-all-done.8 = f32[8,16,256]{2,1,0:T(8,128)S(1)} async-done(((f32[8,16,256]{2,1,0:T(8,128)}), f32[8,16,256]{2,1,0:T(8,128)S(1)}, u32[]{:S(2)}, u32[]{:S(2)}) %all-to-all-start.8) | async-done | bytes 131104 | tf_op jit(solution)/shard_map/all_to_all | solution.py:15
  138.8 15.6 %all_to_all.56 = f32[64,1,576]{2,1,0:T(1,128)S(1)} all-to-all(f32[64,1,576]{2,1,0:T(1,128)S(1)} %all_to_all.42), channel_id=1, replica_groups=mesh['y'=8,'x'=4,'core'=2,'row'=8] {'y','row'}, dimensions={0} | all-to-all | bytes 294912 | tf_op jit(solution)/shard_map/all_to_all | solution.py:69
  (46 shorter events, 9.0 us)
Async XLA Ops:
  0.0 57.4 %copy-start = (f32[2,256,128]{2,1,0:T(8,128)S(1)}, f32[2,256,128]{2,1,0:T(8,128)}, u32[]{:S(2)}) copy-start(f32[2,256,128]{2,1,0:T(8,128)} %param.6) | copy-start | bytes 786436
  0.0 29.8 %copy-start.4 = (f32[32,256]{1,0:T(8,128)S(1)}, f32[32,256]{1,0:T(8,128)}, u32[]{:S(2)}) copy-start(f32[32,256]{1,0:T(8,128)} %param.7) | copy-start | bytes 98308
  2.8 31.2 %slice-start = ((bf16[2,256,2048]{2,1,0:T(8,128)(2,1)}), bf16[1,256,2048]{2,1,0:T(8,128)(2,1)S(1)}, s32[]{:S(2)}) async-start(bf16[2,256,2048]{2,1,0:T(8,128)(2,1)} %param.4), calls=%async_computation.10 | async-start | bytes 2097152 | tf_op jit(solution)/shard_map/slice | solution.py:41
  30.5 13.9 %all-to-all-start.3 = ((f32[8,32,256]{2,1,0:T(8,128)}), f32[8,32,256]{2,1,0:T(8,128)S(1)}, u32[]{:S(2)}, u32[]{:S(2)}) async-start(f32[8,32,256]{2,1,0:T(8,128)} %broadcast_in_dim.23), calls=%async_computation.3 | async-start | bytes 524288 | tf_op jit(solution)/shard_map/all_to_all | solution.py:15
  34.5 16.3 %copy-start.2 = (bf16[2,2048,128]{2,1,0:T(8,128)(2,1)S(1)}, bf16[2,2048,128]{2,1,0:T(8,128)(2,1)}, u32[]{:S(2)}) copy-start(bf16[2,2048,128]{2,1,0:T(8,128)(2,1)} %param.5) | copy-start | bytes 3145732
  44.4 21.6 %all-to-all-start.5 = ((bf16[8,256,256]{1,2,0:T(8,128)(2,1)}), bf16[8,256,256]{1,2,0:T(8,128)(2,1)}, u32[]{:S(2)}, u32[]{:S(2)}) async-start(bf16[8,256,256]{1,2,0:T(8,128)(2,1)} %bitcast.12), calls=%async_computation.5 | async-start | bytes 2097152 | tf_op jit(solution)/shard_map/all_to_all | solution.py:42
  51.7 39.1 %copy-start.1 = (bf16[2,256,2048]{2,1,0:T(8,128)(2,1)S(1)}, bf16[2,256,2048]{2,1,0:T(8,128)(2,1)}, u32[]{:S(2)}) copy-start(bf16[2,256,2048]{2,1,0:T(8,128)(2,1)} %param.4) | copy-start | bytes 6291460
  53.9 36.9 %collective-permute-start = (bf16[2048,128]{0,1:T(8,128)(2,1)}, bf16[2048,128]{0,1:T(8,128)(2,1)}, u32[]{:S(2)}, u32[]{:S(2)}) collective-permute-start(bf16[2048,128]{0,1:T(8,128)(2,1)} %bitcast.57), channel_id=1, source_target_pairs={{0,8},{8,16},{16,24},{24,32},{32,40},{40,48},{48,56},{56,64},{64,7... | collective-permute-start | bytes 1572872 | tf_op jit(solution)/shard_map/ppermute | solution.py:48
  66.7 18.0 %all-to-all-start.4 = ((f32[8,16,256]{2,1,0:T(8,128)}), f32[8,16,256]{2,1,0:T(8,128)S(1)}, u32[]{:S(2)}, u32[]{:S(2)}) async-start(f32[8,16,256]{2,1,0:T(8,128)} %broadcast_in_dim.24), calls=%async_computation.4 | async-start | bytes 262144 | tf_op jit(solution)/shard_map/all_to_all | solution.py:15
  84.7 14.1 %all-to-all-start.6 = ((bf16[8,32,256]{2,1,0:T(8,128)(2,1)}), bf16[8,32,256]{2,1,0:T(8,128)(2,1)S(1)}, u32[]{:S(2)}, u32[]{:S(2)}) async-start(bf16[8,32,256]{2,1,0:T(8,128)(2,1)} %bitcast.13), calls=%async_computation.6 | async-start | bytes 262144 | tf_op jit(solution)/shard_map/all_to_all | solution.py:43
  90.8 47.3 %copy-start.3 = (f32[2,256,16]{1,2,0:T(8,128)S(1)}, f32[2,256,16]{1,2,0:T(8,128)}, u32[]{:S(2)}) copy-start(f32[2,256,16]{1,2,0:T(8,128)} %copy.44) | copy-start | bytes 98308
  98.8 11.2 %all-to-all-start = ((f32[8,16,256]{2,1,0:T(8,128)}), f32[8,16,256]{2,1,0:T(8,128)S(1)}, u32[]{:S(2)}, u32[]{:S(2)}) async-start(f32[8,16,256]{2,1,0:T(8,128)} %bitcast.4), calls=%async_computation | async-start | bytes 262144 | tf_op jit(solution)/shard_map/all_to_all | solution.py:23
  110.7 11.2 %all-to-all-start.7 = ((bf16[8,32,256]{2,1,0:T(8,128)(2,1)}), bf16[8,32,256]{2,1,0:T(8,128)(2,1)S(1)}, u32[]{:S(2)}, u32[]{:S(2)}) async-start(bf16[8,32,256]{2,1,0:T(8,128)(2,1)} %broadcast_in_dim.25), calls=%async_computation.7 | async-start | bytes 262144 | tf_op jit(solution)/shard_map/all_to_all | solution.py:15
  122.7 15.3 %all-to-all-start.8 = ((f32[8,16,256]{2,1,0:T(8,128)}), f32[8,16,256]{2,1,0:T(8,128)S(1)}, u32[]{:S(2)}, u32[]{:S(2)}) async-start(f32[8,16,256]{2,1,0:T(8,128)} %broadcast_in_dim.26), calls=%async_computation.8 | async-start | bytes 262144 | tf_op jit(solution)/shard_map/all_to_all | solution.py:15

commit v2 on v1

v2 whole, which is shorter than its diff:
```python
import numpy as np
import jax
import jax.numpy as jnp
from jax import lax
from jax.sharding import Mesh, PartitionSpec as P

LAG = ("y", "x", "core")
W = ("x", "core")
F32 = jnp.float32
BF16 = jnp.bfloat16


def swap(pieces, axes):
    return lax.all_to_all(pieces, axes, 0, 0, tiled=True)


def everyone(array, axes):
    n = lax.axis_size(axes)
    return jnp.broadcast_to(array, (n, *array.shape))


def split(array):
    high = lax.reduce_precision(array, 8, 7)
    return high.astype(BF16), (array - high).astype(BF16)


def pair_sum(pieces):
    return jnp.sum(pieces.astype(F32), axis=0)


def times(left, right, precision=None):
    return lax.dot_general(
        left, right, (((1,), (1,)), ((), ())), precision=precision, preferred_element_type=F32
    )


def shards(blocks, history, excitation, self_inverse):
    ny, nx, nc, nz = (lax.axis_size(a) for a in ("y", "x", "core", "row"))
    nw = nx * nc
    ix, ic, iw, iz = (lax.axis_index(a) for a in ("x", "core", W, "row"))
    rows, size = blocks.shape[1:]
    columns = history.shape[2]
    cw = columns // nw
    own = self_inverse.shape[0]
    nlag = ny * nw
    cut = rows // nw
    span = nw * own

    whole = blocks[0]
    half = rows // nc
    mine = whole[:half]
    for c in range(1, nc):
        got = lax.ppermute(whole[c * half : (c + 1) * half], LAG, [(0, c)])
        mine = jnp.where(ic == c, got, mine)
    piece = mine[:cut]
    for k in range(1, nx):
        route = [(c, k * nc + c) for c in range(nc)]
        got = lax.ppermute(mine[k * cut : (k + 1) * cut], LAG, route)
        piece = jnp.where(ix == k, got, piece)

    before = lax.ppermute(history[1], LAG, [(i, i + 1) for i in range(nlag - 1)])
    field = excitation.transpose(0, 2, 1)
    field = lax.dynamic_slice_in_dim(field, iw * cw, cw, 1)

    part0 = jnp.einsum("lpq,lqc->cp", blocks, history, preferred_element_type=F32)
    send = jnp.concatenate([part0.reshape(nw, cw, rows), everyone(self_inverse, W)], axis=1)
    got = swap(send, W)
    part0 = jnp.sum(got[:, :cw], axis=0)
    inverse = got[:, cw:].reshape(span, rows)

    pair = everyone(jnp.concatenate(split(part0), axis=0), "y")
    piece = piece.reshape(cut, ny, span).transpose(1, 0, 2)
    got = swap(jnp.concatenate([pair, piece], axis=1), "y")
    resid0 = field[0] - pair_sum(got[:, :cw]) - pair_sum(got[:, cw : 2 * cw])
    piece = got[0, 2 * cw :]

    past1 = jnp.stack([before, history[0]])
    part1 = jnp.einsum("lpq,lqc->cp", blocks, past1, preferred_element_type=F32)
    high, low = split(part1.reshape(nw, cw, rows))
    got = swap(jnp.concatenate([high, low, everyone(piece, W)], axis=1), W)
    part1 = pair_sum(got[:, :cw]) + pair_sum(got[:, cw : 2 * cw])
    first = got[:, 2 * cw :].reshape(nx, nc, cut, span).swapaxes(0, 1).reshape(rows, span)

    term0 = times(resid0, inverse, lax.Precision.HIGHEST)
    cur0 = jnp.sum(swap(everyone(term0, "row"), "row"), axis=0)

    part1 = part1 + times(cur0.astype(BF16), first)
    resid1 = field[1] - jnp.sum(swap(everyone(part1, "y"), "y"), axis=0)
    term1 = times(resid1, inverse, lax.Precision.HIGHEST)

    cz = cw // nz
    mine0 = lax.dynamic_slice_in_dim(cur0, iz * cz, cz, 0)
    both = jnp.concatenate([term1, mine0], axis=0)
    both = both.reshape(cw + cz, nw, own).transpose(1, 0, 2).reshape(nw, 1, (cw + cz) * own)
    both = jnp.broadcast_to(both, (nw, nz, (cw + cz) * own)).reshape(nw * nz, (cw + cz) * own)
    got = swap(both, W + ("row",)).reshape(nw, nz, cw + cz, own)
    out1 = jnp.sum(got[:, :, :cw], axis=1).reshape(columns, own)
    out0 = got[:, :, cw:].reshape(columns, own)
    return jnp.stack([out0.T, out1.T])


def solution(mesh):
    n_row = mesh.shape["row"]
    fine = Mesh(np.asarray(mesh.devices).reshape(-1, 4, 2, n_row), ("y", "x", "core", "row"))
    return jax.shard_map(
        shards,
        mesh=fine,
        in_specs=(
            P(LAG, "row", None),
            P(LAG, None, None),
            P(None, "row", None),
            P(LAG, "row"),
        ),
        out_specs=P(None, LAG, None),
        check_vma=False,
    )
```

time: 157 us -> 113 us (0.72)
  blocking collectives: 42.6 us -> 17.1 us
  waiting for transfers between devices: 47 us -> 35.4 us
  starting transfers between devices: 46.2 us -> 39.6 us
  other arithmetic: 1.19 us -> 4.83 us
  local copies, waits for them, and re-layouts: 11.7 us -> 9.42 us
    all_to_all x3 -> x1, blocking collectives: 42.6 us -> 17.1 us  [swap(): return lax.all_to_all(pieces, axes, 0, 0, tiled=True)]
    all_to_all x7 -> x5, waiting for transfers between devices: 47 us -> 32 us  [swap(): return lax.all_to_all(pieces, axes, 0, 0, tiled=True)]
    all_to_all x7 -> x5, starting transfers between devices: 42.7 us -> 29.3 us  [swap(): return lax.all_to_all(pieces, axes, 0, 0, tiled=True)]
    ppermute x0 -> x4, starting transfers between devices: none -> 6.79 us  [the longest x3 5.38 us: shards(): got = lax.ppermute(mine[k * cut:(k + 1) * cut], LAG, route)]
    ppermute x0 -> x4, waiting for transfers between devices: none -> 3.48 us  [the longest x3 3.48 us: shards(): got = lax.ppermute(mine[k * cut:(k + 1) * cut], LAG, route)]
    unnamed x14, local copies, waits for them, and re-layouts: 4.47 us -> 2.49 us
  transfers between devices with their start and end apart: 8 -> 10, of which waited for: 7 -> 7; matrix products, arithmetic and copies ran while one was open for 8% -> 12% of each run, Pallas kernels for 0% -> 0%
where the time goes in v2:
time: 113 us; the launch traced here: 112 us
  starting transfers between devices  39.6 us (35%)
  waiting for transfers between devices  35.4 us (31%)
  blocking collectives  17.1 us (15%)
  local copies, waits for them, and re-layouts  9.42 us (8%)
  matrix products  5.3 us (5%)
  other arithmetic  4.83 us (4%)
    all_to_all x5, waiting for transfers between devices, swap(): return lax.all_to_all(pieces, axes, 0, 0, tiled=True)  32 us
    all_to_all x5, starting transfers between devices, swap(): return lax.all_to_all(pieces, axes, 0, 0, tiled=True)  29.3 us
    all_to_all x1, blocking collectives, swap(): return lax.all_to_all(pieces, axes, 0, 0, tiled=True)  17.1 us
    ppermute x3, starting transfers between devices, shards(): got = lax.ppermute(mine[k * cut:(k + 1) * cut], LAG, route)  5.38 us
    ppermute x1, starting transfers between devices, shards(): lax.ppermute(history[1], LAG, [(i, i + 1) for i in range(nlag - 1)])  3.54 us
    ppermute x3, waiting for transfers between devices, shards(): got = lax.ppermute(mine[k * cut:(k + 1) * cut], LAG, route)  3.48 us
    dot_general x1, matrix products, shards(): jnp.einsum('lpq,lqc->cp', blocks, history, preferred_element_type=F32)  2.73 us
    unnamed x14, local copies, waits for them, and re-layouts  2.49 us
  transfers between devices with their start and end apart: 10, of which 7 were waited for; matrix products, arithmetic and copies ran while one was open for 12% of the time, Pallas kernels for 0%

profile of v2, /device:TPU:1, one launch (start us, length us, event | category | flops | bytes accessed | tf_op | source)
XLA Modules:
  0.0 112.0 jit_solution(12290581456700746813)
XLA Ops:
  0.0 1.9 %slice_bitcast_fusion = bf16[128,2048]{1,0:T(8,128)(2,1)} fusion(bf16[2,256,2048]{2,1,0:T(8,128)(2,1)} %param.4), kind=kLoop, calls=%fused_computation.7 | loop fusion | bytes 1048576 | tf_op jit(solution)/shard_map/slice | solution.py:53
  1.9 1.4 %collective-permute-start.1 = (bf16[128,2048]{1,0:T(8,128)(2,1)}, bf16[128,2048]{1,0:T(8,128)(2,1)}, u32[]{:S(2)}, u32[]{:S(2)}) collective-permute-start(bf16[128,2048]{1,0:T(8,128)(2,1)} %slice_bitcast_fusion), channel_id=1, source_target_pairs={{0,8},{1,9},{2,10},{3,11},{4,12},{5,13},{6,14},{7,15}} | collective-permute-start | bytes 1572872 | tf_op jit(solution)/shard_map/ppermute | solution.py:53
  3.4 2.7 %fusion.22 = f32[128,256,1]{1,0,2:T(8,128)S(1)} fusion(bf16[2,2048,128]{2,1,0:T(8,128)(2,1)} %param.5, bf16[2,256,2048]{2,1,0:T(8,128)(2,1)} %param.4), kind=kOutput, calls=%fused_computation.46 | convolution fusion | flops 268435456 | bytes 3276800 | tf_op jit(solution)/shard_map/lpq,lqc->cp/dot_general | solution.py:65
  6.9 11.7 %all-to-all-start = ((f32[8,48,256]{2,1,0:T(8,128)}), f32[8,48,256]{2,1,0:T(8,128)}, u32[]{:S(2)}, u32[]{:S(2)}) async-start(f32[8,48,256]{2,1,0:T(8,128)} %pad_maximum_fusion), calls=%async_computation | async-start | bytes 786432 | tf_op jit(solution)/shard_map/all_to_all | solution.py:14
  18.6 1.0 fusion.20
  19.6 2.1 %copy.45 = bf16[1,2048,128]{1,2,0:T(8,128)(2,1)} copy(bf16[1,2048,128]{2,1,0:T(8,128)(2,1)} %get-tuple-element.9) | data formatting | bytes 1048576
  21.8 3.5 %collective-permute-start = (bf16[2048,128]{0,1:T(8,128)(2,1)}, bf16[2048,128]{0,1:T(8,128)(2,1)}, u32[]{:S(2)}, u32[]{:S(2)}) collective-permute-start(bf16[2048,128]{0,1:T(8,128)(2,1)} %bitcast.1), channel_id=1, source_target_pairs={{0,8},{8,16},{16,24},{24,32},{32,40},{40,48},{48,56},{56,64},{64,7... | collective-permute-start | bytes 1572872 | tf_op jit(solution)/shard_map/ppermute | solution.py:61
  25.8 1.0 all-to-all-done
  27.7 1.1 bitcast_select_fusion
  28.9 2.8 %collective-permute-start.2 = (bf16[32,2048]{1,0:T(8,128)(2,1)S(1)}, bf16[32,2048]{1,0:T(8,128)(2,1)S(1)}, u32[]{:S(2)}, u32[]{:S(2)}) collective-permute-start(bf16[32,2048]{1,0:T(8,128)(2,1)S(1)} %get-tuple-element.13), channel_id=1, source_target_pairs={{0,48},{8,56},{1,49},{9,57},{2,50},{10,58},{3,51},{11,59},{4,52},{... | collective-permute-start | bytes 393224 | tf_op jit(solution)/shard_map/ppermute | solution.py:58
  31.7 1.3 %collective-permute-start.3 = (bf16[32,2048]{1,0:T(8,128)(2,1)S(1)}, bf16[32,2048]{1,0:T(8,128)(2,1)S(1)}, u32[]{:S(2)}, u32[]{:S(2)}) collective-permute-start(bf16[32,2048]{1,0:T(8,128)(2,1)S(1)} %get-tuple-element.12), channel_id=1, source_target_pairs={{0,32},{8,40},{1,33},{9,41},{2,34},{10,42},{3,35},{11,43},{4,36},{... | collective-permute-start | bytes 393224 | tf_op jit(solution)/shard_map/ppermute | solution.py:58
  33.0 1.3 %collective-permute-start.4 = (bf16[32,2048]{1,0:T(8,128)(2,1)S(1)}, bf16[32,2048]{1,0:T(8,128)(2,1)S(1)}, u32[]{:S(2)}, u32[]{:S(2)}) collective-permute-start(bf16[32,2048]{1,0:T(8,128)(2,1)S(1)} %get-tuple-element.11), channel_id=1, source_target_pairs={{0,16},{8,24},{1,17},{9,25},{2,18},{10,26},{3,19},{11,27},{4,20},{... | collective-permute-start | bytes 393224 | tf_op jit(solution)/shard_map/ppermute | solution.py:58
  34.3 1.0 slice.103
  36.0 2.8 %collective-permute-done.4 = bf16[32,2048]{1,0:T(8,128)(2,1)S(1)} collective-permute-done((bf16[32,2048]{1,0:T(8,128)(2,1)S(1)}, bf16[32,2048]{1,0:T(8,128)(2,1)S(1)}, u32[]{:S(2)}, u32[]{:S(2)}) %collective-permute-start.4) | collective-permute-done | bytes 131104 | tf_op jit(solution)/shard_map/ppermute | solution.py:58
  39.7 3.4 %all-to-all-start.1 = ((bf16[8,64,256]{2,1,0:T(8,128)(2,1)}), bf16[8,64,256]{2,1,0:T(8,128)(2,1)S(1)}, u32[]{:S(2)}, u32[]{:S(2)}) async-start(bf16[8,64,256]{2,1,0:T(8,128)(2,1)} %copy.34), calls=%async_computation.1 | async-start | bytes 524288 | tf_op jit(solution)/shard_map/all_to_all | solution.py:14
  43.1 1.9 %fusion = f32[128,256,1]{1,0,2:T(8,128)S(1)} fusion(bf16[2,256,2048]{2,1,0:T(8,128)(2,1)S(1)} %copy-done.1, bf16[1,2048,128]{1,2,0:T(8,128)(2,1)S(1)} %copy.46, bf16[1,2048,128]{1,2,0:T(8,128)(2,1)} %bitcast.2), kind=kOutput, calls=%fused_computation.1 | convolution fusion | flops 268959744 | bytes 3276800 | tf_op jit(solution)/shard_map/lpq,lqc->cp/dot_general | solution.py:78
  45.0 8.9 %all-to-all-done.1 = bf16[8,64,256]{2,1,0:T(8,128)(2,1)S(1)} async-done(((bf16[8,64,256]{2,1,0:T(8,128)(2,1)}), bf16[8,64,256]{2,1,0:T(8,128)(2,1)S(1)}, u32[]{:S(2)}, u32[]{:S(2)}) %all-to-all-start.1) | async-done | bytes 262176 | tf_op jit(solution)/shard_map/all_to_all | solution.py:14
  54.6 5.7 %all-to-all-start.2 = ((bf16[8,64,256]{2,1,0:T(8,128)(2,1)}), bf16[8,64,256]{2,1,0:T(8,128)(2,1)S(1)}, u32[]{:S(2)}, u32[]{:S(2)}) async-start(bf16[8,64,256]{2,1,0:T(8,128)(2,1)} %pad_maximum_fusion.2), calls=%async_computation.2 | async-start | bytes 524288 | tf_op jit(solution)/shard_map/all_to_all | solution.py:14
  60.6 6.2 %all-to-all-done.2 = bf16[8,64,256]{2,1,0:T(8,128)(2,1)S(1)} async-done(((bf16[8,64,256]{2,1,0:T(8,128)(2,1)}), bf16[8,64,256]{2,1,0:T(8,128)(2,1)S(1)}, u32[]{:S(2)}, u32[]{:S(2)}) %all-to-all-start.2) | async-done | bytes 262176 | tf_op jit(solution)/shard_map/all_to_all | solution.py:14
  67.4 5.1 %all-to-all-start.3 = ((f32[8,16,256]{2,1,0:T(8,128)}), f32[8,16,256]{2,1,0:T(8,128)S(1)}, u32[]{:S(2)}, u32[]{:S(2)}) async-start(f32[8,16,256]{2,1,0:T(8,128)} %broadcast_in_dim.25), calls=%async_computation.3 | async-start | bytes 262144 | tf_op jit(solution)/shard_map/all_to_all | solution.py:14
  72.6 8.0 %all-to-all-done.3 = f32[8,16,256]{2,1,0:T(8,128)S(1)} async-done(((f32[8,16,256]{2,1,0:T(8,128)}), f32[8,16,256]{2,1,0:T(8,128)S(1)}, u32[]{:S(2)}, u32[]{:S(2)}) %all-to-all-start.3) | async-done | bytes 131104 | tf_op jit(solution)/shard_map/all_to_all | solution.py:14
  81.4 3.4 %all-to-all-start.4 = ((f32[8,16,256]{2,1,0:T(8,128)}), f32[8,16,256]{2,1,0:T(8,128)S(1)}, u32[]{:S(2)}, u32[]{:S(2)}) async-start(f32[8,16,256]{2,1,0:T(8,128)} %broadcast_in_dim.26), calls=%async_computation.4 | async-start | bytes 262144 | tf_op jit(solution)/shard_map/all_to_all | solution.py:14
  84.8 7.9 %all-to-all-done.4 = f32[8,16,256]{2,1,0:T(8,128)S(1)} async-done(((f32[8,16,256]{2,1,0:T(8,128)}), f32[8,16,256]{2,1,0:T(8,128)S(1)}, u32[]{:S(2)}, u32[]{:S(2)}) %all-to-all-start.4) | async-done | bytes 131104 | tf_op jit(solution)/shard_map/all_to_all | solution.py:14
  93.5 17.1 %all_to_all.34 = f32[64,1,576]{2,1,0:T(1,128)S(1)} all-to-all(f32[64,1,576]{2,1,0:T(1,128)S(1)} %all_to_all.26), channel_id=1, replica_groups=mesh['y'=8,'x'=4,'core'=2,'row'=8] {'x','core','row'}, dimensions={0} | all-to-all | bytes 294912 | tf_op jit(solution)/shard_map/all_to_all | solution.py:14
  (57 shorter events, 8.5 us)
Async XLA Ops:
  0.0 25.3 %copy-start = (f32[2,256,128]{2,1,0:T(8,128)S(1)}, f32[2,256,128]{2,1,0:T(8,128)}, u32[]{:S(2)}) copy-start(f32[2,256,128]{2,1,0:T(8,128)} %param.6) | copy-start | bytes 786436
  0.0 6.1 %copy-start.4 = (f32[32,256]{1,0:T(8,128)S(1)}, f32[32,256]{1,0:T(8,128)}, u32[]{:S(2)}) copy-start(f32[32,256]{1,0:T(8,128)} %param.7) | copy-start | bytes 98308
  1.9 16.7 %copy-start.2 = (bf16[2,2048,128]{2,1,0:T(8,128)(2,1)S(1)}, bf16[2,2048,128]{2,1,0:T(8,128)(2,1)}, u32[]{:S(2)}) copy-start(bf16[2,2048,128]{2,1,0:T(8,128)(2,1)} %param.5) | copy-start | bytes 3145732
  1.9 25.8 %collective-permute-start.1 = (bf16[128,2048]{1,0:T(8,128)(2,1)}, bf16[128,2048]{1,0:T(8,128)(2,1)}, u32[]{:S(2)}, u32[]{:S(2)}) collective-permute-start(bf16[128,2048]{1,0:T(8,128)(2,1)} %slice_bitcast_fusion), channel_id=1, source_target_pairs={{0,8},{1,9},{2,10},{3,11},{4,12},{5,13},{6,14},{7,15}} | collective-permute-start | bytes 1572872 | tf_op jit(solution)/shard_map/ppermute | solution.py:53
  6.9 19.9 %all-to-all-start = ((f32[8,48,256]{2,1,0:T(8,128)}), f32[8,48,256]{2,1,0:T(8,128)}, u32[]{:S(2)}, u32[]{:S(2)}) async-start(f32[8,48,256]{2,1,0:T(8,128)} %pad_maximum_fusion), calls=%async_computation | async-start | bytes 786432 | tf_op jit(solution)/shard_map/all_to_all | solution.py:14
  18.6 9.1 %copy-start.1 = (bf16[2,256,2048]{2,1,0:T(8,128)(2,1)S(1)}, bf16[2,256,2048]{2,1,0:T(8,128)(2,1)}, u32[]{:S(2)}) copy-start(bf16[2,256,2048]{2,1,0:T(8,128)(2,1)} %param.4) | copy-start | bytes 6291460
  19.6 5.9 %copy-start.3 = (bf16[1,2048,128]{2,1,0:T(8,128)(2,1)S(1)}, bf16[1,2048,128]{2,1,0:T(8,128)(2,1)}, u32[]{:S(2)}) copy-start(bf16[1,2048,128]{2,1,0:T(8,128)(2,1)} %get-tuple-element.10) | copy-start | bytes 1572868
  21.8 21.3 %collective-permute-start = (bf16[2048,128]{0,1:T(8,128)(2,1)}, bf16[2048,128]{0,1:T(8,128)(2,1)}, u32[]{:S(2)}, u32[]{:S(2)}) collective-permute-start(bf16[2048,128]{0,1:T(8,128)(2,1)} %bitcast.1), channel_id=1, source_target_pairs={{0,8},{8,16},{16,24},{24,32},{32,40},{40,48},{48,56},{56,64},{64,7... | collective-permute-start | bytes 1572872 | tf_op jit(solution)/shard_map/ppermute | solution.py:61
  28.9 6.4 %collective-permute-start.2 = (bf16[32,2048]{1,0:T(8,128)(2,1)S(1)}, bf16[32,2048]{1,0:T(8,128)(2,1)S(1)}, u32[]{:S(2)}, u32[]{:S(2)}) collective-permute-start(bf16[32,2048]{1,0:T(8,128)(2,1)S(1)} %get-tuple-element.13), channel_id=1, source_target_pairs={{0,48},{8,56},{1,49},{9,57},{2,50},{10,58},{3,51},{11,59},{4,52},{... | collective-permute-start | bytes 393224 | tf_op jit(solution)/shard_map/ppermute | solution.py:58
  31.7 4.3 %collective-permute-start.3 = (bf16[32,2048]{1,0:T(8,128)(2,1)S(1)}, bf16[32,2048]{1,0:T(8,128)(2,1)S(1)}, u32[]{:S(2)}, u32[]{:S(2)}) collective-permute-start(bf16[32,2048]{1,0:T(8,128)(2,1)S(1)} %get-tuple-element.12), channel_id=1, source_target_pairs={{0,32},{8,40},{1,33},{9,41},{2,34},{10,42},{3,35},{11,43},{4,36},{... | collective-permute-start | bytes 393224 | tf_op jit(solution)/shard_map/ppermute | solution.py:58
  33.0 5.8 %collective-permute-start.4 = (bf16[32,2048]{1,0:T(8,128)(2,1)S(1)}, bf16[32,2048]{1,0:T(8,128)(2,1)S(1)}, u32[]{:S(2)}, u32[]{:S(2)}) collective-permute-start(bf16[32,2048]{1,0:T(8,128)(2,1)S(1)} %get-tuple-element.11), channel_id=1, source_target_pairs={{0,16},{8,24},{1,17},{9,25},{2,18},{10,26},{3,19},{11,27},{4,20},{... | collective-permute-start | bytes 393224 | tf_op jit(solution)/shard_map/ppermute | solution.py:58
  39.7 14.2 %all-to-all-start.1 = ((bf16[8,64,256]{2,1,0:T(8,128)(2,1)}), bf16[8,64,256]{2,1,0:T(8,128)(2,1)S(1)}, u32[]{:S(2)}, u32[]{:S(2)}) async-start(bf16[8,64,256]{2,1,0:T(8,128)(2,1)} %copy.34), calls=%async_computation.1 | async-start | bytes 524288 | tf_op jit(solution)/shard_map/all_to_all | solution.py:14
  54.6 12.2 %all-to-all-start.2 = ((bf16[8,64,256]{2,1,0:T(8,128)(2,1)}), bf16[8,64,256]{2,1,0:T(8,128)(2,1)S(1)}, u32[]{:S(2)}, u32[]{:S(2)}) async-start(bf16[8,64,256]{2,1,0:T(8,128)(2,1)} %pad_maximum_fusion.2), calls=%async_computation.2 | async-start | bytes 524288 | tf_op jit(solution)/shard_map/all_to_all | solution.py:14
  67.4 13.1 %all-to-all-start.3 = ((f32[8,16,256]{2,1,0:T(8,128)}), f32[8,16,256]{2,1,0:T(8,128)S(1)}, u32[]{:S(2)}, u32[]{:S(2)}) async-start(f32[8,16,256]{2,1,0:T(8,128)} %broadcast_in_dim.25), calls=%async_computation.3 | async-start | bytes 262144 | tf_op jit(solution)/shard_map/all_to_all | solution.py:14
  81.4 11.3 %all-to-all-start.4 = ((f32[8,16,256]{2,1,0:T(8,128)}), f32[8,16,256]{2,1,0:T(8,128)S(1)}, u32[]{:S(2)}, u32[]{:S(2)}) async-start(f32[8,16,256]{2,1,0:T(8,128)} %broadcast_in_dim.26), calls=%async_computation.4 | async-start | bytes 262144 | tf_op jit(solution)/shard_map/all_to_all | solution.py:14

commit v3 on v2

v3 whole, which is shorter than its diff:
```python
import numpy as np
import jax
import jax.numpy as jnp
from jax import lax
from jax.experimental import pallas as pl
from jax.experimental.pallas import tpu as pltpu
from jax.sharding import Mesh, PartitionSpec as P

LAG = ("y", "x", "core")
W = ("x", "core")
F32 = jnp.float32
BF16 = jnp.bfloat16


def swap(pieces, axes):
    return lax.all_to_all(pieces, axes, 0, 0, tiled=True)


def call(body, outs, flops, *args, scratch=()):
    single = not isinstance(outs, list)
    outs = [outs] if single else outs
    shapes = [jax.ShapeDtypeStruct(s, d) for s, d in outs]
    size = sum(a.size * a.dtype.itemsize for a in args)
    size += sum(s.size * s.dtype.itemsize for s in shapes)
    spaces = [pltpu.SMEM if a.dtype == jnp.int32 else pltpu.VMEM for a in args]
    return pl.pallas_call(
        body,
        out_shape=shapes[0] if single else shapes,
        in_specs=[pl.BlockSpec(memory_space=m) for m in spaces],
        scratch_shapes=scratch,
        cost_estimate=pl.CostEstimate(flops=flops, bytes_accessed=size, transcendentals=0),
        compiler_params=pltpu.CompilerParams(vmem_limit_bytes=24 * 1024 * 1024),
    )(*args)


def mm(left, right, precision=None):
    return jnp.dot(left, right, precision=precision, preferred_element_type=F32)


def mm_t(left, right, precision=None):
    return lax.dot_general(
        left, right, (((1,), (1,)), ((), ())), precision=precision, preferred_element_type=F32
    )


def parts(array):
    high = array.astype(BF16)
    return high, (array - high.astype(F32)).astype(BF16)


def sum_first(ref, start, stop):
    total = ref[0, start:stop].astype(F32)
    for i in range(1, ref.shape[0]):
        total = total + ref[i, start:stop].astype(F32)
    return total


def sum_pairs(ref, start, count):
    return sum_first(ref, start, start + count) + sum_first(ref, start + count, start + 2 * count)


def first_sums(where, blocks, history, excitation, inverse, out, field, turned):
    nw = out.shape[0]
    total = mm(blocks[0], history[0]) + mm(blocks[1], history[1])
    total = total.T
    cw = total.shape[0] // nw
    for w in range(nw):
        out[w, :cw] = total[w * cw : (w + 1) * cw]
        out[w, cw:] = inverse[...]
    start = pl.multiple_of(where[1] * cw, cw)
    for s in range(excitation.shape[0]):
        turned[...] = excitation[s].T
        field[s] = turned[pl.ds(start, cw)]


def second_step(where, got, blocks, before, history, got1, got2, got3, out, later):
    ny, depth, span = out.shape
    cut = got1.shape[0]
    cw = (depth - cut) // 2
    high, low = parts(sum_first(got, 0, cw))
    piece = blocks[0, :cut]
    for k, other in enumerate((got1, got2, got3)):
        piece = jnp.where(where[0] == k + 1, other[...], piece)
    for y in range(ny):
        out[y, :cw] = high
        out[y, cw : 2 * cw] = low
        out[y, 2 * cw :] = piece[:, y * span : (y + 1) * span]
    later[...] = (mm(blocks[0], before[...]) + mm(blocks[1], history[0])).T


def third_step(got, later, out):
    nw = out.shape[0]
    cw = later.shape[0] // nw
    for w in range(nw):
        high, low = parts(later[w * cw : (w + 1) * cw])
        out[w, :cw] = high
        out[w, cw : 2 * cw] = low
        out[w, 2 * cw :] = got[0, 2 * cw :]


def fourth_step(got1, got2, got3, field, out, part1, first):
    nz, cw, rows = out.shape
    inverse = got1[:, cw:].reshape(-1, rows)
    resid = field[0] - sum_pairs(got2, 0, cw)
    term = mm_t(resid, inverse, lax.Precision.HIGHEST)
    for z in range(nz):
        out[z] = term
    part1[...] = sum_pairs(got3, 0, cw)
    cut = got3.shape[1] - 2 * cw
    for x in range(first.shape[0] // cut):
        first[x * cut : (x + 1) * cut] = got3[2 * x, 2 * cw :]


def fifth_step(where, got, part1, first, out, mine):
    value = sum_first(got, 0, got.shape[1])
    total = part1[...] + mm_t(value.astype(BF16), first[...])
    for y in range(out.shape[0]):
        out[y] = total
    cz = mine.shape[0]
    share = value[:cz]
    for z in range(1, value.shape[0] // cz):
        share = jnp.where(where[2] == z, value[z * cz : (z + 1) * cz], share)
    mine[...] = share


def sixth_step(got1, got, field, mine, out):
    cw = got.shape[1]
    inverse = got1[:, cw:].reshape(-1, got.shape[2])
    resid = field[1] - sum_first(got, 0, cw)
    out[:cw] = mm_t(resid, inverse, lax.Precision.HIGHEST)
    out[cw:] = mine[...]


def shards(blocks, history, excitation, self_inverse):
    ny, nx, nc, nz = (lax.axis_size(a) for a in ("y", "x", "core", "row"))
    nw = nx * nc
    ix, iw, iz = (lax.axis_index(a) for a in ("x", W, "row"))
    rows, size = blocks.shape[1:]
    columns = history.shape[2]
    cw = columns // nw
    own = self_inverse.shape[0]
    nlag = ny * nw
    cut = rows // nx
    span = nw * own
    work = 2 * rows * size * columns * 2
    small = 2 * cw * rows * span

    where = jnp.stack([ix, iw, iz]).astype(jnp.int32)

    pieces = []
    for k in range(1, nx):
        rows_of_k = blocks[0, k * cut : (k + 1) * cut]
        pieces.append(lax.ppermute(rows_of_k, LAG, [(0, k * nc)]))
    before = lax.ppermute(history[1], LAG, [(i, i + 1) for i in range(nlag - 1)])

    outs = [((nw, cw + own, rows), F32), ((2, cw, rows), F32)]
    turned = [pltpu.VMEM((columns, rows), F32)]
    args = where, blocks, history, excitation, self_inverse
    send, field = call(first_sums, outs, work, *args, scratch=turned)
    got1 = swap(send, W)
    outs = [((ny, 2 * cw + cut, span), BF16), ((columns, rows), F32)]
    args = where, got1, blocks, before, history, *pieces
    send, later = call(second_step, outs, work, *args)
    got2 = swap(send, "y")
    send = call(third_step, ((nw, 2 * cw + cut, rows), BF16), small, got2, later)
    got3 = swap(send, W)
    outs = [((nz, cw, rows), F32), ((cw, rows), F32), ((rows, span), BF16)]
    send, part1, first = call(fourth_step, outs, small, got1, got2, got3, field)
    got4 = swap(send, "row")
    cz = cw // nz
    outs = [((ny, cw, rows), F32), ((cz, span), F32)]
    send, mine0 = call(fifth_step, outs, small, where, got4, part1, first)
    got5 = swap(send, "y")
    both = call(sixth_step, ((cw + cz, span), F32), small, got1, got5, field, mine0)
    both = both.reshape(cw + cz, nw, own).transpose(1, 0, 2).reshape(nw, 1, (cw + cz) * own)
    both = jnp.broadcast_to(both, (nw, nz, (cw + cz) * own)).reshape(nw * nz, (cw + cz) * own)
    got = swap(both, W + ("row",)).reshape(nw, nz, cw + cz, own)
    out1 = jnp.sum(got[:, :, :cw], axis=1).reshape(columns, own)
    out0 = got[:, :, cw:].reshape(columns, own)
    return jnp.stack([out0.T, out1.T])


def solution(mesh):
    n_row = mesh.shape["row"]
    fine = Mesh(np.asarray(mesh.devices).reshape(-1, 4, 2, n_row), ("y", "x", "core", "row"))
    return jax.shard_map(
        shards,
        mesh=fine,
        in_specs=(
            P(LAG, "row", None),
            P(LAG, None, None),
            P(None, "row", None),
            P(LAG, "row"),
        ),
        out_specs=P(None, LAG, None),
        check_vma=False,
    )
```

time: 113 us -> 112 us (level)
  blocking collectives: 17.1 us -> 74.7 us
  waiting for transfers between devices: 35.4 us -> 2.65 us
  starting transfers between devices: 39.6 us -> 15.8 us
  matrix products: 5.3 us -> 0 us
  Pallas kernels: 0 us -> 4.6 us
  other arithmetic: 4.83 us -> 1.14 us
  local copies, waits for them, and re-layouts: 9.42 us -> 12.5 us
    all_to_all x1 -> x5, blocking collectives: 17.1 us -> 74.7 us  [swap(): return lax.all_to_all(pieces, axes, 0, 0, tiled=True)]
    all_to_all x5 -> x1, waiting for transfers between devices: 32 us -> 0.01 us  [swap(): return lax.all_to_all(pieces, axes, 0, 0, tiled=True)]
    all_to_all x5 -> x1, starting transfers between devices: 29.3 us -> 10.2 us  [swap(): return lax.all_to_all(pieces, axes, 0, 0, tiled=True)]
    unnamed x14 -> x30, local copies, waits for them, and re-layouts: 2.49 us -> 10.9 us
    dot_general x5 -> x0, matrix products: 5.3 us -> none  [the longest x1 2.73 us: shards(): jnp.einsum('lpq,lqc->cp', blocks, history, preferred_element_type=F32)]
    ppermute x4 -> x3, starting transfers between devices: 6.79 us -> 2.03 us  [shards(): pieces.append(lax.ppermute(rows_of_k, LAG, [(0, k * nc)]))]
    pallas_call x0 -> x6, Pallas kernels: none -> 4.6 us  [call(): pl.pallas_call(body, out_shape=shapes[0] if single else shapes, in_specs=...]
    slice x5 -> x0, local copies, waits for them, and re-layouts: 3.97 us -> none  [the longest x1 1.93 us: shards(): got = lax.ppermute(whole[c * half:(c + 1) * half], LAG, [(0, c)])]
  transfers between devices with their start and end apart: 10 -> 5, of which waited for: 7 -> 1; matrix products, arithmetic and copies ran while one was open for 12% -> 1% of each run, Pallas kernels for 0% -> 0%
where the time goes in v3:
time: 112 us
  blocking collectives  74.7 us (67%)
  starting transfers between devices  15.8 us (14%)
  local copies, waits for them, and re-layouts  12.5 us (11%)
  Pallas kernels  4.6 us (4%)
  waiting for transfers between devices  2.65 us (2%)
  other arithmetic  1.14 us (1%)
    all_to_all x5, blocking collectives, swap(): return lax.all_to_all(pieces, axes, 0, 0, tiled=True)  74.7 us
    unnamed x30, local copies, waits for them, and re-layouts  10.9 us
    all_to_all x1, starting transfers between devices, swap(): return lax.all_to_all(pieces, axes, 0, 0, tiled=True)  10.2 us
    pallas_call x6, Pallas kernels, call(): pl.pallas_call(body, out_shape=shapes[0] if single else shapes, in_specs=...  4.6 us
    ppermute x1, starting transfers between devices, shards(): lax.ppermute(history[1], LAG, [(i, i + 1) for i in range(nlag - 1)])  3.54 us
    ppermute x1, waiting for transfers between devices, shards(): lax.ppermute(history[1], LAG, [(i, i + 1) for i in range(nlag - 1)])  2.64 us
  transfers between devices with their start and end apart: 5, of which 1 were waited for; matrix products, arithmetic and copies ran while one was open for 1% of the time, Pallas kernels for 0%

profile of v3, /device:TPU:1, one launch (start us, length us, event | category | flops | bytes accessed | tf_op | source)
XLA Modules:
  0.0 111.6 jit_solution(2758649423034808693)
XLA Ops:
  0.1 1.6 %copy-done = bf16[2,256,2048]{2,1,0:T(8,128)(2,1)S(1)} copy-done((bf16[2,256,2048]{2,1,0:T(8,128)(2,1)S(1)}, bf16[2,256,2048]{2,1,0:T(8,128)(2,1)}, u32[]{:S(2)}) %copy-start) | copy-done | bytes 2097176
  1.7 1.2 %copy-done.2 = bf16[2,2048,128]{2,1,0:T(8,128)(2,1)S(1)} copy-done((bf16[2,2048,128]{2,1,0:T(8,128)(2,1)S(1)}, bf16[2,2048,128]{2,1,0:T(8,128)(2,1)}, u32[]{:S(2)}) %copy-start.2) | copy-done | bytes 1048600
  2.9 0.9 copy-done.5
  3.8 0.8 copy-done.14
  4.6 1.3 %shard_map.46 = (f32[8,48,256]{2,1,0:T(8,128)S(1)}, f32[2,16,256]{2,1,0:T(8,128)S(1)}) custom-call(s32[3]{0:T(128)S(1)} %pad_add_fusion.where, bf16[2,256,2048]{2,1,0:T(8,128)(2,1)S(1)} %copy-done, bf16[2,2048,128]{2,1,0:T(8,128)(2,1)S(1)} %copy-done.2, f32[2,256,128]{2,1,0:T(8,128)S(1)} %copy-done.5, f32[32,256]{1,0:T(8,128)S(1)} %copy-done.14), custom_call_target="tpu_custom_call" | custom-call | flops 268435456 | bytes 3866636 | tf_op jit(solution)/shard_map/pallas_call | solution.py:26
  6.0 0.8 copy-done.4
  7.3 10.2 %all-to-all-start = ((f32[8,48,256]{2,1,0:T(8,128)}), f32[8,48,256]{2,1,0:T(8,128)S(1)}, u32[]{:S(2)}, u32[]{:S(2)}) async-start(f32[8,48,256]{2,1,0:T(8,128)} %copy-done.4), calls=%async_computation | async-start | bytes 786432 | tf_op jit(solution)/shard_map/all_to_all | solution.py:16
  17.6 0.8 slice_bitcast_fusion
  18.4 3.5 %collective-permute-start = (bf16[2048,128]{1,0:T(8,128)(2,1)}, bf16[2048,128]{1,0:T(8,128)(2,1)}, u32[]{:S(2)}, u32[]{:S(2)}) collective-permute-start(bf16[2048,128]{1,0:T(8,128)(2,1)} %slice_bitcast_fusion), channel_id=1, source_target_pairs={{0,8},{8,16},{16,24},{24,32},{32,40},{40,48},{48,56},{56,64},{64,7... | collective-permute-start | bytes 1572872 | tf_op jit(solution)/shard_map/ppermute | solution.py:154
  22.0 0.7 collective-permute-start.3
  22.7 0.7 collective-permute-start.2
  24.8 0.7 copy-done.8
  25.5 0.7 copy-done.10
  26.2 2.6 %collective-permute-done.before = bf16[2048,128]{1,0:T(8,128)(2,1)} collective-permute-done((bf16[2048,128]{1,0:T(8,128)(2,1)}, bf16[2048,128]{1,0:T(8,128)(2,1)}, u32[]{:S(2)}, u32[]{:S(2)}) %collective-permute-start) | collective-permute-done | bytes 524320 | tf_op jit(solution)/shard_map/ppermute | solution.py:154
  28.9 0.9 copy-done.7
  29.8 0.9 copy-done.9
  30.8 0.9 copy-done.11
  31.7 1.9 %shard_map.47 = (bf16[8,96,256]{2,1,0:T(8,128)(2,1)S(1)}, f32[128,256]{1,0:T(8,128)S(1)}) custom-call(s32[3]{0:T(128)S(1)} %pad_add_fusion.where, f32[8,48,256]{2,1,0:T(8,128)S(1)} %all-to-all-done.got.got1, bf16[2,256,2048]{2,1,0:T(8,128)(2,1)S(1)} %copy-done.1, bf16[2048,128]{1,0:T(8,128)(2,1)} %collective-permute-done.before, ...), custom_call_target="tpu_custom_call" | custom-call | flops 268435456 | bytes 5373964 | tf_op jit(solution)/shard_map/pallas_call | solution.py:26
  33.6 13.2 %all_to_all.34.got.got2 = bf16[8,96,256]{2,1,0:T(8,128)(2,1)S(1)} all-to-all(bf16[8,96,256]{2,1,0:T(8,128)(2,1)S(1)} %get-tuple-element.15), channel_id=1, replica_groups=mesh['y'=8,'x'=4,'core'=2,'row'=8] {'y'}, dimensions={0} | all-to-all | bytes 786432 | tf_op jit(solution)/shard_map/all_to_all | solution.py:16
  46.9 18.8 %all_to_all.35.got3 = bf16[8,96,256]{2,1,0:T(8,128)(2,1)S(1)} all-to-all(bf16[8,96,256]{2,1,0:T(8,128)(2,1)S(1)} %shard_map.48), channel_id=1, replica_groups=mesh['y'=8,'x'=4,'core'=2,'row'=8] {'x','core'}, dimensions={0} | all-to-all | bytes 786432 | tf_op jit(solution)/shard_map/all_to_all | solution.py:16
  66.0 15.2 %all_to_all.36.got = f32[8,16,256]{2,1,0:T(8,128)S(1)} all-to-all(f32[8,16,256]{2,1,0:T(8,128)S(1)} %get-tuple-element.18), channel_id=1, replica_groups=mesh['y'=8,'x'=4,'core'=2,'row'=8] {'row'}, dimensions={0} | all-to-all | bytes 262144 | tf_op jit(solution)/shard_map/all_to_all | solution.py:16
  81.2 0.7 shard_map.50
  81.9 10.4 %all_to_all.37.got = f32[8,16,256]{2,1,0:T(8,128)S(1)} all-to-all(f32[8,16,256]{2,1,0:T(8,128)S(1)} %get-tuple-element.21), channel_id=1, replica_groups=mesh['y'=8,'x'=4,'core'=2,'row'=8] {'y'}, dimensions={0} | all-to-all | bytes 262144 | tf_op jit(solution)/shard_map/all_to_all | solution.py:16
  93.0 17.1 %all_to_all.38 = f32[64,1,576]{2,1,0:T(1,128)S(1)} all-to-all(f32[64,1,576]{2,1,0:T(1,128)S(1)} %all_to_all.26), channel_id=1, replica_groups=mesh['y'=8,'x'=4,'core'=2,'row'=8] {'x','core','row'}, dimensions={0} | all-to-all | bytes 294912 | tf_op jit(solution)/shard_map/all_to_all | solution.py:16
  (42 shorter events, 4.6 us)
Async XLA Ops:
  0.1 1.6 %copy-start = (bf16[2,256,2048]{2,1,0:T(8,128)(2,1)S(1)}, bf16[2,256,2048]{2,1,0:T(8,128)(2,1)}, u32[]{:S(2)}) copy-start(bf16[2,256,2048]{2,1,0:T(8,128)(2,1)} %blocks.3) | copy-start | bytes 6291460
  1.7 1.2 %copy-start.2 = (bf16[2,2048,128]{2,1,0:T(8,128)(2,1)S(1)}, bf16[2,2048,128]{2,1,0:T(8,128)(2,1)}, u32[]{:S(2)}) copy-start(bf16[2,2048,128]{2,1,0:T(8,128)(2,1)} %history.3) | copy-start | bytes 3145732
  2.9 0.9 copy-start.5
  3.8 0.8 copy-start.14
  4.6 13.0 %copy-start.3 = (bf16[2,2048,128]{2,1,0:T(8,128)(2,1)S(1)}, bf16[2,2048,128]{2,1,0:T(8,128)(2,1)}, u32[]{:S(2)}) copy-start(bf16[2,2048,128]{2,1,0:T(8,128)(2,1)} %history.3) | copy-start | bytes 3145732
  4.6 17.3 %copy-start.1 = (bf16[2,256,2048]{2,1,0:T(8,128)(2,1)S(1)}, bf16[2,256,2048]{2,1,0:T(8,128)(2,1)}, u32[]{:S(2)}) copy-start(bf16[2,256,2048]{2,1,0:T(8,128)(2,1)} %blocks.3) | copy-start | bytes 6291460
  5.9 0.8 copy-start.4
  6.7 0.6 copy-start.12
  7.3 18.9 %all-to-all-start = ((f32[8,48,256]{2,1,0:T(8,128)}), f32[8,48,256]{2,1,0:T(8,128)S(1)}, u32[]{:S(2)}, u32[]{:S(2)}) async-start(f32[8,48,256]{2,1,0:T(8,128)} %copy-done.4), calls=%async_computation | async-start | bytes 786432 | tf_op jit(solution)/shard_map/all_to_all | solution.py:16
  18.4 10.5 %collective-permute-start = (bf16[2048,128]{1,0:T(8,128)(2,1)}, bf16[2048,128]{1,0:T(8,128)(2,1)}, u32[]{:S(2)}, u32[]{:S(2)}) collective-permute-start(bf16[2048,128]{1,0:T(8,128)(2,1)} %slice_bitcast_fusion), channel_id=1, source_target_pairs={{0,8},{8,16},{16,24},{24,32},{32,40},{40,48},{48,56},{56,64},{64,7... | collective-permute-start | bytes 1572872 | tf_op jit(solution)/shard_map/ppermute | solution.py:154
  22.0 2.1 %collective-permute-start.3 = (bf16[64,2048]{1,0:T(8,128)(2,1)S(1)}, bf16[64,2048]{1,0:T(8,128)(2,1)S(1)}, u32[]{:S(2)}, u32[]{:S(2)}) collective-permute-start(bf16[64,2048]{1,0:T(8,128)(2,1)S(1)} %get-tuple-element.23), channel_id=1, source_target_pairs={{0,48},{1,49},{2,50},{3,51},{4,52},{5,53},{6,54},{7,55}} | collective-permute-start | bytes 786440 | tf_op jit(solution)/shard_map/ppermute | solution.py:153
  22.7 2.1 %collective-permute-start.2 = (bf16[64,2048]{1,0:T(8,128)(2,1)S(1)}, bf16[64,2048]{1,0:T(8,128)(2,1)S(1)}, u32[]{:S(2)}, u32[]{:S(2)}) collective-permute-start(bf16[64,2048]{1,0:T(8,128)(2,1)S(1)} %get-tuple-element.24), channel_id=1, source_target_pairs={{0,32},{1,33},{2,34},{3,35},{4,36},{5,37},{6,38},{7,39}} | collective-permute-start | bytes 786440 | tf_op jit(solution)/shard_map/ppermute | solution.py:153
  23.4 2.1 %collective-permute-start.1 = (bf16[64,2048]{1,0:T(8,128)(2,1)S(1)}, bf16[64,2048]{1,0:T(8,128)(2,1)S(1)}, u32[]{:S(2)}, u32[]{:S(2)}) collective-permute-start(bf16[64,2048]{1,0:T(8,128)(2,1)S(1)} %get-tuple-element.25), channel_id=1, source_target_pairs={{0,16},{1,17},{2,18},{3,19},{4,20},{5,21},{6,22},{7,23}} | collective-permute-start | bytes 786440 | tf_op jit(solution)/shard_map/ppermute | solution.py:153
  24.1 0.7 copy-start.6
  24.8 0.7 copy-start.8
  25.5 0.7 copy-start.10
  28.9 0.9 copy-start.7
  29.8 0.9 copy-start.9
  30.8 0.9 copy-start.11
  33.6 32.1 %copy-start.13 = (f32[2,16,256]{2,1,0:T(8,128)S(1)}, f32[2,16,256]{2,1,0:T(8,128)}, u32[]{:S(2)}) copy-start(f32[2,16,256]{2,1,0:T(8,128)} %copy-done.12) | copy-start | bytes 98308

commit v4 on v3

--- a/solution.py
+++ b/solution.py
@@ -16,20 +16,23 @@
     return lax.all_to_all(pieces, axes, 0, 0, tiled=True)
 
 
-def call(body, outs, flops, *args, scratch=()):
+def call(body, outs, flops, *args, scratch=(), held=None, given=None, limit=24):
     single = not isinstance(outs, list)
     outs = [outs] if single else outs
     shapes = [jax.ShapeDtypeStruct(s, d) for s, d in outs]
     size = sum(a.size * a.dtype.itemsize for a in args)
     size += sum(s.size * s.dtype.itemsize for s in shapes)
-    spaces = [pltpu.SMEM if a.dtype == jnp.int32 else pltpu.VMEM for a in args]
+    held = held or [pltpu.SMEM if a.dtype == jnp.int32 else pltpu.VMEM for a in args]
+    given = given or [pltpu.VMEM] * len(outs)
+    specs = [pl.BlockSpec(memory_space=m) for m in given]
     return pl.pallas_call(
         body,
         out_shape=shapes[0] if single else shapes,
-        in_specs=[pl.BlockSpec(memory_space=m) for m in spaces],
+        in_specs=[pl.BlockSpec(memory_space=m) for m in held],
+        out_specs=specs[0] if single else specs,
         scratch_shapes=scratch,
         cost_estimate=pl.CostEstimate(flops=flops, bytes_accessed=size, transcendentals=0),
-        compiler_params=pltpu.CompilerParams(vmem_limit_bytes=24 * 1024 * 1024),
+        compiler_params=pltpu.CompilerParams(vmem_limit_bytes=limit * 1024 * 1024),
     )(*args)
 
 
@@ -59,33 +62,69 @@
     return sum_first(ref, start, start + count) + sum_first(ref, start + count, start + 2 * count)
 
 
-def first_sums(where, blocks, history, excitation, inverse, out, field, turned):
-    nw = out.shape[0]
-    total = mm(blocks[0], history[0]) + mm(blocks[1], history[1])
-    total = total.T
-    cw = total.shape[0] // nw
+def first_sums(
+    where, blocks, history, excitation, inverse, out, field, b, h, e, own, turned, o, f, sems
+):
+    loads = [
+        pltpu.make_async_copy(blocks.at[0], b.at[0], sems.at[0]),
+        pltpu.make_async_copy(history.at[0], h.at[0], sems.at[1]),
+        pltpu.make_async_copy(blocks.at[1], b.at[1], sems.at[2]),
+        pltpu.make_async_copy(history.at[1], h.at[1], sems.at[3]),
+        pltpu.make_async_copy(inverse, own, sems.at[4]),
+        pltpu.make_async_copy(excitation, e, sems.at[5]),
+    ]
+    for load in loads:
+        load.start()
+    nw, depth, _ = out.shape
+    cw = depth - own.shape[0]
+    loads[0].wait()
+    loads[1].wait()
+    total = mm(b[0], h[0])
+    loads[2].wait()
+    loads[3].wait()
+    total = (total + mm(b[1], h[1])).T
+    loads[4].wait()
     for w in range(nw):
-        out[w, :cw] = total[w * cw : (w + 1) * cw]
-        out[w, cw:] = inverse[...]
+        o[w, :cw] = total[w * cw : (w + 1) * cw]
+        o[w, cw:] = own[...]
+    store = pltpu.make_async_copy(o, out, sems.at[6])
+    store.start()
+    loads[5].wait()
     start = pl.multiple_of(where[1] * cw, cw)
-    for s in range(excitation.shape[0]):
-        turned[...] = excitation[s].T
-        field[s] = turned[pl.ds(start, cw)]
-
-
-def second_step(where, got, blocks, before, history, got1, got2, got3, out, later):
+    for s in range(e.shape[0]):
+        turned[...] = e[s].T
+        f[s] = turned[pl.ds(start, cw)]
+    other = pltpu.make_async_copy(f, field, sems.at[7])
+    other.start()
+    store.wait()
+    other.wait()
+
+
+def later_sums(blocks, before, history, out, prior, sem):
+    load = pltpu.make_async_copy(before, prior, sem)
+    load.start()
+    total = mm(blocks[1], history[0])
+    load.wait()
+    out[...] = (total + mm(blocks[0], prior[...])).T
+
+
+def second_step(where, got, blocks, got1, got2, got3, out, piece, sem):
+    cut = piece.shape[0]
+    for k, source in enumerate((blocks.at[0, :cut], got1, got2, got3)):
+
+        @pl.when(where[0] == k)
+        def _():
+            pltpu.make_async_copy(source, piece, sem).start()
+
     ny, depth, span = out.shape
-    cut = got1.shape[0]
     cw = (depth - cut) // 2
     high, low = parts(sum_first(got, 0, cw))
-    piece = blocks[0, :cut]
-    for k, other in enumerate((got1, got2, got3)):
-        piece = jnp.where(where[0] == k + 1, other[...], piece)
     for y in range(ny):
         out[y, :cw] = high
         out[y, cw : 2 * cw] = low
+    pltpu.make_async_copy(got1, piece, sem).wait()
+    for y in range(ny):
         out[y, 2 * cw :] = piece[:, y * span : (y + 1) * span]
-    later[...] = (mm(blocks[0], before[...]) + mm(blocks[1], history[0])).T
 
 
 def third_step(got, later, out):
@@ -154,13 +193,37 @@
     before = lax.ppermute(history[1], LAG, [(i, i + 1) for i in range(nlag - 1)])
 
     outs = [((nw, cw + own, rows), F32), ((2, cw, rows), F32)]
-    turned = [pltpu.VMEM((columns, rows), F32)]
+    scratch = [pltpu.VMEM(a.shape, a.dtype) for a in (blocks, history, excitation, self_inverse)]
+    scratch += [pltpu.VMEM((columns, rows), F32)] + [pltpu.VMEM(*o) for o in outs]
+    scratch += [pltpu.SemaphoreType.DMA((8,))]
     args = where, blocks, history, excitation, self_inverse
-    send, field = call(first_sums, outs, work, *args, scratch=turned)
+    held = [pltpu.SMEM] + [pltpu.HBM] * 4
+    send, field = call(
+        first_sums, outs, work, *args, scratch=scratch, held=held, given=[pltpu.HBM] * 2, limit=60
+    )
     got1 = swap(send, W)
-    outs = [((ny, 2 * cw + cut, span), BF16), ((columns, rows), F32)]
-    args = where, got1, blocks, before, history, *pieces
-    send, later = call(second_step, outs, work, *args)
+    later = call(
+        later_sums,
+        ((columns, rows), F32),
+        work,
+        blocks,
+        before,
+        history,
+        scratch=[pltpu.VMEM(before.shape, BF16), pltpu.SemaphoreType.DMA(())],
+        held=[pltpu.VMEM, pltpu.HBM, pltpu.VMEM],
+    )
+    got1, later = lax.optimization_barrier((got1, later))
+    send = call(
+        second_step,
+        ((ny, 2 * cw + cut, span), BF16),
+        small,
+        where,
+        got1,
+        blocks,
+        *pieces,
+        scratch=[pltpu.VMEM((cut, size), BF16), pltpu.SemaphoreType.DMA(())],
+        held=[pltpu.SMEM, pltpu.VMEM] + [pltpu.HBM] * 4,
+    )
     got2 = swap(send, "y")
     send = call(third_step, ((nw, 2 * cw + cut, rows), BF16), small, got2, later)
     got3 = swap(send, W)

time: 112 us -> 108 us (0.964)
  local copies, waits for them, and re-layouts: 12.5 us -> 2.39 us
  Pallas kernels: 4.6 us -> 7.32 us
  starting transfers between devices: 15.8 us -> 18 us
  blocking collectives: 74.7 us -> 76.3 us
    unnamed x30 -> x12, local copies, waits for them, and re-layouts: 10.9 us -> 0.68 us
    pallas_call x6 -> x7, Pallas kernels: 4.6 us -> 7.32 us  [call(): pl.pallas_call(body, out_shape=shapes[0] if single else shapes, in_specs=...]
    ppermute x3, starting transfers between devices: 2.03 us -> 4.2 us  [shards(): pieces.append(lax.ppermute(rows_of_k, LAG, [(0, k * nc)]))]
    all_to_all x5, blocking collectives: 74.7 us -> 76.3 us  [swap(): return lax.all_to_all(pieces, axes, 0, 0, tiled=True)]
  transfers between devices with their start and end apart: 5 -> 5, of which waited for: 1 -> 1; matrix products, arithmetic and copies ran while one was open for 1% -> 1% of each run, Pallas kernels for 0% -> 1%
where the time goes in v4:
time: 108 us
  blocking collectives  76.3 us (71%)
  starting transfers between devices  18 us (17%)
  Pallas kernels  7.32 us (7%)
  local copies, waits for them, and re-layouts  2.39 us (2%)
  waiting for transfers between devices  1.8 us (2%)
  other arithmetic  1.72 us (2%)
    all_to_all x5, blocking collectives, swap(): return lax.all_to_all(pieces, axes, 0, 0, tiled=True)  76.3 us
    all_to_all x1, starting transfers between devices, swap(): return lax.all_to_all(pieces, axes, 0, 0, tiled=True)  10.2 us
    pallas_call x7, Pallas kernels, call(): pl.pallas_call(body, out_shape=shapes[0] if single else shapes, in_specs=...  7.32 us
    ppermute x3, starting transfers between devices, shards(): pieces.append(lax.ppermute(rows_of_k, LAG, [(0, k * nc)]))  4.2 us
    ppermute x1, starting transfers between devices, shards(): lax.ppermute(history[1], LAG, [(i, i + 1) for i in range(nlag - 1)])  3.55 us
  transfers between devices with their start and end apart: 5, of which 1 were waited for; matrix products, arithmetic and copies ran while one was open for 1% of the time, Pallas kernels for 1%

profile of v4, /device:TPU:1, one launch (start us, length us, event | category | flops | bytes accessed | tf_op | source)
XLA Modules:
  0.0 107.7 jit_solution(9644763033399558628)
XLA Ops:
  0.0 0.7 pad_add_fusion.where
  0.7 4.4 %shard_map.46 = (f32[8,48,256]{2,1,0:T(8,128)}, f32[2,16,256]{2,1,0:T(8,128)}) custom-call(s32[3]{0:T(128)} %pad_add_fusion.where, bf16[2,256,2048]{2,1,0:T(8,128)(2,1)} %blocks.5, bf16[2,2048,128]{2,1,0:T(8,128)(2,1)} %history.3, f32[2,256,128]{2,1,0:T(8,128)} %excitation.1, f32[32,256]{1,0:T(8,128)} %inverse.1), custom_call_target="tpu_custom_call" | custom-call | flops 268435456 | bytes 3866636 | tf_op jit(solution)/shard_map/pallas_call | solution.py:28
  5.0 10.2 %all-to-all-start = ((f32[8,48,256]{2,1,0:T(8,128)}), f32[8,48,256]{2,1,0:T(8,128)S(1)}, u32[]{:S(2)}, u32[]{:S(2)}) async-start(f32[8,48,256]{2,1,0:T(8,128)} %get-tuple-element.14), calls=%async_computation | async-start | bytes 786432 | tf_op jit(solution)/shard_map/all_to_all | solution.py:16
  15.3 3.5 %collective-permute-start = (bf16[2048,128]{1,0:T(8,128)(2,1)S(1)}, bf16[2048,128]{1,0:T(8,128)(2,1)S(1)}, u32[]{:S(2)}, u32[]{:S(2)}) collective-permute-start(bf16[2048,128]{1,0:T(8,128)(2,1)S(1)} %slice_bitcast_fusion), channel_id=1, source_target_pairs={{0,8},{8,16},{16,24},{24,32},{32,40},{40,48},{48,56},{56,64},{64,7... | collective-permute-start | bytes 1572872 | tf_op jit(solution)/shard_map/ppermute | solution.py:193
  18.9 0.9 slice_bitcast_fusion.1
  19.8 1.5 %collective-permute-start.3 = (bf16[64,2048]{1,0:T(8,128)(2,1)}, bf16[64,2048]{1,0:T(8,128)(2,1)}, u32[]{:S(2)}, u32[]{:S(2)}) collective-permute-start(bf16[64,2048]{1,0:T(8,128)(2,1)} %get-tuple-element.23), channel_id=1, source_target_pairs={{0,48},{1,49},{2,50},{3,51},{4,52},{5,53},{6,54},{7,55}} | collective-permute-start | bytes 786440 | tf_op jit(solution)/shard_map/ppermute | solution.py:192
  21.3 1.4 %collective-permute-start.2 = (bf16[64,2048]{1,0:T(8,128)(2,1)}, bf16[64,2048]{1,0:T(8,128)(2,1)}, u32[]{:S(2)}, u32[]{:S(2)}) collective-permute-start(bf16[64,2048]{1,0:T(8,128)(2,1)} %get-tuple-element.24), channel_id=1, source_target_pairs={{0,32},{1,33},{2,34},{3,35},{4,36},{5,37},{6,38},{7,39}} | collective-permute-start | bytes 786440 | tf_op jit(solution)/shard_map/ppermute | solution.py:192
  22.7 1.4 %collective-permute-start.1 = (bf16[64,2048]{1,0:T(8,128)(2,1)}, bf16[64,2048]{1,0:T(8,128)(2,1)}, u32[]{:S(2)}, u32[]{:S(2)}) collective-permute-start(bf16[64,2048]{1,0:T(8,128)(2,1)} %get-tuple-element.25), channel_id=1, source_target_pairs={{0,16},{1,17},{2,18},{3,19},{4,20},{5,21},{6,22},{7,23}} | collective-permute-start | bytes 786440 | tf_op jit(solution)/shard_map/ppermute | solution.py:192
  24.0 1.8 %collective-permute-done.before = bf16[2048,128]{1,0:T(8,128)(2,1)S(1)} collective-permute-done((bf16[2048,128]{1,0:T(8,128)(2,1)S(1)}, bf16[2048,128]{1,0:T(8,128)(2,1)S(1)}, u32[]{:S(2)}, u32[]{:S(2)}) %collective-permute-start) | collective-permute-done | bytes 524320 | tf_op jit(solution)/shard_map/ppermute | solution.py:193
  25.8 0.9 shard_map.47.later
  26.8 0.7 copy-done.2
  27.5 0.6 shard_map.48
  28.1 13.3 %all_to_all.34.got.got2 = bf16[8,96,256]{2,1,0:T(8,128)(2,1)S(1)} all-to-all(bf16[8,96,256]{2,1,0:T(8,128)(2,1)S(1)} %shard_map.48), channel_id=1, replica_groups=mesh['y'=8,'x'=4,'core'=2,'row'=8] {'y'}, dimensions={0} | all-to-all | bytes 786432 | tf_op jit(solution)/shard_map/all_to_all | solution.py:16
  41.5 18.6 %all_to_all.35.got3 = bf16[8,96,256]{2,1,0:T(8,128)(2,1)S(1)} all-to-all(bf16[8,96,256]{2,1,0:T(8,128)(2,1)S(1)} %shard_map.49), channel_id=1, replica_groups=mesh['y'=8,'x'=4,'core'=2,'row'=8] {'x','core'}, dimensions={0} | all-to-all | bytes 786432 | tf_op jit(solution)/shard_map/all_to_all | solution.py:16
  60.1 0.3 shard_map.50
  60.5 16.8 %all_to_all.36.got = f32[8,16,256]{2,1,0:T(8,128)S(1)} all-to-all(f32[8,16,256]{2,1,0:T(8,128)S(1)} %get-tuple-element.18), channel_id=1, replica_groups=mesh['y'=8,'x'=4,'core'=2,'row'=8] {'row'}, dimensions={0} | all-to-all | bytes 262144 | tf_op jit(solution)/shard_map/all_to_all | solution.py:16
  77.3 0.7 shard_map.51
  78.0 10.4 %all_to_all.37.got = f32[8,16,256]{2,1,0:T(8,128)S(1)} all-to-all(f32[8,16,256]{2,1,0:T(8,128)S(1)} %get-tuple-element.21), channel_id=1, replica_groups=mesh['y'=8,'x'=4,'core'=2,'row'=8] {'y'}, dimensions={0} | all-to-all | bytes 262144 | tf_op jit(solution)/shard_map/all_to_all | solution.py:16
  88.4 0.3 shard_map.52
  89.0 0.2 all_to_all.26
  89.1 17.1 %all_to_all.38 = f32[64,1,576]{2,1,0:T(1,128)S(1)} all-to-all(f32[64,1,576]{2,1,0:T(1,128)S(1)} %all_to_all.26), channel_id=1, replica_groups=mesh['y'=8,'x'=4,'core'=2,'row'=8] {'x','core','row'}, dimensions={0} | all-to-all | bytes 294912 | tf_op jit(solution)/shard_map/all_to_all | solution.py:16
  106.2 0.4 reduce
  106.6 0.2 reshape.20
  107.0 0.6 pad_maximum_fusion
  (25 shorter events, 0.5 us)
Async XLA Ops:
  0.7 14.6 %copy-start.1 = (bf16[2,2048,128]{2,1,0:T(8,128)(2,1)S(1)}, bf16[2,2048,128]{2,1,0:T(8,128)(2,1)}, u32[]{:S(2)}) copy-start(bf16[2,2048,128]{2,1,0:T(8,128)(2,1)} %history.3) | copy-start | bytes 3145732
  0.7 18.2 %copy-start = (bf16[2,256,2048]{2,1,0:T(8,128)(2,1)S(1)}, bf16[2,256,2048]{2,1,0:T(8,128)(2,1)}, u32[]{:S(2)}) copy-start(bf16[2,256,2048]{2,1,0:T(8,128)(2,1)} %blocks.5) | copy-start | bytes 6291460
  5.0 22.4 %all-to-all-start = ((f32[8,48,256]{2,1,0:T(8,128)}), f32[8,48,256]{2,1,0:T(8,128)S(1)}, u32[]{:S(2)}, u32[]{:S(2)}) async-start(f32[8,48,256]{2,1,0:T(8,128)} %get-tuple-element.14), calls=%async_computation | async-start | bytes 786432 | tf_op jit(solution)/shard_map/all_to_all | solution.py:16
  15.3 10.5 %collective-permute-start = (bf16[2048,128]{1,0:T(8,128)(2,1)S(1)}, bf16[2048,128]{1,0:T(8,128)(2,1)S(1)}, u32[]{:S(2)}, u32[]{:S(2)}) collective-permute-start(bf16[2048,128]{1,0:T(8,128)(2,1)S(1)} %slice_bitcast_fusion), channel_id=1, source_target_pairs={{0,8},{8,16},{16,24},{24,32},{32,40},{40,48},{48,56},{56,64},{64,7... | collective-permute-start | bytes 1572872 | tf_op jit(solution)/shard_map/ppermute | solution.py:193
  19.8 7.7 %copy-start.5 = (s32[3]{0:T(128)S(1)}, s32[3]{0:T(128)}, u32[]{:S(2)}) copy-start(s32[3]{0:T(128)} %pad_add_fusion.where) | copy-start | bytes 40
  19.8 7.6 %collective-permute-start.3 = (bf16[64,2048]{1,0:T(8,128)(2,1)}, bf16[64,2048]{1,0:T(8,128)(2,1)}, u32[]{:S(2)}, u32[]{:S(2)}) collective-permute-start(bf16[64,2048]{1,0:T(8,128)(2,1)} %get-tuple-element.23), channel_id=1, source_target_pairs={{0,48},{1,49},{2,50},{3,51},{4,52},{5,53},{6,54},{7,55}} | collective-permute-start | bytes 786440 | tf_op jit(solution)/shard_map/ppermute | solution.py:192
  21.3 6.1 %collective-permute-start.2 = (bf16[64,2048]{1,0:T(8,128)(2,1)}, bf16[64,2048]{1,0:T(8,128)(2,1)}, u32[]{:S(2)}, u32[]{:S(2)}) collective-permute-start(bf16[64,2048]{1,0:T(8,128)(2,1)} %get-tuple-element.24), channel_id=1, source_target_pairs={{0,32},{1,33},{2,34},{3,35},{4,36},{5,37},{6,38},{7,39}} | collective-permute-start | bytes 786440 | tf_op jit(solution)/shard_map/ppermute | solution.py:192
  22.7 4.8 %collective-permute-start.1 = (bf16[64,2048]{1,0:T(8,128)(2,1)}, bf16[64,2048]{1,0:T(8,128)(2,1)}, u32[]{:S(2)}, u32[]{:S(2)}) collective-permute-start(bf16[64,2048]{1,0:T(8,128)(2,1)} %get-tuple-element.25), channel_id=1, source_target_pairs={{0,16},{1,17},{2,18},{3,19},{4,20},{5,21},{6,22},{7,23}} | collective-permute-start | bytes 786440 | tf_op jit(solution)/shard_map/ppermute | solution.py:192
  26.8 0.7 copy-start.2
  27.5 14.0 %copy-start.3 = (f32[128,256]{1,0:T(8,128)S(1)}, f32[128,256]{1,0:T(8,128)}, u32[]{:S(2)}) copy-start(f32[128,256]{1,0:T(8,128)} %copy-done.2) | copy-start | bytes 393220
  28.1 32.0 %copy-start.4 = (f32[2,16,256]{2,1,0:T(8,128)S(1)}, f32[2,16,256]{2,1,0:T(8,128)}, u32[]{:S(2)}) copy-start(f32[2,16,256]{2,1,0:T(8,128)} %get-tuple-element.17.field) | copy-start | bytes 98308

commit v5 on v4

--- a/solution.py
+++ b/solution.py
@@ -62,9 +62,9 @@
     return sum_first(ref, start, start + count) + sum_first(ref, start + count, start + 2 * count)
 
 
-def first_sums(
-    where, blocks, history, excitation, inverse, out, field, b, h, e, own, turned, o, f, sems
-):
+def first_sums(where, blocks, history, excitation, inverse, out, field, *rest):
+    pieces, (b, h, e, own, turned, o, f, sems) = rest[:-8], rest[-8:]
+    cut = pieces[0].shape[0]
     loads = [
         pltpu.make_async_copy(blocks.at[0], b.at[0], sems.at[0]),
         pltpu.make_async_copy(history.at[0], h.at[0], sems.at[1]),
@@ -78,6 +78,11 @@
     nw, depth, _ = out.shape
     cw = depth - own.shape[0]
     loads[0].wait()
+    stores = []
+    for k, piece in enumerate(pieces):
+        rows = b.at[0, k * cut : (k + 1) * cut]
+        stores.append(pltpu.make_async_copy(rows, piece, sems.at[8 + k]))
+        stores[-1].start()
     loads[1].wait()
     total = mm(b[0], h[0])
     loads[2].wait()
@@ -87,30 +92,43 @@
     for w in range(nw):
         o[w, :cw] = total[w * cw : (w + 1) * cw]
         o[w, cw:] = own[...]
-    store = pltpu.make_async_copy(o, out, sems.at[6])
-    store.start()
+    stores.append(pltpu.make_async_copy(o, out, sems.at[6]))
+    stores[-1].start()
     loads[5].wait()
     start = pl.multiple_of(where[1] * cw, cw)
     for s in range(e.shape[0]):
         turned[...] = e[s].T
         f[s] = turned[pl.ds(start, cw)]
-    other = pltpu.make_async_copy(f, field, sems.at[7])
-    other.start()
+    stores.append(pltpu.make_async_copy(f, field, sems.at[7]))
+    stores[-1].start()
+    for store in stores:
+        store.wait()
+
+
+def later_sums(blocks, before, history, out, b, h, o, sems):
+    loads = [
+        pltpu.make_async_copy(blocks.at[1], b.at[1], sems.at[0]),
+        pltpu.make_async_copy(history.at[0], h.at[0], sems.at[1]),
+        pltpu.make_async_copy(blocks.at[0], b.at[0], sems.at[2]),
+        pltpu.make_async_copy(before, h.at[1], sems.at[3]),
+    ]
+    for load in loads:
+        load.start()
+    loads[0].wait()
+    loads[1].wait()
+    total = mm(b[1], h[0])
+    loads[2].wait()
+    loads[3].wait()
+    o[...] = (total + mm(b[0], h[1])).T
+    store = pltpu.make_async_copy(o, out, sems.at[0])
+    store.start()
     store.wait()
-    other.wait()
-
-
-def later_sums(blocks, before, history, out, prior, sem):
-    load = pltpu.make_async_copy(before, prior, sem)
-    load.start()
-    total = mm(blocks[1], history[0])
-    load.wait()
-    out[...] = (total + mm(blocks[0], prior[...])).T
-
-
-def second_step(where, got, blocks, got1, got2, got3, out, piece, sem):
+
+
+def second_step(where, got, *rest):
+    sources, (out, piece, sem) = rest[:-3], rest[-3:]
     cut = piece.shape[0]
-    for k, source in enumerate((blocks.at[0, :cut], got1, got2, got3)):
+    for k, source in enumerate(sources):
 
         @pl.when(where[0] == k)
         def _():
@@ -122,7 +140,7 @@
     for y in range(ny):
         out[y, :cw] = high
         out[y, cw : 2 * cw] = low
-    pltpu.make_async_copy(got1, piece, sem).wait()
+    pltpu.make_async_copy(sources[0], piece, sem).wait()
     for y in range(ny):
         out[y, 2 * cw :] = piece[:, y * span : (y + 1) * span]
 
@@ -186,22 +204,33 @@
 
     where = jnp.stack([ix, iw, iz]).astype(jnp.int32)
 
-    pieces = []
-    for k in range(1, nx):
-        rows_of_k = blocks[0, k * cut : (k + 1) * cut]
-        pieces.append(lax.ppermute(rows_of_k, LAG, [(0, k * nc)]))
     before = lax.ppermute(history[1], LAG, [(i, i + 1) for i in range(nlag - 1)])
 
-    outs = [((nw, cw + own, rows), F32), ((2, cw, rows), F32)]
+    outs = [((nw, cw + own, rows), F32), ((2, cw, rows), F32)] + [((cut, size), BF16)] * nx
     scratch = [pltpu.VMEM(a.shape, a.dtype) for a in (blocks, history, excitation, self_inverse)]
-    scratch += [pltpu.VMEM((columns, rows), F32)] + [pltpu.VMEM(*o) for o in outs]
-    scratch += [pltpu.SemaphoreType.DMA((8,))]
+    scratch += [pltpu.VMEM((columns, rows), F32)] + [pltpu.VMEM(*o) for o in outs[:2]]
+    scratch += [pltpu.SemaphoreType.DMA((8 + nx,))]
     args = where, blocks, history, excitation, self_inverse
     held = [pltpu.SMEM] + [pltpu.HBM] * 4
-    send, field = call(
-        first_sums, outs, work, *args, scratch=scratch, held=held, given=[pltpu.HBM] * 2, limit=60
+    given = [pltpu.HBM] * len(outs)
+    send, field, *pieces = call(
+        first_sums, outs, work, *args, scratch=scratch, held=held, given=given, limit=60
     )
     got1 = swap(send, W)
+    for k in range(1, nx):
+        route = [(x * nc, (x + k) % nx * nc) for x in range(nx)]
+        pieces[k] = lax.ppermute(pieces[k], LAG, route)
+    send = call(
+        second_step,
+        ((ny, 2 * cw + cut, span), BF16),
+        small,
+        where,
+        got1,
+        *pieces,
+        scratch=[pltpu.VMEM((cut, size), BF16), pltpu.SemaphoreType.DMA(())],
+        held=[pltpu.SMEM, pltpu.VMEM] + [pltpu.HBM] * nx,
+    )
+    got2 = swap(send, "y")
     later = call(
         later_sums,
         ((columns, rows), F32),
@@ -209,22 +238,16 @@
         blocks,
         before,
         history,
-        scratch=[pltpu.VMEM(before.shape, BF16), pltpu.SemaphoreType.DMA(())],
-        held=[pltpu.VMEM, pltpu.HBM, pltpu.VMEM],
-    )
-    got1, later = lax.optimization_barrier((got1, later))
-    send = call(
-        second_step,
-        ((ny, 2 * cw + cut, span), BF16),
-        small,
-        where,
-        got1,
-        blocks,
-        *pieces,
-        scratch=[pltpu.VMEM((cut, size), BF16), pltpu.SemaphoreType.DMA(())],
-        held=[pltpu.SMEM, pltpu.VMEM] + [pltpu.HBM] * 4,
-    )
-    got2 = swap(send, "y")
+        scratch=[
+            pltpu.VMEM(blocks.shape, BF16),
+            pltpu.VMEM(history.shape, BF16),
+            pltpu.VMEM((columns, rows), F32),
+            pltpu.SemaphoreType.DMA((4,)),
+        ],
+        held=[pltpu.HBM] * 3,
+        given=[pltpu.HBM],
+        limit=60,
+    )
     send = call(third_step, ((nw, 2 * cw + cut, rows), BF16), small, got2, later)
     got3 = swap(send, W)
     outs = [((nz, cw, rows), F32), ((cw, rows), F32), ((rows, span), BF16)]

time: 108 us -> 117 us (1.083)
  blocking collectives: 76.3 us -> 61.3 us
  waiting for transfers between devices: 1.8 us -> 12.2 us
  starting transfers between devices: 18 us -> 27.3 us
  Pallas kernels: 7.32 us -> 10.4 us
    all_to_all x5 -> x4, blocking collectives: 76.3 us -> 61.3 us  [swap(): return lax.all_to_all(pieces, axes, 0, 0, tiled=True)]
    ppermute x1, starting transfers between devices: 3.55 us -> 11.6 us  [shards(): lax.ppermute(history[1], LAG, [(i, i + 1) for i in range(nlag - 1)])]
    all_to_all x1 -> x2, waiting for transfers between devices: 0.01 us -> 6.07 us  [swap(): return lax.all_to_all(pieces, axes, 0, 0, tiled=True)]
    ppermute x1, waiting for transfers between devices: 1.79 us -> 6.1 us  [shards(): lax.ppermute(history[1], LAG, [(i, i + 1) for i in range(nlag - 1)])]
    all_to_all x1 -> x2, starting transfers between devices: 10.2 us -> 13.7 us  [swap(): return lax.all_to_all(pieces, axes, 0, 0, tiled=True)]
    pallas_call x7, Pallas kernels: 7.32 us -> 10.4 us  [call(): pl.pallas_call(body, out_shape=shapes[0] if single else shapes, in_specs=...]
    ppermute x3, starting transfers between devices: 4.2 us -> 2.02 us  [shards(): pieces[k] = lax.ppermute(pieces[k], LAG, route)]
    unnamed x12, local copies, waits for them, and re-layouts: 0.68 us -> 2.65 us
  transfers between devices with their start and end apart: 5 -> 6, of which waited for: 1 -> 2; matrix products, arithmetic and copies ran while one was open for 1% -> 0% of each run, Pallas kernels for 1% -> 3%
where the time goes in v5:
time: 117 us; the launch traced here: 116 us
  blocking collectives  61.3 us (52%)
  starting transfers between devices  27.3 us (23%)
  waiting for transfers between devices  12.2 us (10%)
  Pallas kernels  10.4 us (9%)
  local copies, waits for them, and re-layouts  3.41 us (3%)
  other arithmetic  1.62 us (1%)
    all_to_all x4, blocking collectives, swap(): return lax.all_to_all(pieces, axes, 0, 0, tiled=True)  61.3 us
    all_to_all x2, starting transfers between devices, swap(): return lax.all_to_all(pieces, axes, 0, 0, tiled=True)  13.7 us
    ppermute x1, starting transfers between devices, shards(): lax.ppermute(history[1], LAG, [(i, i + 1) for i in range(nlag - 1)])  11.6 us
    pallas_call x7, Pallas kernels, call(): pl.pallas_call(body, out_shape=shapes[0] if single else shapes, in_specs=...  10.4 us
    ppermute x1, waiting for transfers between devices, shards(): lax.ppermute(history[1], LAG, [(i, i + 1) for i in range(nlag - 1)])  6.1 us
    all_to_all x2, waiting for transfers between devices, swap(): return lax.all_to_all(pieces, axes, 0, 0, tiled=True)  6.07 us
    unnamed x12, local copies, waits for them, and re-layouts  2.65 us
  transfers between devices with their start and end apart: 6, of which 2 were waited for; matrix products, arithmetic and copies ran while one was open for 0% of the time, Pallas kernels for 3%

profile of v5, /device:TPU:1, one launch (start us, length us, event | category | flops | bytes accessed | tf_op | source)
XLA Modules:
  0.0 116.4 jit_solution(9616986893724305882)
XLA Ops:
  0.0 0.6 pad_add_fusion.where
  0.6 4.4 %shard_map.46 = (f32[8,48,256]{2,1,0:T(8,128)}, f32[2,16,256]{2,1,0:T(8,128)}, bf16[64,2048]{1,0:T(8,128)(2,1)}, bf16[64,2048]{1,0:T(8,128)(2,1)}, bf16[64,2048]{1,0:T(8,128)(2,1)}, /*index=5*/bf16[64,2048]{1,0:T(8,128)(2,1)}) custom-call(s32[3]{0:T(128)} %pad_add_fusion.where, bf16[2,256,2048]{2,1,0:T(8,128)(2,1)} %blocks.3, bf16[2,2048,128]{2,1,0:T(8,128)(2,1)} %history.3, ...), custom_call_target="tpu_custom_call" | custom-call | flops 268435456 | bytes 4915212 | tf_op jit(solution)/shard_map/pallas_call | solution.py:28
  4.9 10.2 %all-to-all-start = ((f32[8,48,256]{2,1,0:T(8,128)}), f32[8,48,256]{2,1,0:T(8,128)S(1)}, u32[]{:S(2)}, u32[]{:S(2)}) async-start(f32[8,48,256]{2,1,0:T(8,128)} %get-tuple-element.16), calls=%async_computation | async-start | bytes 786432 | tf_op jit(solution)/shard_map/all_to_all | solution.py:16
  15.2 0.7 collective-permute-start
  15.9 0.7 collective-permute-start.1
  16.5 0.7 collective-permute-start.2
  17.3 6.1 %all-to-all-done.got.got1 = f32[8,48,256]{2,1,0:T(8,128)S(1)} async-done(((f32[8,48,256]{2,1,0:T(8,128)}), f32[8,48,256]{2,1,0:T(8,128)S(1)}, u32[]{:S(2)}, u32[]{:S(2)}) %all-to-all-start) | async-done | bytes 393248 | tf_op jit(solution)/shard_map/all_to_all | solution.py:16
  23.3 0.9 copy-done.1
  24.3 1.4 %shard_map.47 = bf16[8,96,256]{2,1,0:T(8,128)(2,1)} custom-call(s32[3]{0:T(128)S(1)} %copy-done.3, f32[8,48,256]{2,1,0:T(8,128)S(1)} %all-to-all-done.got.got1, bf16[64,2048]{1,0:T(8,128)(2,1)S(1)} %copy-done.1, bf16[64,2048]{1,0:T(8,128)(2,1)S(1)} %collective-permute-done.rest_1_, bf16[64,2048]{1,0:T(8,128)(2,1)S(1)} %collective-permute-done.1.rest_2_, ...), custom_call_target="tpu_custom_call" | custom-call | flops 2097152 | bytes 1835020 | tf_op jit(solution)/shard_map/pallas_call | solution.py:28
  25.7 3.5 %all-to-all-start.1 = ((bf16[8,96,256]{2,1,0:T(8,128)(2,1)}), bf16[8,96,256]{2,1,0:T(8,128)(2,1)S(1)}, u32[]{:S(2)}, u32[]{:S(2)}) async-start(bf16[8,96,256]{2,1,0:T(8,128)(2,1)} %shard_map.47), calls=%async_computation.1 | async-start | bytes 786432 | tf_op jit(solution)/shard_map/all_to_all | solution.py:16
  29.2 11.6 %collective-permute-start.3 = (bf16[2048,128]{1,0:T(8,128)(2,1)S(1)}, bf16[2048,128]{1,0:T(8,128)(2,1)S(1)}, u32[]{:S(2)}, u32[]{:S(2)}) collective-permute-start(bf16[2048,128]{1,0:T(8,128)(2,1)S(1)} %slice_bitcast_fusion), channel_id=1, source_target_pairs={{0,8},{8,16},{16,24},{24,32},{32,40},{40,48},{48,56},{56,64},{64,7... | collective-permute-start | bytes 1572872 | tf_op jit(solution)/shard_map/ppermute | solution.py:207
  40.8 6.1 %collective-permute-done.3.before = bf16[2048,128]{1,0:T(8,128)(2,1)S(1)} collective-permute-done((bf16[2048,128]{1,0:T(8,128)(2,1)S(1)}, bf16[2048,128]{1,0:T(8,128)(2,1)S(1)}, u32[]{:S(2)}, u32[]{:S(2)}) %collective-permute-start.3) | collective-permute-done | bytes 524320 | tf_op jit(solution)/shard_map/ppermute | solution.py:207
  46.9 0.8 copy-done.5
  47.7 3.3 %shard_map.48.later = f32[128,256]{1,0:T(8,128)} custom-call(bf16[2,256,2048]{2,1,0:T(8,128)(2,1)} %blocks.3, bf16[2048,128]{1,0:T(8,128)(2,1)} %copy-done.5, bf16[2,2048,128]{2,1,0:T(8,128)(2,1)} %history.3), custom_call_target="tpu_custom_call" | custom-call | flops 268435456 | bytes 3801088 | tf_op jit(solution)/shard_map/pallas_call | solution.py:28
  51.0 0.9 copy-done
  51.9 14.3 %all_to_all.34.got3 = bf16[8,96,256]{2,1,0:T(8,128)(2,1)S(1)} all-to-all(bf16[8,96,256]{2,1,0:T(8,128)(2,1)S(1)} %shard_map.49), channel_id=1, replica_groups=mesh['y'=8,'x'=4,'core'=2,'row'=8] {'x','core'}, dimensions={0} | all-to-all | bytes 786432 | tf_op jit(solution)/shard_map/all_to_all | solution.py:16
  66.2 0.3 shard_map.50
  66.5 13.2 %all_to_all.35.got = f32[8,16,256]{2,1,0:T(8,128)S(1)} all-to-all(f32[8,16,256]{2,1,0:T(8,128)S(1)} %get-tuple-element.22), channel_id=1, replica_groups=mesh['y'=8,'x'=4,'core'=2,'row'=8] {'row'}, dimensions={0} | all-to-all | bytes 262144 | tf_op jit(solution)/shard_map/all_to_all | solution.py:16
  79.8 0.7 shard_map.51
  80.5 16.2 %all_to_all.36.got = f32[8,16,256]{2,1,0:T(8,128)S(1)} all-to-all(f32[8,16,256]{2,1,0:T(8,128)S(1)} %get-tuple-element.25), channel_id=1, replica_groups=mesh['y'=8,'x'=4,'core'=2,'row'=8] {'y'}, dimensions={0} | all-to-all | bytes 262144 | tf_op jit(solution)/shard_map/all_to_all | solution.py:16
  96.7 0.3 shard_map.52
  97.4 17.5 %all_to_all.37 = f32[64,1,576]{2,1,0:T(1,128)S(1)} all-to-all(f32[64,1,576]{2,1,0:T(1,128)S(1)} %all_to_all.26), channel_id=1, replica_groups=mesh['y'=8,'x'=4,'core'=2,'row'=8] {'x','core','row'}, dimensions={0} | all-to-all | bytes 294912 | tf_op jit(solution)/shard_map/all_to_all | solution.py:16
  114.9 0.4 reduce
  115.7 0.6 pad_maximum_fusion
  (25 shorter events, 0.9 us)
Async XLA Ops:
  0.6 22.8 %copy-start.3 = (s32[3]{0:T(128)S(1)}, s32[3]{0:T(128)}, u32[]{:S(2)}) copy-start(s32[3]{0:T(128)} %pad_add_fusion.where) | copy-start | bytes 40
  0.6 28.6 %copy-start.4 = (bf16[2,2048,128]{2,1,0:T(8,128)(2,1)S(1)}, bf16[2,2048,128]{2,1,0:T(8,128)(2,1)}, u32[]{:S(2)}) copy-start(bf16[2,2048,128]{2,1,0:T(8,128)(2,1)} %history.3) | copy-start | bytes 3145732
  4.9 18.4 %all-to-all-start = ((f32[8,48,256]{2,1,0:T(8,128)}), f32[8,48,256]{2,1,0:T(8,128)S(1)}, u32[]{:S(2)}, u32[]{:S(2)}) async-start(f32[8,48,256]{2,1,0:T(8,128)} %get-tuple-element.16), calls=%async_computation | async-start | bytes 786432 | tf_op jit(solution)/shard_map/all_to_all | solution.py:16
  15.2 2.0 %collective-permute-start = (bf16[64,2048]{1,0:T(8,128)(2,1)}, bf16[64,2048]{1,0:T(8,128)(2,1)S(1)}, u32[]{:S(2)}, u32[]{:S(2)}) collective-permute-start(bf16[64,2048]{1,0:T(8,128)(2,1)} %get-tuple-element.18), channel_id=1, source_target_pairs={{0,16},{16,32},{32,48},{48,0},{1,17},{17,33},{33,49},{49,1},{2,18}... | collective-permute-start | bytes 786440 | tf_op jit(solution)/shard_map/ppermute | solution.py:222
  15.9 1.4 %collective-permute-start.1 = (bf16[64,2048]{1,0:T(8,128)(2,1)}, bf16[64,2048]{1,0:T(8,128)(2,1)S(1)}, u32[]{:S(2)}, u32[]{:S(2)}) collective-permute-start(bf16[64,2048]{1,0:T(8,128)(2,1)} %get-tuple-element.19), channel_id=1, source_target_pairs={{0,32},{16,48},{32,0},{48,16},{1,33},{17,49},{33,1},{49,17},{2,34}... | collective-permute-start | bytes 786440 | tf_op jit(solution)/shard_map/ppermute | solution.py:222
  16.5 0.7 collective-permute-start.2
  23.3 1.0 copy-start.1
  25.7 25.3 %all-to-all-start.1 = ((bf16[8,96,256]{2,1,0:T(8,128)(2,1)}), bf16[8,96,256]{2,1,0:T(8,128)(2,1)S(1)}, u32[]{:S(2)}, u32[]{:S(2)}) async-start(bf16[8,96,256]{2,1,0:T(8,128)(2,1)} %shard_map.47), calls=%async_computation.1 | async-start | bytes 786432 | tf_op jit(solution)/shard_map/all_to_all | solution.py:16
  29.2 37.0 %copy-start.2 = (f32[2,16,256]{2,1,0:T(8,128)S(1)}, f32[2,16,256]{2,1,0:T(8,128)}, u32[]{:S(2)}) copy-start(f32[2,16,256]{2,1,0:T(8,128)} %get-tuple-element.21.field) | copy-start | bytes 98308
  29.2 17.7 %collective-permute-start.3 = (bf16[2048,128]{1,0:T(8,128)(2,1)S(1)}, bf16[2048,128]{1,0:T(8,128)(2,1)S(1)}, u32[]{:S(2)}, u32[]{:S(2)}) collective-permute-start(bf16[2048,128]{1,0:T(8,128)(2,1)S(1)} %slice_bitcast_fusion), channel_id=1, source_target_pairs={{0,8},{8,16},{16,24},{24,32},{32,40},{40,48},{48,56},{56,64},{64,7... | collective-permute-start | bytes 1572872 | tf_op jit(solution)/shard_map/ppermute | solution.py:207
  46.9 0.8 copy-start.5
  51.0 0.9 copy-start

commit v6 on v4

v6 whole, which is shorter than its diff:
```python
import numpy as np
import jax
import jax.numpy as jnp
from jax import lax
from jax.experimental import pallas as pl
from jax.experimental.pallas import tpu as pltpu
from jax.sharding import Mesh, PartitionSpec as P

LAG = ("y", "x", "core")
W = ("x", "core")
F32 = jnp.float32
BF16 = jnp.bfloat16


def swap(pieces, axes):
    return lax.all_to_all(pieces, axes, 0, 0, tiled=True)


def call(body, outs, flops, *args, scratch=(), held=None, given=None, limit=24):
    single = not isinstance(outs, list)
    outs = [outs] if single else outs
    shapes = [jax.ShapeDtypeStruct(s, d) for s, d in outs]
    size = sum(a.size * a.dtype.itemsize for a in args)
    size += sum(s.size * s.dtype.itemsize for s in shapes)
    held = held or [pltpu.VMEM] * len(args)
    given = given or [pltpu.VMEM] * len(outs)
    specs = [pl.BlockSpec(memory_space=m) for m in given]
    return pl.pallas_call(
        body,
        out_shape=shapes[0] if single else shapes,
        in_specs=[pl.BlockSpec(memory_space=m) for m in held],
        out_specs=specs[0] if single else specs,
        scratch_shapes=scratch,
        cost_estimate=pl.CostEstimate(flops=flops, bytes_accessed=size, transcendentals=0),
        compiler_params=pltpu.CompilerParams(vmem_limit_bytes=limit * 1024 * 1024),
    )(*args)


def mm(left, right, precision=None):
    return jnp.dot(left, right, precision=precision, preferred_element_type=F32)


def mm_t(left, right, precision=None):
    return lax.dot_general(
        left, right, (((1,), (1,)), ((), ())), precision=precision, preferred_element_type=F32
    )


def parts(array):
    high = array.astype(BF16)
    return high, (array - high.astype(F32)).astype(BF16)


def sum_first(ref, start, stop):
    total = ref[0, start:stop].astype(F32)
    for i in range(1, ref.shape[0]):
        total = total + ref[i, start:stop].astype(F32)
    return total


def first_sums(blocks, history, excitation, inverse, out, field, *rest):
    pieces, (b, h, e, own, turned, slabs, o, f, sems) = rest[:-9], rest[-9:]
    loads = [
        pltpu.make_async_copy(history.at[0], h.at[0], sems.at[0]),
        pltpu.make_async_copy(blocks.at[0], b.at[0], sems.at[1]),
        pltpu.make_async_copy(history.at[1], h.at[1], sems.at[2]),
        pltpu.make_async_copy(blocks.at[1], b.at[1], sems.at[3]),
        pltpu.make_async_copy(inverse, own, sems.at[4]),
        pltpu.make_async_copy(excitation, e, sems.at[5]),
    ]
    for load in loads:
        load.start()
    nw, depth, rows = out.shape
    cw = depth - own.shape[0]
    loads[0].wait()
    loads[1].wait()
    total = mm(b[0], h[0])
    loads[2].wait()
    loads[3].wait()
    total = (total + mm(b[1], h[1])).T
    loads[4].wait()
    for w in range(nw):
        o[w, :cw] = total[w * cw : (w + 1) * cw]
        o[w, cw:] = own[...]
    store = pltpu.make_async_copy(o, out, sems.at[6])
    store.start()
    loads[5].wait()
    start = pl.multiple_of(lax.axis_index(W) * cw, cw)
    for s in range(e.shape[0]):
        turned[...] = e[s].T
        f[s] = turned[pl.ds(start, cw)]
    other = pltpu.make_async_copy(f, field, sems.at[7])
    other.start()

    @pl.when(lax.axis_index(LAG) == 0)
    def _():
        nx = len(pieces)
        span = nw * own.shape[0]
        cut = span // nx
        for y in range(b.shape[2] // span):
            slab = b[0, :, y * span : (y + 1) * span].T
            for x in range(nx):
                slabs[x, y * cut : (y + 1) * cut] = slab[x * cut : (x + 1) * cut]
        stores = []
        for x in range(nx):
            stores.append(pltpu.make_async_copy(slabs.at[x], pieces[x], sems.at[8 + x]))
            stores[-1].start()
        for s in stores:
            s.wait()

    store.wait()
    other.wait()


def later_sums(blocks, before, history, out):
    out[...] = (mm(blocks[1], history[0]) + mm(blocks[0], before[...])).T


def second_step(got, *rest):
    sources, (out, piece, sem) = rest[:-3], rest[-3:]
    for k, source in enumerate(sources):

        @pl.when(lax.axis_index("x") == k)
        def _():
            pltpu.make_async_copy(source, piece, sem).start()

    peers, depth, _ = out.shape
    cut = piece.shape[0] // peers
    cw = (depth - cut) // 2
    high, low = parts(sum_first(got, 0, cw))
    for i in range(peers):
        out[i, :cw] = high
        out[i, cw : 2 * cw] = low
    pltpu.make_async_copy(sources[0], piece, sem).wait()
    for i in range(peers):
        out[i, 2 * cw :] = piece[i * cut : (i + 1) * cut]


def third_step(got1, got2, field, out):
    cw = out.shape[0]
    inverse = got1[:, cw:].reshape(-1, out.shape[1])
    core = lax.axis_index("core")
    total = field[0]
    for y in range(got2.shape[0] // 2):
        pair = got2[2 * y + core, : 2 * cw].astype(F32)
        total = total - (pair[:cw] + pair[cw:])
    out[...] = mm_t(total, inverse, lax.Precision.HIGHEST)


def fourth_step(current, got2, later, out):
    nw, cw, _ = out.shape
    first = got2[0, 2 * cw :]
    total = later[...] + mm(current[...].astype(BF16), first)
    for w in range(nw):
        out[w] = total[w * cw : (w + 1) * cw]


def fifth_step(got, out):
    total = sum_first(got, 0, got.shape[1])
    for y in range(out.shape[0]):
        out[y] = total


def sixth_step(got1, got, field, out):
    cw = got.shape[1]
    inverse = got1[:, cw:].reshape(-1, got.shape[2])
    resid = field[1] - sum_first(got, 0, cw)
    out[...] = mm_t(resid, inverse, lax.Precision.HIGHEST)


def to_owners(terms, nw, nz):
    cw, span = terms.shape
    own = span // nw
    sends = terms.reshape(cw, nw, own).transpose(1, 0, 2).reshape(nw, 1, cw * own)
    sends = jnp.broadcast_to(sends, (nw, nz, cw * own)).reshape(nw * nz, cw * own)
    got = swap(sends, W + ("row",)).reshape(nw, nz, cw, own)
    return jnp.sum(got, axis=1).reshape(nw * cw, own)


def shards(blocks, history, excitation, self_inverse):
    ny, nx, nc, nz = (lax.axis_size(a) for a in ("y", "x", "core", "row"))
    nw = nx * nc
    rows, size = blocks.shape[1:]
    columns = history.shape[2]
    cw = columns // nw
    own = self_inverse.shape[0]
    nlag = ny * nw
    span = nw * own
    work = 2 * rows * size * columns * 2
    small = 2 * cw * rows * span

    before = lax.ppermute(history[1], LAG, [(i, i + 1) for i in range(nlag - 1)])
    later = call(later_sums, ((columns, rows), F32), work, blocks, before, history)

    part = (ny * nc * own, rows)
    outs = [((nw, cw + own, rows), F32), ((2, cw, rows), F32)] + [(part, BF16)] * nx
    scratch = [pltpu.VMEM(a.shape, a.dtype) for a in (blocks, history, excitation, self_inverse)]
    scratch += [pltpu.VMEM((columns, rows), F32), pltpu.VMEM((nx, *part), BF16)]
    scratch += [pltpu.VMEM(*o) for o in outs[:2]] + [pltpu.SemaphoreType.DMA((8 + nx,))]
    args = blocks, history, excitation, self_inverse
    held, given = [pltpu.HBM] * len(args), [pltpu.HBM] * len(outs)
    send, field, *pieces = call(
        first_sums, outs, work, *args, scratch=scratch, held=held, given=given, limit=60
    )
    got1 = swap(send, W)
    for k in range(1, nx):
        pieces[k] = lax.ppermute(pieces[k], LAG, [(0, k * nc)])
    got1, later = lax.optimization_barrier((got1, later))
    send = call(
        second_step,
        ((ny * nc, 2 * cw + own, rows), BF16),
        small,
        got1,
        *pieces,
        scratch=[pltpu.VMEM(part, BF16), pltpu.SemaphoreType.DMA(())],
        held=[pltpu.VMEM] + [pltpu.HBM] * nx,
    )
    got2 = swap(send, ("y", "core"))
    term = call(third_step, ((cw, span), F32), small, got1, got2, field)
    current0 = to_owners(term, nw, nz)
    send = call(fourth_step, ((nw, cw, rows), F32), small, current0, got2, later)
    got4 = swap(send, W)
    send = call(fifth_step, ((ny, cw, rows), F32), small, got4)
    got5 = swap(send, "y")
    term = call(sixth_step, ((cw, span), F32), small, got1, got5, field)
    current1 = to_owners(term, nw, nz)
    current0, current1 = lax.optimization_barrier((current0, current1))
    return jnp.stack([current0.T, current1.T])


def solution(mesh):
    n_row = mesh.shape["row"]
    fine = Mesh(np.asarray(mesh.devices).reshape(-1, 4, 2, n_row), ("y", "x", "core", "row"))
    return jax.shard_map(
        shards,
        mesh=fine,
        in_specs=(
            P(LAG, "row", None),
            P(LAG, None, None),
            P(None, "row", None),
            P(LAG, "row"),
        ),
        out_specs=P(None, LAG, None),
        check_vma=False,
    )
```

time: 108 us -> 113 us (1.046)
  blocking collectives: 76.3 us -> 80.8 us
  local copies, waits for them, and re-layouts: 2.39 us -> 5.44 us
  Pallas kernels: 7.32 us -> 6.14 us
    all_to_all x5, blocking collectives: 76.3 us -> 80.8 us  [swap(): return lax.all_to_all(pieces, axes, 0, 0, tiled=True)]
    squeeze x1, local copies, waits for them, and re-layouts: 0.03 us -> 1.87 us  [shards(): history[1]]
    all_to_all x1, starting transfers between devices: 10.2 us -> 8.44 us  [swap(): return lax.all_to_all(pieces, axes, 0, 0, tiled=True)]
    ppermute x1, waiting for transfers between devices: 1.79 us -> 0.01 us  [shards(): lax.ppermute(history[1], LAG, [(i, i + 1) for i in range(nlag - 1)])]
    unnamed x12 -> x14, local copies, waits for them, and re-layouts: 0.68 us -> 2.36 us
    all_to_all x1, waiting for transfers between devices: 0.01 us -> 1.55 us  [swap(): return lax.all_to_all(pieces, axes, 0, 0, tiled=True)]
    ppermute x1, starting transfers between devices: 3.55 us -> 4.76 us  [shards(): lax.ppermute(history[1], LAG, [(i, i + 1) for i in range(nlag - 1)])]
    pallas_call x7, Pallas kernels: 7.32 us -> 6.14 us  [call(): pl.pallas_call(body, out_shape=shapes[0] if single else shapes, in_specs=...]
  transfers between devices with their start and end apart: 5 -> 5, of which waited for: 1 -> 1; matrix products, arithmetic and copies ran while one was open for 1% -> 0% of each run, Pallas kernels for 1% -> 5%
where the time goes in v6:
time: 113 us
  blocking collectives  80.8 us (72%)
  starting transfers between devices  17.3 us (15%)
  Pallas kernels  6.14 us (5%)
  local copies, waits for them, and re-layouts  5.44 us (5%)
  waiting for transfers between devices  1.56 us (1%)
  other arithmetic  1.34 us (1%)
    all_to_all x5, blocking collectives, swap(): return lax.all_to_all(pieces, axes, 0, 0, tiled=True)  80.8 us
    all_to_all x1, starting transfers between devices, swap(): return lax.all_to_all(pieces, axes, 0, 0, tiled=True)  8.44 us
    pallas_call x7, Pallas kernels, call(): pl.pallas_call(body, out_shape=shapes[0] if single else shapes, in_specs=...  6.14 us
    ppermute x1, starting transfers between devices, shards(): lax.ppermute(history[1], LAG, [(i, i + 1) for i in range(nlag - 1)])  4.76 us
    ppermute x3, starting transfers between devices, shards(): pieces[k] = lax.ppermute(pieces[k], LAG, [(0, k * nc)])  4.08 us
    unnamed x14, local copies, waits for them, and re-layouts  2.36 us
  transfers between devices with their start and end apart: 5, of which 1 were waited for; matrix products, arithmetic and copies ran while one was open for 0% of the time, Pallas kernels for 5%

profile of v6, /device:TPU:1, one launch (start us, length us, event | category | flops | bytes accessed | tf_op | source)
XLA Modules:
  0.0 112.7 jit_solution(9856744677160732681)
XLA Ops:
  0.0 1.9 %slice_bitcast_fusion = bf16[2048,128]{1,0:T(8,128)(2,1)} fusion(bf16[2,2048,128]{2,1,0:T(8,128)(2,1)} %history.3), kind=kLoop, calls=%fused_computation | loop fusion | bytes 1048576 | tf_op jit(solution)/shard_map/squeeze | solution.py:192
  1.9 4.8 %collective-permute-start = (bf16[2048,128]{1,0:T(8,128)(2,1)}, bf16[2048,128]{1,0:T(8,128)(2,1)}, u32[]{:S(2)}, u32[]{:S(2)}) collective-permute-start(bf16[2048,128]{1,0:T(8,128)(2,1)} %slice_bitcast_fusion), channel_id=1, source_target_pairs={{0,8},{8,16},{16,24},{24,32},{32,40},{40,48},{48,56},{56,64},{64,7... | collective-permute-start | bytes 1572872 | tf_op jit(solution)/shard_map/ppermute | solution.py:192
  6.6 3.5 %shard_map.46 = (f32[8,48,256]{2,1,0:T(8,128)}, f32[2,16,256]{2,1,0:T(8,128)}, bf16[512,256]{1,0:T(8,128)(2,1)}, bf16[512,256]{1,0:T(8,128)(2,1)}, bf16[512,256]{1,0:T(8,128)(2,1)}, /*index=5*/bf16[512,256]{1,0:T(8,128)(2,1)}) custom-call(bf16[2,256,2048]{2,1,0:T(8,128)(2,1)} %blocks.3, bf16[2,2048,128]{2,1,0:T(8,128)(2,1)} %history.3, ...), custom_call_target="tpu_custom_call" | custom-call | flops 268435456 | bytes 4915200 | tf_op jit(solution)/shard_map/pallas_call | solution.py:28
  10.2 8.4 %all-to-all-start = ((f32[8,48,256]{2,1,0:T(8,128)}), f32[8,48,256]{2,1,0:T(8,128)S(1)}, u32[]{:S(2)}, u32[]{:S(2)}) async-start(f32[8,48,256]{2,1,0:T(8,128)} %get-tuple-element.15), calls=%async_computation | async-start | bytes 786432 | tf_op jit(solution)/shard_map/all_to_all | solution.py:16
  18.6 1.4 %collective-permute-start.1 = (bf16[512,256]{1,0:T(8,128)(2,1)}, bf16[512,256]{1,0:T(8,128)(2,1)}, u32[]{:S(2)}, u32[]{:S(2)}) collective-permute-start(bf16[512,256]{1,0:T(8,128)(2,1)} %get-tuple-element.18), channel_id=1, source_target_pairs={{0,16},{1,17},{2,18},{3,19},{4,20},{5,21},{6,22},{7,23}} | collective-permute-start | bytes 786440 | tf_op jit(solution)/shard_map/ppermute | solution.py:207
  20.0 1.4 %collective-permute-start.2 = (bf16[512,256]{1,0:T(8,128)(2,1)}, bf16[512,256]{1,0:T(8,128)(2,1)}, u32[]{:S(2)}, u32[]{:S(2)}) collective-permute-start(bf16[512,256]{1,0:T(8,128)(2,1)} %get-tuple-element.19), channel_id=1, source_target_pairs={{0,32},{1,33},{2,34},{3,35},{4,36},{5,37},{6,38},{7,39}} | collective-permute-start | bytes 786440 | tf_op jit(solution)/shard_map/ppermute | solution.py:207
  21.3 1.4 %collective-permute-start.3 = (bf16[512,256]{1,0:T(8,128)(2,1)}, bf16[512,256]{1,0:T(8,128)(2,1)}, u32[]{:S(2)}, u32[]{:S(2)}) collective-permute-start(bf16[512,256]{1,0:T(8,128)(2,1)} %get-tuple-element.20), channel_id=1, source_target_pairs={{0,48},{1,49},{2,50},{3,51},{4,52},{5,53},{6,54},{7,55}} | collective-permute-start | bytes 786440 | tf_op jit(solution)/shard_map/ppermute | solution.py:207
  22.7 1.8 %shard_map.47.later = f32[128,256]{1,0:T(8,128)S(1)} custom-call(bf16[2,256,2048]{2,1,0:T(8,128)(2,1)S(1)} %copy-done, bf16[2048,128]{1,0:T(8,128)(2,1)} %collective-permute-done.before, bf16[2,2048,128]{2,1,0:T(8,128)(2,1)S(1)} %copy-done.1), custom_call_target="tpu_custom_call" | custom-call | flops 268435456 | bytes 3801088 | tf_op jit(solution)/shard_map/pallas_call | solution.py:28
  24.5 0.6 copy-done.2
  25.2 1.5 %all-to-all-done.got.got1 = f32[8,48,256]{2,1,0:T(8,128)S(1)} async-done(((f32[8,48,256]{2,1,0:T(8,128)}), f32[8,48,256]{2,1,0:T(8,128)S(1)}, u32[]{:S(2)}, u32[]{:S(2)}) %all-to-all-start) | async-done | bytes 393248 | tf_op jit(solution)/shard_map/all_to_all | solution.py:16
  26.7 0.9 copy-done.4
  27.8 24.8 %all_to_all.38.got2 = bf16[16,64,256]{2,1,0:T(8,128)(2,1)S(1)} all-to-all(bf16[16,64,256]{2,1,0:T(8,128)(2,1)S(1)} %shard_map.48), channel_id=1, replica_groups=mesh['y'=8,'x'=4,'core'=2,'row'=8] {'y','core'}, dimensions={0} | all-to-all | bytes 1048576 | tf_op jit(solution)/shard_map/all_to_all | solution.py:16
  52.6 0.8 copy-done.5
  53.3 0.3 shard_map.49
  54.0 20.5 %all_to_all.39 = f32[64,1,512]{2,1,0:T(1,128)S(1)} all-to-all(f32[64,1,512]{2,1,0:T(1,128)S(1)} %all_to_all.26), channel_id=1, replica_groups=mesh['y'=8,'x'=4,'core'=2,'row'=8] {'x','core','row'}, dimensions={0} | all-to-all | bytes 262144 | tf_op jit(solution)/shard_map/all_to_all | solution.py:16
  74.5 0.3 reduce
  74.8 0.2 reshape.33
  75.2 9.7 %all_to_all.40.got = f32[8,16,256]{2,1,0:T(8,128)S(1)} all-to-all(f32[8,16,256]{2,1,0:T(8,128)S(1)} %shard_map.50), channel_id=1, replica_groups=mesh['y'=8,'x'=4,'core'=2,'row'=8] {'x','core'}, dimensions={0} | all-to-all | bytes 262144 | tf_op jit(solution)/shard_map/all_to_all | solution.py:16
  84.9 10.1 %all_to_all.41.got = f32[8,16,256]{2,1,0:T(8,128)S(1)} all-to-all(f32[8,16,256]{2,1,0:T(8,128)S(1)} %shard_map.51), channel_id=1, replica_groups=mesh['y'=8,'x'=4,'core'=2,'row'=8] {'y'}, dimensions={0} | all-to-all | bytes 262144 | tf_op jit(solution)/shard_map/all_to_all | solution.py:16
  95.0 0.3 shard_map.52
  95.7 15.7 %all_to_all.42 = f32[64,1,512]{2,1,0:T(1,128)S(1)} all-to-all(f32[64,1,512]{2,1,0:T(1,128)S(1)} %all_to_all.30), channel_id=1, replica_groups=mesh['y'=8,'x'=4,'core'=2,'row'=8] {'x','core','row'}, dimensions={0} | all-to-all | bytes 262144 | tf_op jit(solution)/shard_map/all_to_all | solution.py:16
  111.4 0.3 reduce.1
  111.7 0.2 reshape.36
  112.1 0.6 pad_maximum_fusion
  (32 shorter events, 1.2 us)
Async XLA Ops:
  1.9 20.8 %copy-start = (bf16[2,256,2048]{2,1,0:T(8,128)(2,1)S(1)}, bf16[2,256,2048]{2,1,0:T(8,128)(2,1)}, u32[]{:S(2)}) copy-start(bf16[2,256,2048]{2,1,0:T(8,128)(2,1)} %blocks.3) | copy-start | bytes 6291460
  1.9 20.8 %copy-start.1 = (bf16[2,2048,128]{2,1,0:T(8,128)(2,1)S(1)}, bf16[2,2048,128]{2,1,0:T(8,128)(2,1)}, u32[]{:S(2)}) copy-start(bf16[2,2048,128]{2,1,0:T(8,128)(2,1)} %history.3) | copy-start | bytes 3145732
  1.9 20.8 %collective-permute-start = (bf16[2048,128]{1,0:T(8,128)(2,1)}, bf16[2048,128]{1,0:T(8,128)(2,1)}, u32[]{:S(2)}, u32[]{:S(2)}) collective-permute-start(bf16[2048,128]{1,0:T(8,128)(2,1)} %slice_bitcast_fusion), channel_id=1, source_target_pairs={{0,8},{8,16},{16,24},{24,32},{32,40},{40,48},{48,56},{56,64},{64,7... | collective-permute-start | bytes 1572872 | tf_op jit(solution)/shard_map/ppermute | solution.py:192
  10.2 16.5 %all-to-all-start = ((f32[8,48,256]{2,1,0:T(8,128)}), f32[8,48,256]{2,1,0:T(8,128)S(1)}, u32[]{:S(2)}, u32[]{:S(2)}) async-start(f32[8,48,256]{2,1,0:T(8,128)} %get-tuple-element.15), calls=%async_computation | async-start | bytes 786432 | tf_op jit(solution)/shard_map/all_to_all | solution.py:16
  18.6 8.1 %collective-permute-start.1 = (bf16[512,256]{1,0:T(8,128)(2,1)}, bf16[512,256]{1,0:T(8,128)(2,1)}, u32[]{:S(2)}, u32[]{:S(2)}) collective-permute-start(bf16[512,256]{1,0:T(8,128)(2,1)} %get-tuple-element.18), channel_id=1, source_target_pairs={{0,16},{1,17},{2,18},{3,19},{4,20},{5,21},{6,22},{7,23}} | collective-permute-start | bytes 786440 | tf_op jit(solution)/shard_map/ppermute | solution.py:207
  20.0 6.7 %collective-permute-start.2 = (bf16[512,256]{1,0:T(8,128)(2,1)}, bf16[512,256]{1,0:T(8,128)(2,1)}, u32[]{:S(2)}, u32[]{:S(2)}) collective-permute-start(bf16[512,256]{1,0:T(8,128)(2,1)} %get-tuple-element.19), channel_id=1, source_target_pairs={{0,32},{1,33},{2,34},{3,35},{4,36},{5,37},{6,38},{7,39}} | collective-permute-start | bytes 786440 | tf_op jit(solution)/shard_map/ppermute | solution.py:207
  21.3 5.4 %collective-permute-start.3 = (bf16[512,256]{1,0:T(8,128)(2,1)}, bf16[512,256]{1,0:T(8,128)(2,1)}, u32[]{:S(2)}, u32[]{:S(2)}) collective-permute-start(bf16[512,256]{1,0:T(8,128)(2,1)} %get-tuple-element.20), channel_id=1, source_target_pairs={{0,48},{1,49},{2,50},{3,51},{4,52},{5,53},{6,54},{7,55}} | collective-permute-start | bytes 786440 | tf_op jit(solution)/shard_map/ppermute | solution.py:207
  24.5 0.7 copy-start.2
  26.7 1.0 copy-start.4
  27.8 47.2 %copy-start.3 = (f32[128,256]{1,0:T(8,128)S(1)}, f32[128,256]{1,0:T(8,128)}, u32[]{:S(2)}) copy-start(f32[128,256]{1,0:T(8,128)} %copy-done.2) | copy-start | bytes 393220
  52.6 0.8 copy-start.5
  53.6 41.4 %copy-start.6 = (f32[2,16,256]{2,1,0:T(8,128)S(1)}, f32[2,16,256]{2,1,0:T(8,128)}, u32[]{:S(2)}) copy-start(f32[2,16,256]{2,1,0:T(8,128)} %get-tuple-element.21.field) | copy-start | bytes 98308

commit v7 on v5

v7 whole, which is shorter than its diff:
```python
import numpy as np
import jax
import jax.numpy as jnp
from jax import lax
from jax.experimental import pallas as pl
from jax.experimental.pallas import tpu as pltpu
from jax.sharding import Mesh, PartitionSpec as P

LAG = ("y", "x", "core")
W = ("x", "core")
F32 = jnp.float32
BF16 = jnp.bfloat16


def swap(pieces, axes):
    return lax.all_to_all(pieces, axes, 0, 0, tiled=True)


def call(body, outs, flops, *args, scratch=(), held=None, given=None, limit=24):
    single = not isinstance(outs, list)
    outs = [outs] if single else outs
    shapes = [jax.ShapeDtypeStruct(s, d) for s, d in outs]
    size = sum(a.size * a.dtype.itemsize for a in args)
    size += sum(s.size * s.dtype.itemsize for s in shapes)
    held = held or [pltpu.VMEM] * len(args)
    given = given or [pltpu.VMEM] * len(outs)
    specs = [pl.BlockSpec(memory_space=m) for m in given]
    return pl.pallas_call(
        body,
        out_shape=shapes[0] if single else shapes,
        in_specs=[pl.BlockSpec(memory_space=m) for m in held],
        out_specs=specs[0] if single else specs,
        scratch_shapes=scratch,
        cost_estimate=pl.CostEstimate(flops=flops, bytes_accessed=size, transcendentals=0),
        compiler_params=pltpu.CompilerParams(vmem_limit_bytes=limit * 1024 * 1024),
    )(*args)


def mm(left, right, precision=None):
    return jnp.dot(left, right, precision=precision, preferred_element_type=F32)


def mm_t(left, right, precision=None):
    return lax.dot_general(
        left, right, (((1,), (1,)), ((), ())), precision=precision, preferred_element_type=F32
    )


def parts(array):
    high = array.astype(BF16)
    return high, (array - high.astype(F32)).astype(BF16)


def sum_first(ref, start, stop):
    total = ref[0, start:stop].astype(F32)
    for i in range(1, ref.shape[0]):
        total = total + ref[i, start:stop].astype(F32)
    return total


def sum_pairs(ref, start, count):
    return sum_first(ref, start, start + count) + sum_first(ref, start + count, start + 2 * count)


def less_field(total, field):
    return jnp.where(lax.axis_index(LAG) == 0, total - field, total).T


def last_of(history, out, sems):
    count = sems.shape[0]
    step = out.shape[0] // count
    loads = []
    for i in range(count):
        rows = pl.ds(i * step, step)
        loads.append(pltpu.make_async_copy(history.at[1, rows], out.at[rows], sems.at[i]))
        loads[-1].start()
    for load in loads:
        load.wait()


def first_sums(blocks, history, excitation, inverse, out, lead, *rest):
    pieces, (b, h, e, own, o, f, sems) = rest[:-7], rest[-7:]
    cut = pieces[0].shape[0]
    loads = [
        pltpu.make_async_copy(history.at[0], h.at[0], sems.at[0]),
        pltpu.make_async_copy(blocks.at[0], b.at[0], sems.at[1]),
        pltpu.make_async_copy(history.at[1], h.at[1], sems.at[2]),
        pltpu.make_async_copy(blocks.at[1], b.at[1], sems.at[3]),
        pltpu.make_async_copy(inverse, own, sems.at[4]),
        pltpu.make_async_copy(excitation, e, sems.at[5]),
    ]
    for load in loads:
        load.start()
    nw, depth, _ = out.shape
    cw = depth - own.shape[0]
    loads[0].wait()
    loads[1].wait()
    stores = []
    for k, piece in enumerate(pieces):
        rows = b.at[0, (k + 1) * cut : (k + 2) * cut]
        stores.append(pltpu.make_async_copy(rows, piece, sems.at[8 + k]))
        stores[-1].start()
    total = mm(b[0], h[0])
    loads[2].wait()
    loads[3].wait()
    total = total + mm(b[1], h[1])
    loads[4].wait()
    loads[5].wait()
    total = less_field(total, e[0])
    for w in range(nw):
        o[w, :cw] = total[w * cw : (w + 1) * cw]
        o[w, cw:] = own[...]
    stores.append(pltpu.make_async_copy(o, out, sems.at[6]))
    stores[-1].start()
    f[...] = less_field(jnp.zeros_like(e[1]), e[1])
    stores.append(pltpu.make_async_copy(f, lead, sems.at[7]))
    stores[-1].start()
    for store in stores:
        store.wait()


def later_sums(blocks, before, history, out):
    out[...] = (mm(blocks[1], history[0]) + mm(blocks[0], before[...])).T


def second_step(got, blocks, *rest):
    sources, (out, piece, sem) = rest[:-3], rest[-3:]
    sources = (blocks.at[0, : piece.shape[0]], *sources)
    for k, source in enumerate(sources):

        @pl.when(lax.axis_index("x") == k)
        def _():
            pltpu.make_async_copy(source, piece, sem).start()

    ny, depth, span = out.shape
    cw = (depth - piece.shape[0]) // 2
    high, low = parts(sum_first(got, 0, cw))
    for y in range(ny):
        out[y, :cw] = high
        out[y, cw : 2 * cw] = low
    pltpu.make_async_copy(sources[0], piece, sem).wait()
    for y in range(ny):
        out[y, 2 * cw :] = piece[:, y * span : (y + 1) * span]


def third_step(got, later, lead, out):
    nw = out.shape[0]
    cw = later.shape[0] // nw
    total = later[...] + lead[...]
    for w in range(nw):
        high, low = parts(total[w * cw : (w + 1) * cw])
        out[w, :cw] = high
        out[w, cw : 2 * cw] = low
        out[w, 2 * cw :] = got[0, 2 * cw :]


def fourth_step(got1, got2, got3, out, part1, first):
    nz, cw, rows = out.shape
    inverse = got1[:, cw:].reshape(-1, rows)
    term = -mm_t(sum_pairs(got2, 0, cw), inverse, lax.Precision.HIGHEST)
    for z in range(nz):
        out[z] = term
    part1[...] = sum_pairs(got3, 0, cw)
    cut = got3.shape[1] - 2 * cw
    for x in range(first.shape[0] // cut):
        first[x * cut : (x + 1) * cut] = got3[2 * x, 2 * cw :]


def fifth_step(got, part1, first, out, mine):
    value = sum_first(got, 0, got.shape[1])
    total = part1[...] + mm_t(value.astype(BF16), first[...])
    for y in range(out.shape[0]):
        out[y] = total
    cz = mine.shape[0]
    share = value[:cz]
    for z in range(1, value.shape[0] // cz):
        share = jnp.where(lax.axis_index("row") == z, value[z * cz : (z + 1) * cz], share)
    mine[...] = share


def sixth_step(got1, got, mine, out):
    cw = got.shape[1]
    inverse = got1[:, cw:].reshape(-1, got.shape[2])
    out[:cw] = -mm_t(sum_first(got, 0, cw), inverse, lax.Precision.HIGHEST)
    out[cw:] = mine[...]


def shards(blocks, history, excitation, self_inverse):
    ny, nx, nc, nz = (lax.axis_size(a) for a in ("y", "x", "core", "row"))
    nw = nx * nc
    rows, size = blocks.shape[1:]
    columns = history.shape[2]
    cw = columns // nw
    own = self_inverse.shape[0]
    nlag = ny * nw
    cut = rows // nx
    span = nw * own
    work = 2 * rows * size * columns * 2
    small = 2 * cw * rows * span

    before = call(
        last_of,
        (history.shape[1:], BF16),
        0,
        history,
        scratch=[pltpu.SemaphoreType.DMA((4,))],
        held=[pltpu.HBM],
        given=[pltpu.HBM],
        limit=60,
    )
    before = lax.ppermute(before, LAG, [(i, i + 1) for i in range(nlag - 1)])
    later = call(later_sums, ((columns, rows), F32), work, blocks, before, history)

    outs = [((nw, cw + own, rows), F32), ((columns, rows), F32)] + [((cut, size), BF16)] * (nx - 1)
    scratch = [pltpu.VMEM(blocks.shape, BF16), pltpu.VMEM(history.shape, BF16)]
    scratch += [pltpu.VMEM(excitation.shape, F32), pltpu.VMEM((own, rows), F32)]
    scratch += [pltpu.VMEM(*o) for o in outs[:2]] + [pltpu.SemaphoreType.DMA((8 + nx,))]
    args = blocks, history, excitation, self_inverse
    held, given = [pltpu.HBM] * len(args), [pltpu.HBM] * len(outs)
    send, lead, *pieces = call(
        first_sums, outs, work, *args, scratch=scratch, held=held, given=given, limit=60
    )
    got1 = swap(send, W)
    for k in range(1, nx):
        pieces[k - 1] = lax.ppermute(pieces[k - 1], LAG, [(0, k * nc)])
    got1, later = lax.optimization_barrier((got1, later))
    send = call(
        second_step,
        ((ny, 2 * cw + cut, span), BF16),
        small,
        got1,
        blocks,
        *pieces,
        scratch=[pltpu.VMEM((cut, size), BF16), pltpu.SemaphoreType.DMA(())],
        held=[pltpu.VMEM] + [pltpu.HBM] * nx,
    )
    got2 = swap(send, "y")
    send = call(third_step, ((nw, 2 * cw + cut, rows), BF16), small, got2, later, lead)
    got3 = swap(send, W)
    outs = [((nz, cw, rows), F32), ((cw, rows), F32), ((rows, span), BF16)]
    send, part1, first = call(fourth_step, outs, small, got1, got2, got3)
    got4 = swap(send, "row")
    cz = cw // nz
    outs = [((ny, cw, rows), F32), ((cz, span), F32)]
    send, mine0 = call(fifth_step, outs, small, got4, part1, first)
    got5 = swap(send, "y")
    both = call(sixth_step, ((cw + cz, span), F32), small, got1, got5, mine0)
    both = both.reshape(cw + cz, nw, own).transpose(1, 0, 2).reshape(nw, 1, (cw + cz) * own)
    both = jnp.broadcast_to(both, (nw, nz, (cw + cz) * own)).reshape(nw * nz, (cw + cz) * own)
    got = swap(both, W + ("row",)).reshape(nw, nz, cw + cz, own)
    out1 = jnp.sum(got[:, :, :cw], axis=1).reshape(columns, own)
    out0 = got[:, :, cw:].reshape(columns, own)
    return jnp.stack([out0.T, out1.T])


def solution(mesh):
    n_row = mesh.shape["row"]
    fine = Mesh(np.asarray(mesh.devices).reshape(-1, 4, 2, n_row), ("y", "x", "core", "row"))
    return jax.shard_map(
        shards,
        mesh=fine,
        in_specs=(
            P(LAG, "row", None),
            P(LAG, None, None),
            P(None, "row", None),
            P(LAG, "row"),
        ),
        out_specs=P(None, LAG, None),
        check_vma=False,
    )
```

time: 117 us -> 120 us (1.026)
  blocking collectives: 61.3 us -> 75.6 us
  Pallas kernels: 10.4 us -> 23.3 us
  waiting for transfers between devices: 12.2 us -> 1.51 us
  starting transfers between devices: 27.3 us -> 16.7 us
  local copies, waits for them, and re-layouts: 3.41 us -> 1.39 us
    all_to_all x4 -> x5, blocking collectives: 61.3 us -> 75.6 us  [swap(): return lax.all_to_all(pieces, axes, 0, 0, tiled=True)]
    pallas_call x7 -> x8, Pallas kernels: 10.4 us -> 23.3 us  [call(): pl.pallas_call(body, out_shape=shapes[0] if single else shapes, in_specs=...]
    ppermute x4, waiting for transfers between devices: 6.11 us -> 0.01 us  [the longest x3 0.01 us: shards(): pieces[k - 1] = lax.ppermute(pieces[k - 1], LAG, [(0, k * nc)])]
    all_to_all x2 -> x1, starting transfers between devices: 13.7 us -> 7.81 us  [swap(): return lax.all_to_all(pieces, axes, 0, 0, tiled=True)]
    ppermute x4, starting transfers between devices: 13.6 us -> 8.9 us  [the longest x1 4.77 us: shards(): before = lax.ppermute(before, LAG, [(i, i + 1) for i in range(nlag - 1)])]
    all_to_all x2 -> x1, waiting for transfers between devices: 6.07 us -> 1.5 us  [swap(): return lax.all_to_all(pieces, axes, 0, 0, tiled=True)]
    unnamed x12 -> x10, local copies, waits for them, and re-layouts: 2.65 us -> 0.67 us
  transfers between devices with their start and end apart: 6 -> 5, of which waited for: 2 -> 1; matrix products, arithmetic and copies ran while one was open for 0% -> 0% of each run, Pallas kernels for 3% -> 4%
where the time goes in v7:
time: 120 us
  blocking collectives  75.6 us (63%)
  Pallas kernels  23.3 us (19%)
  starting transfers between devices  16.7 us (14%)
  waiting for transfers between devices  1.51 us (1%)
  local copies, waits for them, and re-layouts  1.39 us (1%)
    all_to_all x5, blocking collectives, swap(): return lax.all_to_all(pieces, axes, 0, 0, tiled=True)  75.6 us
    pallas_call x8, Pallas kernels, call(): pl.pallas_call(body, out_shape=shapes[0] if single else shapes, in_specs=...  23.3 us
    all_to_all x1, starting transfers between devices, swap(): return lax.all_to_all(pieces, axes, 0, 0, tiled=True)  7.81 us
    ppermute x1, starting transfers between devices, shards(): before = lax.ppermute(before, LAG, [(i, i + 1) for i in range(nlag - 1)])  4.77 us
    ppermute x3, starting transfers between devices, shards(): pieces[k - 1] = lax.ppermute(pieces[k - 1], LAG, [(0, k * nc)])  4.13 us
  transfers between devices with their start and end apart: 5, of which 1 were waited for; matrix products, arithmetic and copies ran while one was open for 0% of the time, Pallas kernels for 4%

profile of v7, /device:TPU:1, one launch (start us, length us, event | category | flops | bytes accessed | tf_op | source)
XLA Modules:
  0.0 119.8 jit_solution(15726606195830080158)
XLA Ops:
  0.0 17.0 %shard_map.47 = bf16[2048,128]{1,0:T(8,128)(2,1)} custom-call(bf16[2,2048,128]{2,1,0:T(8,128)(2,1)} %history.5), custom_call_target="tpu_custom_call" | custom-call | bytes 1572864 | tf_op jit(solution)/shard_map/pallas_call | solution.py:28
  17.0 4.8 %collective-permute-start = (bf16[2048,128]{1,0:T(8,128)(2,1)}, bf16[2048,128]{1,0:T(8,128)(2,1)}, u32[]{:S(2)}, u32[]{:S(2)}) collective-permute-start(bf16[2048,128]{1,0:T(8,128)(2,1)} %shard_map.47), channel_id=1, source_target_pairs={{0,8},{8,16},{16,24},{24,32},{32,40},{40,48},{48,56},{56,64},{64,7... | collective-permute-start | bytes 1572872 | tf_op jit(solution)/shard_map/ppermute | solution.py:211
  21.8 3.6 %shard_map.46 = (f32[8,48,256]{2,1,0:T(8,128)}, f32[128,256]{1,0:T(8,128)}, bf16[64,2048]{1,0:T(8,128)(2,1)}, bf16[64,2048]{1,0:T(8,128)(2,1)}, bf16[64,2048]{1,0:T(8,128)(2,1)}) custom-call(bf16[2,256,2048]{2,1,0:T(8,128)(2,1)} %blocks.5, bf16[2,2048,128]{2,1,0:T(8,128)(2,1)} %history.5, f32[2,256,128]{2,1,0:T(8,128)} %excitation.1, f32[32,256]{1,0:T(8,128)} %inverse.1), custom_call_target="tpu_custom_call" | custom-call | flops 268435456 | bytes 4751360 | tf_op jit(solution)/shard_map/pallas_call | solution.py:28
  25.4 7.8 %all-to-all-start = ((f32[8,48,256]{2,1,0:T(8,128)}), f32[8,48,256]{2,1,0:T(8,128)S(1)}, u32[]{:S(2)}, u32[]{:S(2)}) async-start(f32[8,48,256]{2,1,0:T(8,128)} %get-tuple-element.17), calls=%async_computation | async-start | bytes 786432 | tf_op jit(solution)/shard_map/all_to_all | solution.py:16
  33.2 1.4 %collective-permute-start.1 = (bf16[64,2048]{1,0:T(8,128)(2,1)}, bf16[64,2048]{1,0:T(8,128)(2,1)}, u32[]{:S(2)}, u32[]{:S(2)}) collective-permute-start(bf16[64,2048]{1,0:T(8,128)(2,1)} %get-tuple-element.19), channel_id=1, source_target_pairs={{0,16},{1,17},{2,18},{3,19},{4,20},{5,21},{6,22},{7,23}} | collective-permute-start | bytes 786440 | tf_op jit(solution)/shard_map/ppermute | solution.py:225
  34.6 1.4 %collective-permute-start.2 = (bf16[64,2048]{1,0:T(8,128)(2,1)}, bf16[64,2048]{1,0:T(8,128)(2,1)}, u32[]{:S(2)}, u32[]{:S(2)}) collective-permute-start(bf16[64,2048]{1,0:T(8,128)(2,1)} %get-tuple-element.20), channel_id=1, source_target_pairs={{0,32},{1,33},{2,34},{3,35},{4,36},{5,37},{6,38},{7,39}} | collective-permute-start | bytes 786440 | tf_op jit(solution)/shard_map/ppermute | solution.py:225
  36.0 1.4 %collective-permute-start.3 = (bf16[64,2048]{1,0:T(8,128)(2,1)}, bf16[64,2048]{1,0:T(8,128)(2,1)}, u32[]{:S(2)}, u32[]{:S(2)}) collective-permute-start(bf16[64,2048]{1,0:T(8,128)(2,1)} %get-tuple-element.21), channel_id=1, source_target_pairs={{0,48},{1,49},{2,50},{3,51},{4,52},{5,53},{6,54},{7,55}} | collective-permute-start | bytes 786440 | tf_op jit(solution)/shard_map/ppermute | solution.py:225
  37.4 1.8 %shard_map.48.later = f32[128,256]{1,0:T(8,128)S(1)} custom-call(bf16[2,256,2048]{2,1,0:T(8,128)(2,1)S(1)} %copy-done, bf16[2048,128]{1,0:T(8,128)(2,1)} %collective-permute-done.before, bf16[2,2048,128]{2,1,0:T(8,128)(2,1)S(1)} %copy-done.1), custom_call_target="tpu_custom_call" | custom-call | flops 268435456 | bytes 3801088 | tf_op jit(solution)/shard_map/pallas_call | solution.py:28
  39.2 0.6 copy-done.2
  39.8 1.5 %all-to-all-done.got.got1 = f32[8,48,256]{2,1,0:T(8,128)S(1)} async-done(((f32[8,48,256]{2,1,0:T(8,128)}), f32[8,48,256]{2,1,0:T(8,128)S(1)}, u32[]{:S(2)}, u32[]{:S(2)}) %all-to-all-start) | async-done | bytes 393248 | tf_op jit(solution)/shard_map/all_to_all | solution.py:16
  41.4 13.8 %all_to_all.34.got.got2 = bf16[8,96,256]{2,1,0:T(8,128)(2,1)S(1)} all-to-all(bf16[8,96,256]{2,1,0:T(8,128)(2,1)S(1)} %shard_map.49), channel_id=1, replica_groups=mesh['y'=8,'x'=4,'core'=2,'row'=8] {'y'}, dimensions={0} | all-to-all | bytes 786432 | tf_op jit(solution)/shard_map/all_to_all | solution.py:16
  55.3 19.1 %all_to_all.35.got3 = bf16[8,96,256]{2,1,0:T(8,128)(2,1)S(1)} all-to-all(bf16[8,96,256]{2,1,0:T(8,128)(2,1)S(1)} %shard_map.50), channel_id=1, replica_groups=mesh['y'=8,'x'=4,'core'=2,'row'=8] {'x','core'}, dimensions={0} | all-to-all | bytes 786432 | tf_op jit(solution)/shard_map/all_to_all | solution.py:16
  74.4 0.3 shard_map.51
  74.7 15.2 %all_to_all.36.got = f32[8,16,256]{2,1,0:T(8,128)S(1)} all-to-all(f32[8,16,256]{2,1,0:T(8,128)S(1)} %get-tuple-element.24), channel_id=1, replica_groups=mesh['y'=8,'x'=4,'core'=2,'row'=8] {'row'}, dimensions={0} | all-to-all | bytes 262144 | tf_op jit(solution)/shard_map/all_to_all | solution.py:16
  89.9 0.2 shard_map.52
  90.1 10.4 %all_to_all.37.got = f32[8,16,256]{2,1,0:T(8,128)S(1)} all-to-all(f32[8,16,256]{2,1,0:T(8,128)S(1)} %get-tuple-element.27), channel_id=1, replica_groups=mesh['y'=8,'x'=4,'core'=2,'row'=8] {'y'}, dimensions={0} | all-to-all | bytes 262144 | tf_op jit(solution)/shard_map/all_to_all | solution.py:16
  100.5 0.3 shard_map.53
  100.8 0.1 reshape.19
  100.9 0.1 broadcast_in_dim.7
  101.1 0.2 all_to_all.26
  101.2 17.1 %all_to_all.38 = f32[64,1,576]{2,1,0:T(1,128)S(1)} all-to-all(f32[64,1,576]{2,1,0:T(1,128)S(1)} %all_to_all.26), channel_id=1, replica_groups=mesh['y'=8,'x'=4,'core'=2,'row'=8] {'x','core','row'}, dimensions={0} | all-to-all | bytes 294912 | tf_op jit(solution)/shard_map/all_to_all | solution.py:16
  118.3 0.4 reduce
  118.7 0.2 reshape.20
  119.1 0.6 pad_maximum_fusion
  (21 shorter events, 0.4 us)
Async XLA Ops:
  17.0 20.4 %copy-start = (bf16[2,256,2048]{2,1,0:T(8,128)(2,1)S(1)}, bf16[2,256,2048]{2,1,0:T(8,128)(2,1)}, u32[]{:S(2)}) copy-start(bf16[2,256,2048]{2,1,0:T(8,128)(2,1)} %blocks.5) | copy-start | bytes 6291460
  17.0 20.3 %copy-start.1 = (bf16[2,2048,128]{2,1,0:T(8,128)(2,1)S(1)}, bf16[2,2048,128]{2,1,0:T(8,128)(2,1)}, u32[]{:S(2)}) copy-start(bf16[2,2048,128]{2,1,0:T(8,128)(2,1)} %history.5) | copy-start | bytes 3145732
  17.0 20.3 %collective-permute-start = (bf16[2048,128]{1,0:T(8,128)(2,1)}, bf16[2048,128]{1,0:T(8,128)(2,1)}, u32[]{:S(2)}, u32[]{:S(2)}) collective-permute-start(bf16[2048,128]{1,0:T(8,128)(2,1)} %shard_map.47), channel_id=1, source_target_pairs={{0,8},{8,16},{16,24},{24,32},{32,40},{40,48},{48,56},{56,64},{64,7... | collective-permute-start | bytes 1572872 | tf_op jit(solution)/shard_map/ppermute | solution.py:211
  25.4 15.9 %all-to-all-start = ((f32[8,48,256]{2,1,0:T(8,128)}), f32[8,48,256]{2,1,0:T(8,128)S(1)}, u32[]{:S(2)}, u32[]{:S(2)}) async-start(f32[8,48,256]{2,1,0:T(8,128)} %get-tuple-element.17), calls=%async_computation | async-start | bytes 786432 | tf_op jit(solution)/shard_map/all_to_all | solution.py:16
  33.2 8.1 %collective-permute-start.1 = (bf16[64,2048]{1,0:T(8,128)(2,1)}, bf16[64,2048]{1,0:T(8,128)(2,1)}, u32[]{:S(2)}, u32[]{:S(2)}) collective-permute-start(bf16[64,2048]{1,0:T(8,128)(2,1)} %get-tuple-element.19), channel_id=1, source_target_pairs={{0,16},{1,17},{2,18},{3,19},{4,20},{5,21},{6,22},{7,23}} | collective-permute-start | bytes 786440 | tf_op jit(solution)/shard_map/ppermute | solution.py:225
  34.6 6.7 %collective-permute-start.2 = (bf16[64,2048]{1,0:T(8,128)(2,1)}, bf16[64,2048]{1,0:T(8,128)(2,1)}, u32[]{:S(2)}, u32[]{:S(2)}) collective-permute-start(bf16[64,2048]{1,0:T(8,128)(2,1)} %get-tuple-element.20), channel_id=1, source_target_pairs={{0,32},{1,33},{2,34},{3,35},{4,36},{5,37},{6,38},{7,39}} | collective-permute-start | bytes 786440 | tf_op jit(solution)/shard_map/ppermute | solution.py:225
  36.0 5.4 %collective-permute-start.3 = (bf16[64,2048]{1,0:T(8,128)(2,1)}, bf16[64,2048]{1,0:T(8,128)(2,1)}, u32[]{:S(2)}, u32[]{:S(2)}) collective-permute-start(bf16[64,2048]{1,0:T(8,128)(2,1)} %get-tuple-element.21), channel_id=1, source_target_pairs={{0,48},{1,49},{2,50},{3,51},{4,52},{5,53},{6,54},{7,55}} | collective-permute-start | bytes 786440 | tf_op jit(solution)/shard_map/ppermute | solution.py:225
  39.2 0.7 copy-start.2
  39.8 15.4 %copy-start.4 = (f32[128,256]{1,0:T(8,128)S(1)}, f32[128,256]{1,0:T(8,128)}, u32[]{:S(2)}) copy-start(f32[128,256]{1,0:T(8,128)} %get-tuple-element.23.lead) | copy-start | bytes 393220
  41.3 13.9 %copy-start.3 = (f32[128,256]{1,0:T(8,128)S(1)}, f32[128,256]{1,0:T(8,128)}, u32[]{:S(2)}) copy-start(f32[128,256]{1,0:T(8,128)} %copy-done.2) | copy-start | bytes 393220

commit v8 on v7

--- a/solution.py
+++ b/solution.py
@@ -8,6 +8,7 @@
 
 LAG = ("y", "x", "core")
 W = ("x", "core")
+ORDER = (2, 3, 1)
 F32 = jnp.float32
 BF16 = jnp.bfloat16
 
@@ -126,7 +127,7 @@
 def second_step(got, blocks, *rest):
     sources, (out, piece, sem) = rest[:-3], rest[-3:]
     sources = (blocks.at[0, : piece.shape[0]], *sources)
-    for k, source in enumerate(sources):
+    for k, source in zip((0,) + ORDER, sources):
 
         @pl.when(lax.axis_index("x") == k)
         def _():
@@ -205,7 +206,6 @@
         history,
         scratch=[pltpu.SemaphoreType.DMA((4,))],
         held=[pltpu.HBM],
-        given=[pltpu.HBM],
         limit=60,
     )
     before = lax.ppermute(before, LAG, [(i, i + 1) for i in range(nlag - 1)])
@@ -221,8 +221,7 @@
         first_sums, outs, work, *args, scratch=scratch, held=held, given=given, limit=60
     )
     got1 = swap(send, W)
-    for k in range(1, nx):
-        pieces[k - 1] = lax.ppermute(pieces[k - 1], LAG, [(0, k * nc)])
+    pieces = [lax.ppermute(pieces[k - 1], LAG, [(0, k * nc), (1, 0)]) for k in ORDER]
     got1, later = lax.optimization_barrier((got1, later))
     send = call(
         second_step,

time: 120 us -> 105 us (0.88)
  Pallas kernels: 23.3 us -> 8.23 us
  starting transfers between devices: 16.7 us -> 22.7 us
  blocking collectives: 75.6 us -> 71.1 us
  waiting for transfers between devices: 1.51 us -> 0.01 us
    pallas_call x8, Pallas kernels: 23.3 us -> 8.23 us  [call(): pl.pallas_call(body, out_shape=shapes[0] if single else shapes, in_specs=...]
    ppermute x3, starting transfers between devices: 4.13 us -> 10.1 us  [shards(): lax.ppermute(pieces[k - 1], LAG, [(0, k * nc), (1, 0)])]
    all_to_all x5, blocking collectives: 75.6 us -> 71.1 us  [swap(): return lax.all_to_all(pieces, axes, 0, 0, tiled=True)]
    all_to_all x1, waiting for transfers between devices: 1.5 us -> 0.01 us  [swap(): return lax.all_to_all(pieces, axes, 0, 0, tiled=True)]
  transfers between devices with their start and end apart: 5 -> 5, of which waited for: 1 -> 0; matrix products, arithmetic and copies ran while one was open for 0% -> 0% of each run, Pallas kernels for 4% -> 5%
where the time goes in v8:
time: 105 us
  blocking collectives  71.1 us (68%)
  starting transfers between devices  22.7 us (22%)
  Pallas kernels  8.23 us (8%)
  local copies, waits for them, and re-layouts  1.39 us (1%)
  other arithmetic  1.07 us (1%)
    all_to_all x5, blocking collectives, swap(): return lax.all_to_all(pieces, axes, 0, 0, tiled=True)  71.1 us
    ppermute x3, starting transfers between devices, shards(): lax.ppermute(pieces[k - 1], LAG, [(0, k * nc), (1, 0)])  10.1 us
    pallas_call x8, Pallas kernels, call(): pl.pallas_call(body, out_shape=shapes[0] if single else shapes, in_specs=...  8.23 us
    all_to_all x1, starting transfers between devices, swap(): return lax.all_to_all(pieces, axes, 0, 0, tiled=True)  7.82 us
    ppermute x1, starting transfers between devices, shards(): before = lax.ppermute(before, LAG, [(i, i + 1) for i in range(nlag - 1)])  4.77 us
  transfers between devices with their start and end apart: 5, of which 0 were waited for; matrix products, arithmetic and copies ran while one was open for 0% of the time, Pallas kernels for 5%

profile of v8, /device:TPU:1, one launch (start us, length us, event | category | flops | bytes accessed | tf_op | source)
XLA Modules:
  0.0 104.7 jit_solution(2508793542278347584)
XLA Ops:
  0.0 1.9 %shard_map.47 = bf16[2048,128]{1,0:T(8,128)(2,1)} custom-call(bf16[2,2048,128]{2,1,0:T(8,128)(2,1)} %history.5), custom_call_target="tpu_custom_call" | custom-call | bytes 1572864 | tf_op jit(solution)/shard_map/pallas_call | solution.py:29
  2.0 4.8 %collective-permute-start = (bf16[2048,128]{1,0:T(8,128)(2,1)}, bf16[2048,128]{1,0:T(8,128)(2,1)}, u32[]{:S(2)}, u32[]{:S(2)}) collective-permute-start(bf16[2048,128]{1,0:T(8,128)(2,1)} %shard_map.47), channel_id=1, source_target_pairs={{0,8},{8,16},{16,24},{24,32},{32,40},{40,48},{48,56},{56,64},{64,7... | collective-permute-start | bytes 1572872 | tf_op jit(solution)/shard_map/ppermute | solution.py:211
  6.7 3.6 %shard_map.46 = (f32[8,48,256]{2,1,0:T(8,128)}, f32[128,256]{1,0:T(8,128)}, bf16[64,2048]{1,0:T(8,128)(2,1)}, bf16[64,2048]{1,0:T(8,128)(2,1)}, bf16[64,2048]{1,0:T(8,128)(2,1)}) custom-call(bf16[2,256,2048]{2,1,0:T(8,128)(2,1)} %blocks.5, bf16[2,2048,128]{2,1,0:T(8,128)(2,1)} %history.5, f32[2,256,128]{2,1,0:T(8,128)} %excitation.1, f32[32,256]{1,0:T(8,128)} %inverse.1), custom_call_target="tpu_custom_call" | custom-call | flops 268435456 | bytes 4751360 | tf_op jit(solution)/shard_map/pallas_call | solution.py:29
  10.3 7.8 %all-to-all-start = ((f32[8,48,256]{2,1,0:T(8,128)}), f32[8,48,256]{2,1,0:T(8,128)S(1)}, u32[]{:S(2)}, u32[]{:S(2)}) async-start(f32[8,48,256]{2,1,0:T(8,128)} %get-tuple-element.17), calls=%async_computation | async-start | bytes 786432 | tf_op jit(solution)/shard_map/all_to_all | solution.py:17
  18.2 2.7 %collective-permute-start.1 = (bf16[64,2048]{1,0:T(8,128)(2,1)}, bf16[64,2048]{1,0:T(8,128)(2,1)}, u32[]{:S(2)}, u32[]{:S(2)}) collective-permute-start(bf16[64,2048]{1,0:T(8,128)(2,1)} %get-tuple-element.19), channel_id=1, source_target_pairs={{0,32},{8,0},{1,33},{9,1},{2,34},{10,2},{3,35},{11,3},{4,36},{12,4... | collective-permute-start | bytes 786440 | tf_op jit(solution)/shard_map/ppermute | solution.py:224
  20.9 5.3 %collective-permute-start.2 = (bf16[64,2048]{1,0:T(8,128)(2,1)}, bf16[64,2048]{1,0:T(8,128)(2,1)}, u32[]{:S(2)}, u32[]{:S(2)}) collective-permute-start(bf16[64,2048]{1,0:T(8,128)(2,1)} %get-tuple-element.20), channel_id=1, source_target_pairs={{0,48},{8,0},{1,49},{9,1},{2,50},{10,2},{3,51},{11,3},{4,52},{12,4... | collective-permute-start | bytes 786440 | tf_op jit(solution)/shard_map/ppermute | solution.py:224
  26.2 2.0 %collective-permute-start.3 = (bf16[64,2048]{1,0:T(8,128)(2,1)}, bf16[64,2048]{1,0:T(8,128)(2,1)}, u32[]{:S(2)}, u32[]{:S(2)}) collective-permute-start(bf16[64,2048]{1,0:T(8,128)(2,1)} %get-tuple-element.21), channel_id=1, source_target_pairs={{0,16},{8,0},{1,17},{9,1},{2,18},{10,2},{3,19},{11,3},{4,20},{12,4... | collective-permute-start | bytes 786440 | tf_op jit(solution)/shard_map/ppermute | solution.py:224
  28.3 1.8 %shard_map.48.later = f32[128,256]{1,0:T(8,128)S(1)} custom-call(bf16[2,256,2048]{2,1,0:T(8,128)(2,1)S(1)} %copy-done, bf16[2048,128]{1,0:T(8,128)(2,1)} %collective-permute-done.before, bf16[2,2048,128]{2,1,0:T(8,128)(2,1)S(1)} %copy-done.1), custom_call_target="tpu_custom_call" | custom-call | flops 268435456 | bytes 3801088 | tf_op jit(solution)/shard_map/pallas_call | solution.py:29
  30.1 0.6 copy-done.2
  30.8 0.1 shard_map.49
  30.8 16.0 %all_to_all.34.got.got2 = bf16[8,96,256]{2,1,0:T(8,128)(2,1)S(1)} all-to-all(bf16[8,96,256]{2,1,0:T(8,128)(2,1)S(1)} %shard_map.49), channel_id=1, replica_groups=mesh['y'=8,'x'=4,'core'=2,'row'=8] {'y'}, dimensions={0} | all-to-all | bytes 786432 | tf_op jit(solution)/shard_map/all_to_all | solution.py:17
  46.9 12.5 %all_to_all.35.got3 = bf16[8,96,256]{2,1,0:T(8,128)(2,1)S(1)} all-to-all(bf16[8,96,256]{2,1,0:T(8,128)(2,1)S(1)} %shard_map.50), channel_id=1, replica_groups=mesh['y'=8,'x'=4,'core'=2,'row'=8] {'x','core'}, dimensions={0} | all-to-all | bytes 786432 | tf_op jit(solution)/shard_map/all_to_all | solution.py:17
  59.4 0.3 shard_map.51
  59.7 15.1 %all_to_all.36.got = f32[8,16,256]{2,1,0:T(8,128)S(1)} all-to-all(f32[8,16,256]{2,1,0:T(8,128)S(1)} %get-tuple-element.24), channel_id=1, replica_groups=mesh['y'=8,'x'=4,'core'=2,'row'=8] {'row'}, dimensions={0} | all-to-all | bytes 262144 | tf_op jit(solution)/shard_map/all_to_all | solution.py:17
  74.8 0.2 shard_map.52
  75.0 10.4 %all_to_all.37.got = f32[8,16,256]{2,1,0:T(8,128)S(1)} all-to-all(f32[8,16,256]{2,1,0:T(8,128)S(1)} %get-tuple-element.27), channel_id=1, replica_groups=mesh['y'=8,'x'=4,'core'=2,'row'=8] {'y'}, dimensions={0} | all-to-all | bytes 262144 | tf_op jit(solution)/shard_map/all_to_all | solution.py:17
  85.4 0.3 shard_map.53
  85.7 0.1 reshape.19
  85.9 0.1 broadcast_in_dim.7
  86.0 0.2 all_to_all.26
  86.1 17.1 %all_to_all.38 = f32[64,1,576]{2,1,0:T(1,128)S(1)} all-to-all(f32[64,1,576]{2,1,0:T(1,128)S(1)} %all_to_all.26), channel_id=1, replica_groups=mesh['y'=8,'x'=4,'core'=2,'row'=8] {'x','core','row'}, dimensions={0} | all-to-all | bytes 294912 | tf_op jit(solution)/shard_map/all_to_all | solution.py:17
  103.3 0.4 reduce
  103.6 0.2 reshape.20
  104.1 0.6 pad_maximum_fusion
  (21 shorter events, 0.3 us)
Async XLA Ops:
  1.9 26.3 %copy-start = (bf16[2,256,2048]{2,1,0:T(8,128)(2,1)S(1)}, bf16[2,256,2048]{2,1,0:T(8,128)(2,1)}, u32[]{:S(2)}) copy-start(bf16[2,256,2048]{2,1,0:T(8,128)(2,1)} %blocks.5) | copy-start | bytes 6291460
  1.9 26.3 %copy-start.1 = (bf16[2,2048,128]{2,1,0:T(8,128)(2,1)S(1)}, bf16[2,2048,128]{2,1,0:T(8,128)(2,1)}, u32[]{:S(2)}) copy-start(bf16[2,2048,128]{2,1,0:T(8,128)(2,1)} %history.5) | copy-start | bytes 3145732
  2.0 26.3 %collective-permute-start = (bf16[2048,128]{1,0:T(8,128)(2,1)}, bf16[2048,128]{1,0:T(8,128)(2,1)}, u32[]{:S(2)}, u32[]{:S(2)}) collective-permute-start(bf16[2048,128]{1,0:T(8,128)(2,1)} %shard_map.47), channel_id=1, source_target_pairs={{0,8},{8,16},{16,24},{24,32},{32,40},{40,48},{48,56},{56,64},{64,7... | collective-permute-start | bytes 1572872 | tf_op jit(solution)/shard_map/ppermute | solution.py:211
  10.3 20.4 %all-to-all-start = ((f32[8,48,256]{2,1,0:T(8,128)}), f32[8,48,256]{2,1,0:T(8,128)S(1)}, u32[]{:S(2)}, u32[]{:S(2)}) async-start(f32[8,48,256]{2,1,0:T(8,128)} %get-tuple-element.17), calls=%async_computation | async-start | bytes 786432 | tf_op jit(solution)/shard_map/all_to_all | solution.py:17
  18.2 12.6 %collective-permute-start.1 = (bf16[64,2048]{1,0:T(8,128)(2,1)}, bf16[64,2048]{1,0:T(8,128)(2,1)}, u32[]{:S(2)}, u32[]{:S(2)}) collective-permute-start(bf16[64,2048]{1,0:T(8,128)(2,1)} %get-tuple-element.19), channel_id=1, source_target_pairs={{0,32},{8,0},{1,33},{9,1},{2,34},{10,2},{3,35},{11,3},{4,36},{12,4... | collective-permute-start | bytes 786440 | tf_op jit(solution)/shard_map/ppermute | solution.py:224
  20.9 9.8 %collective-permute-start.2 = (bf16[64,2048]{1,0:T(8,128)(2,1)}, bf16[64,2048]{1,0:T(8,128)(2,1)}, u32[]{:S(2)}, u32[]{:S(2)}) collective-permute-start(bf16[64,2048]{1,0:T(8,128)(2,1)} %get-tuple-element.20), channel_id=1, source_target_pairs={{0,48},{8,0},{1,49},{9,1},{2,50},{10,2},{3,51},{11,3},{4,52},{12,4... | collective-permute-start | bytes 786440 | tf_op jit(solution)/shard_map/ppermute | solution.py:224
  26.2 4.5 %collective-permute-start.3 = (bf16[64,2048]{1,0:T(8,128)(2,1)}, bf16[64,2048]{1,0:T(8,128)(2,1)}, u32[]{:S(2)}, u32[]{:S(2)}) collective-permute-start(bf16[64,2048]{1,0:T(8,128)(2,1)} %get-tuple-element.21), channel_id=1, source_target_pairs={{0,16},{8,0},{1,17},{9,1},{2,18},{10,2},{3,19},{11,3},{4,20},{12,4... | collective-permute-start | bytes 786440 | tf_op jit(solution)/shard_map/ppermute | solution.py:224
  30.1 0.7 copy-start.2
  30.7 16.1 %copy-start.4 = (f32[128,256]{1,0:T(8,128)S(1)}, f32[128,256]{1,0:T(8,128)}, u32[]{:S(2)}) copy-start(f32[128,256]{1,0:T(8,128)} %get-tuple-element.23.lead) | copy-start | bytes 393220
  30.7 16.1 %copy-start.3 = (f32[128,256]{1,0:T(8,128)S(1)}, f32[128,256]{1,0:T(8,128)}, u32[]{:S(2)}) copy-start(f32[128,256]{1,0:T(8,128)} %copy-done.2) | copy-start | bytes 393220

commit v9 on v8

--- a/solution.py
+++ b/solution.py
@@ -67,20 +67,28 @@
     return jnp.where(lax.axis_index(LAG) == 0, total - field, total).T
 
 
-def last_of(history, out, sems):
-    count = sems.shape[0]
-    step = out.shape[0] // count
-    loads = []
-    for i in range(count):
-        rows = pl.ds(i * step, step)
-        loads.append(pltpu.make_async_copy(history.at[1, rows], out.at[rows], sems.at[i]))
-        loads[-1].start()
-    for load in loads:
+def own_copies(history, blocks, out_h, out_b, held_h, held_b, sems):
+    moves = []
+    for j, (source, held, out) in enumerate(
+        ((blocks.at[0, out_b.shape[0] :], held_b, out_b), (history.at[1], held_h, out_h))
+    ):
+        count = sems.shape[2]
+        step = out.shape[0] // count
+        for i in range(count):
+            rows = pl.ds(i * step, step)
+            load = pltpu.make_async_copy(source.at[rows], held.at[rows], sems.at[0, j, i])
+            store = pltpu.make_async_copy(held.at[rows], out.at[rows], sems.at[1, j, i])
+            moves.append((load, store))
+            load.start()
+    for load, store in moves:
         load.wait()
-
-
-def first_sums(blocks, history, excitation, inverse, out, lead, *rest):
-    pieces, (b, h, e, own, o, f, sems) = rest[:-7], rest[-7:]
+        store.start()
+    for _, store in moves:
+        store.wait()
+
+
+def first_sums(blocks, history, excitation, inverse, half, out, lead, *rest):
+    pieces, (b, h, e, own, o, f, g, sems) = rest[:-8], rest[-8:]
     cut = pieces[0].shape[0]
     loads = [
         pltpu.make_async_copy(history.at[0], h.at[0], sems.at[0]),
@@ -89,6 +97,7 @@
         pltpu.make_async_copy(blocks.at[1], b.at[1], sems.at[3]),
         pltpu.make_async_copy(inverse, own, sems.at[4]),
         pltpu.make_async_copy(excitation, e, sems.at[5]),
+        pltpu.make_async_copy(half, g, sems.at[6]),
     ]
     for load in loads:
         load.start()
@@ -96,12 +105,16 @@
     cw = depth - own.shape[0]
     loads[0].wait()
     loads[1].wait()
-    stores = []
-    for k, piece in enumerate(pieces):
-        rows = b.at[0, (k + 1) * cut : (k + 2) * cut]
-        stores.append(pltpu.make_async_copy(rows, piece, sems.at[8 + k]))
-        stores[-1].start()
     total = mm(b[0], h[0])
+    loads[6].wait()
+    for core, source in enumerate((b.at[0, : g.shape[0]], g)):
+
+        @pl.when(lax.axis_index("core") == core)
+        def _():
+            for k, piece in enumerate(pieces):
+                rows = source.at[k * cut : (k + 1) * cut]
+                pltpu.make_async_copy(rows, piece, sems.at[9 + k]).start()
+
     loads[2].wait()
     loads[3].wait()
     total = total + mm(b[1], h[1])
@@ -111,22 +124,24 @@
     for w in range(nw):
         o[w, :cw] = total[w * cw : (w + 1) * cw]
         o[w, cw:] = own[...]
-    stores.append(pltpu.make_async_copy(o, out, sems.at[6]))
+    stores = [pltpu.make_async_copy(o, out, sems.at[7])]
     stores[-1].start()
     f[...] = less_field(jnp.zeros_like(e[1]), e[1])
-    stores.append(pltpu.make_async_copy(f, lead, sems.at[7]))
+    stores.append(pltpu.make_async_copy(f, lead, sems.at[8]))
     stores[-1].start()
+    for k, piece in enumerate(pieces):
+        rows = g.at[k * cut : (k + 1) * cut]
+        stores.append(pltpu.make_async_copy(rows, piece, sems.at[9 + k]))
     for store in stores:
         store.wait()
 
 
-def later_sums(blocks, before, history, out):
-    out[...] = (mm(blocks[1], history[0]) + mm(blocks[0], before[...])).T
-
-
-def second_step(got, blocks, *rest):
+def later_sums(blocks, before, history, lead, out):
+    out[...] = (mm(blocks[1], history[0]) + mm(blocks[0], before[...])).T + lead[...]
+
+
+def second_step(got, *rest):
     sources, (out, piece, sem) = rest[:-3], rest[-3:]
-    sources = (blocks.at[0, : piece.shape[0]], *sources)
     for k, source in zip((0,) + ORDER, sources):
 
         @pl.when(lax.axis_index("x") == k)
@@ -144,12 +159,11 @@
         out[y, 2 * cw :] = piece[:, y * span : (y + 1) * span]
 
 
-def third_step(got, later, lead, out):
+def third_step(got, later, out):
     nw = out.shape[0]
     cw = later.shape[0] // nw
-    total = later[...] + lead[...]
     for w in range(nw):
-        high, low = parts(total[w * cw : (w + 1) * cw])
+        high, low = parts(later[w * cw : (w + 1) * cw])
         out[w, :cw] = high
         out[w, cw : 2 * cw] = low
         out[w, 2 * cw :] = got[0, 2 * cw :]
@@ -162,9 +176,12 @@
     for z in range(nz):
         out[z] = term
     part1[...] = sum_pairs(got3, 0, cw)
-    cut = got3.shape[1] - 2 * cw
-    for x in range(first.shape[0] // cut):
-        first[x * cut : (x + 1) * cut] = got3[2 * x, 2 * cw :]
+    nw, depth, _ = got3.shape
+    cut = depth - 2 * cw
+    for x in range(nw // 2):
+        for core in range(2):
+            start = (core * nw // 2 + x) * cut
+            first[start : start + cut] = got3[2 * x + core, 2 * cw :]
 
 
 def fifth_step(got, part1, first, out, mine):
@@ -194,47 +211,57 @@
     cw = columns // nw
     own = self_inverse.shape[0]
     nlag = ny * nw
-    cut = rows // nx
+    cut = rows // nw
     span = nw * own
     work = 2 * rows * size * columns * 2
     small = 2 * cw * rows * span
 
-    before = call(
-        last_of,
-        (history.shape[1:], BF16),
+    part = (rows // nc, size)
+    before, half = call(
+        own_copies,
+        [(history.shape[1:], BF16), (part, BF16)],
         0,
         history,
-        scratch=[pltpu.SemaphoreType.DMA((4,))],
-        held=[pltpu.HBM],
+        blocks,
+        scratch=[
+            pltpu.VMEM(history.shape[1:], BF16),
+            pltpu.VMEM(part, BF16),
+            pltpu.SemaphoreType.DMA((2, 2, 4)),
+        ],
+        held=[pltpu.HBM] * 2,
+        given=[pltpu.HBM] * 2,
         limit=60,
     )
+    half = lax.ppermute(half, LAG, [(i, i ^ 1) for i in range(nlag)])
     before = lax.ppermute(before, LAG, [(i, i + 1) for i in range(nlag - 1)])
-    later = call(later_sums, ((columns, rows), F32), work, blocks, before, history)
-
-    outs = [((nw, cw + own, rows), F32), ((columns, rows), F32)] + [((cut, size), BF16)] * (nx - 1)
+
+    outs = [((nw, cw + own, rows), F32), ((columns, rows), F32)] + [((cut, size), BF16)] * nx
     scratch = [pltpu.VMEM(blocks.shape, BF16), pltpu.VMEM(history.shape, BF16)]
     scratch += [pltpu.VMEM(excitation.shape, F32), pltpu.VMEM((own, rows), F32)]
-    scratch += [pltpu.VMEM(*o) for o in outs[:2]] + [pltpu.SemaphoreType.DMA((8 + nx,))]
-    args = blocks, history, excitation, self_inverse
+    scratch += [pltpu.VMEM(*o) for o in outs[:2]] + [pltpu.VMEM(part, BF16)]
+    scratch += [pltpu.SemaphoreType.DMA((9 + nx,))]
+    args = blocks, history, excitation, self_inverse, half
     held, given = [pltpu.HBM] * len(args), [pltpu.HBM] * len(outs)
     send, lead, *pieces = call(
         first_sums, outs, work, *args, scratch=scratch, held=held, given=given, limit=60
     )
     got1 = swap(send, W)
-    pieces = [lax.ppermute(pieces[k - 1], LAG, [(0, k * nc), (1, 0)]) for k in ORDER]
+    routes = {k: [(c, k * nc + c) for c in range(nc)] for k in ORDER}
+    sent = [lax.ppermute(pieces[k], LAG, routes[k]) for k in ORDER]
+    later = call(later_sums, ((columns, rows), F32), work, blocks, before, history, lead)
     got1, later = lax.optimization_barrier((got1, later))
     send = call(
         second_step,
         ((ny, 2 * cw + cut, span), BF16),
         small,
         got1,
-        blocks,
-        *pieces,
+        pieces[0],
+        *sent,
         scratch=[pltpu.VMEM((cut, size), BF16), pltpu.SemaphoreType.DMA(())],
         held=[pltpu.VMEM] + [pltpu.HBM] * nx,
     )
     got2 = swap(send, "y")
-    send = call(third_step, ((nw, 2 * cw + cut, rows), BF16), small, got2, later, lead)
+    send = call(third_step, ((nw, 2 * cw + cut, rows), BF16), small, got2, later)
     got3 = swap(send, W)
     outs = [((nz, cw, rows), F32), ((cw, rows), F32), ((rows, span), BF16)]
     send, part1, first = call(fourth_step, outs, small, got1, got2, got3)

time: 105 us -> 107 us (1.019)
  blocking collectives: 71.1 us -> 66.1 us
  local copies, waits for them, and re-layouts: 1.39 us -> 4.9 us
  starting transfers between devices: 22.7 us -> 25 us
    ppermute x3 -> x4, starting transfers between devices: 10.1 us -> 18.1 us  [the longest x3 9.32 us: shards(): sent = [lax.ppermute(pieces[k], LAG, routes[k]) for k in ORDER]]
    all_to_all x5, blocking collectives: 71.1 us -> 66.1 us  [swap(): return lax.all_to_all(pieces, axes, 0, 0, tiled=True)]
    unnamed x10 -> x14, local copies, waits for them, and re-layouts: 0.67 us -> 4.17 us
    all_to_all x1, starting transfers between devices: 7.82 us -> 4.65 us  [swap(): return lax.all_to_all(pieces, axes, 0, 0, tiled=True)]
    ppermute x1, starting transfers between devices: 4.77 us -> 2.18 us  [shards(): before = lax.ppermute(before, LAG, [(i, i + 1) for i in range(nlag - 1)])]
  transfers between devices with their start and end apart: 5 -> 6, of which waited for: 0 -> 0; matrix products, arithmetic and copies ran while one was open for 0% -> 0% of each run, Pallas kernels for 5% -> 5%
where the time goes in v9:
time: 107 us; the launch traced here: 106 us
  blocking collectives  66.1 us (62%)
  starting transfers between devices  25 us (23%)
  Pallas kernels  8.7 us (8%)
  local copies, waits for them, and re-layouts  4.9 us (5%)
  other arithmetic  1.07 us (1%)
    all_to_all x5, blocking collectives, swap(): return lax.all_to_all(pieces, axes, 0, 0, tiled=True)  66.1 us
    ppermute x3, starting transfers between devices, shards(): sent = [lax.ppermute(pieces[k], LAG, routes[k]) for k in ORDER]  9.32 us
    ppermute x1, starting transfers between devices, shards(): half = lax.ppermute(half, LAG, [(i, i ^ 1) for i in range(nlag)])  8.79 us
    pallas_call x8, Pallas kernels, call(): pl.pallas_call(body, out_shape=shapes[0] if single else shapes, in_specs=...  8.7 us
    all_to_all x1, starting transfers between devices, swap(): return lax.all_to_all(pieces, axes, 0, 0, tiled=True)  4.65 us
    unnamed x14, local copies, waits for them, and re-layouts  4.17 us
    ppermute x1, starting transfers between devices, shards(): before = lax.ppermute(before, LAG, [(i, i + 1) for i in range(nlag - 1)])  2.18 us
  transfers between devices with their start and end apart: 6, of which 0 were waited for; matrix products, arithmetic and copies ran while one was open for 0% of the time, Pallas kernels for 5%

profile of v9, /device:TPU:1, one launch (start us, length us, event | category | flops | bytes accessed | tf_op | source)
XLA Modules:
  0.0 105.9 jit_solution(11167869312961714787)
XLA Ops:
  0.0 2.1 %shard_map.46 = (bf16[2048,128]{1,0:T(8,128)(2,1)}, bf16[128,2048]{1,0:T(8,128)(2,1)}) custom-call(bf16[2,2048,128]{2,1,0:T(8,128)(2,1)} %history.5, bf16[2,256,2048]{2,1,0:T(8,128)(2,1)} %blocks.5), custom_call_target="tpu_custom_call" | custom-call | bytes 4194304 | tf_op jit(solution)/shard_map/pallas_call | solution.py:29
  2.1 8.8 %collective-permute-start = (bf16[128,2048]{1,0:T(8,128)(2,1)}, bf16[128,2048]{1,0:T(8,128)(2,1)S(1)}, u32[]{:S(2)}, u32[]{:S(2)}) collective-permute-start(bf16[128,2048]{1,0:T(8,128)(2,1)} %get-tuple-element.20), channel_id=1, source_target_pairs={{0,8},{8,0},{16,24},{24,16},{32,40},{40,32},{48,56},{56,48},{64,72... | collective-permute-start | bytes 1572872 | tf_op jit(solution)/shard_map/ppermute | solution.py:235
  10.9 2.2 %collective-permute-start.1 = (bf16[2048,128]{1,0:T(8,128)(2,1)}, bf16[2048,128]{1,0:T(8,128)(2,1)}, u32[]{:S(2)}, u32[]{:S(2)}) collective-permute-start(bf16[2048,128]{1,0:T(8,128)(2,1)} %get-tuple-element.22), channel_id=1, source_target_pairs={{0,8},{8,16},{16,24},{24,32},{32,40},{40,48},{48,56},{56,64},{64,7... | collective-permute-start | bytes 1572872 | tf_op jit(solution)/shard_map/ppermute | solution.py:236
  13.1 0.8 copy-done.6
  13.9 3.8 %shard_map.47 = (f32[8,48,256]{2,1,0:T(8,128)}, f32[128,256]{1,0:T(8,128)}, bf16[32,2048]{1,0:T(8,128)(2,1)}, bf16[32,2048]{1,0:T(8,128)(2,1)}, bf16[32,2048]{1,0:T(8,128)(2,1)}, /*index=5*/bf16[32,2048]{1,0:T(8,128)(2,1)}) custom-call(bf16[2,256,2048]{2,1,0:T(8,128)(2,1)} %blocks.5, bf16[2,2048,128]{2,1,0:T(8,128)(2,1)} %history.5, ...), custom_call_target="tpu_custom_call" | custom-call | flops 268435456 | bytes 5013504 | tf_op jit(solution)/shard_map/pallas_call | solution.py:29
  17.8 4.7 %all-to-all-start = ((f32[8,48,256]{2,1,0:T(8,128)}), f32[8,48,256]{2,1,0:T(8,128)S(1)}, u32[]{:S(2)}, u32[]{:S(2)}) async-start(f32[8,48,256]{2,1,0:T(8,128)} %get-tuple-element.21), calls=%async_computation | async-start | bytes 786432 | tf_op jit(solution)/shard_map/all_to_all | solution.py:17
  22.4 5.5 %collective-permute-start.2 = (bf16[32,2048]{1,0:T(8,128)(2,1)}, bf16[32,2048]{1,0:T(8,128)(2,1)}, u32[]{:S(2)}, u32[]{:S(2)}) collective-permute-start(bf16[32,2048]{1,0:T(8,128)(2,1)} %get-tuple-element.26), channel_id=1, source_target_pairs={{0,32},{8,40},{1,33},{9,41},{2,34},{10,42},{3,35},{11,43},{4,36},{... | collective-permute-start | bytes 393224 | tf_op jit(solution)/shard_map/ppermute | solution.py:250
  27.9 1.9 %collective-permute-start.3 = (bf16[32,2048]{1,0:T(8,128)(2,1)}, bf16[32,2048]{1,0:T(8,128)(2,1)}, u32[]{:S(2)}, u32[]{:S(2)}) collective-permute-start(bf16[32,2048]{1,0:T(8,128)(2,1)} %get-tuple-element.27), channel_id=1, source_target_pairs={{0,48},{8,56},{1,49},{9,57},{2,50},{10,58},{3,51},{11,59},{4,52},{... | collective-permute-start | bytes 393224 | tf_op jit(solution)/shard_map/ppermute | solution.py:250
  29.8 1.9 %collective-permute-start.4 = (bf16[32,2048]{1,0:T(8,128)(2,1)}, bf16[32,2048]{1,0:T(8,128)(2,1)}, u32[]{:S(2)}, u32[]{:S(2)}) collective-permute-start(bf16[32,2048]{1,0:T(8,128)(2,1)} %get-tuple-element.28), channel_id=1, source_target_pairs={{0,16},{8,24},{1,17},{9,25},{2,18},{10,26},{3,19},{11,27},{4,20},{... | collective-permute-start | bytes 393224 | tf_op jit(solution)/shard_map/ppermute | solution.py:250
  31.7 0.9 copy-done.5
  32.6 1.8 %shard_map.48.later = f32[128,256]{1,0:T(8,128)S(1)} custom-call(bf16[2,256,2048]{2,1,0:T(8,128)(2,1)S(1)} %copy-done, bf16[2048,128]{1,0:T(8,128)(2,1)} %collective-permute-done.1.before, bf16[2,2048,128]{2,1,0:T(8,128)(2,1)S(1)} %copy-done.1, f32[128,256]{1,0:T(8,128)S(1)} %copy-done.5), custom_call_target="tpu_custom_call" | custom-call | flops 268435456 | bytes 3932160 | tf_op jit(solution)/shard_map/pallas_call | solution.py:29
  34.5 0.6 copy-done.2
  35.1 0.9 copy-done.4
  36.2 13.5 %all_to_all.34.got.got2 = bf16[8,64,256]{2,1,0:T(8,128)(2,1)S(1)} all-to-all(bf16[8,64,256]{2,1,0:T(8,128)(2,1)S(1)} %shard_map.49), channel_id=1, replica_groups=mesh['y'=8,'x'=4,'core'=2,'row'=8] {'y'}, dimensions={0} | all-to-all | bytes 524288 | tf_op jit(solution)/shard_map/all_to_all | solution.py:17
  49.8 0.9 copy-done.3
  50.7 11.3 %all_to_all.35.got3 = bf16[8,64,256]{2,1,0:T(8,128)(2,1)S(1)} all-to-all(bf16[8,64,256]{2,1,0:T(8,128)(2,1)S(1)} %shard_map.50), channel_id=1, replica_groups=mesh['y'=8,'x'=4,'core'=2,'row'=8] {'x','core'}, dimensions={0} | all-to-all | bytes 524288 | tf_op jit(solution)/shard_map/all_to_all | solution.py:17
  62.0 0.3 shard_map.51
  62.3 13.8 %all_to_all.36.got = f32[8,16,256]{2,1,0:T(8,128)S(1)} all-to-all(f32[8,16,256]{2,1,0:T(8,128)S(1)} %get-tuple-element.30), channel_id=1, replica_groups=mesh['y'=8,'x'=4,'core'=2,'row'=8] {'row'}, dimensions={0} | all-to-all | bytes 262144 | tf_op jit(solution)/shard_map/all_to_all | solution.py:17
  76.3 10.4 %all_to_all.37.got = f32[8,16,256]{2,1,0:T(8,128)S(1)} all-to-all(f32[8,16,256]{2,1,0:T(8,128)S(1)} %get-tuple-element.33), channel_id=1, replica_groups=mesh['y'=8,'x'=4,'core'=2,'row'=8] {'y'}, dimensions={0} | all-to-all | bytes 262144 | tf_op jit(solution)/shard_map/all_to_all | solution.py:17
  86.7 0.3 shard_map.53
  87.4 17.1 %all_to_all.38 = f32[64,1,576]{2,1,0:T(1,128)S(1)} all-to-all(f32[64,1,576]{2,1,0:T(1,128)S(1)} %all_to_all.26), channel_id=1, replica_groups=mesh['y'=8,'x'=4,'core'=2,'row'=8] {'x','core','row'}, dimensions={0} | all-to-all | bytes 294912 | tf_op jit(solution)/shard_map/all_to_all | solution.py:17
  104.5 0.4 reduce
  104.9 0.2 reshape.20
  105.3 0.6 pad_maximum_fusion
  (27 shorter events, 1.0 us)
Async XLA Ops:
  2.1 11.0 %collective-permute-start = (bf16[128,2048]{1,0:T(8,128)(2,1)}, bf16[128,2048]{1,0:T(8,128)(2,1)S(1)}, u32[]{:S(2)}, u32[]{:S(2)}) collective-permute-start(bf16[128,2048]{1,0:T(8,128)(2,1)} %get-tuple-element.20), channel_id=1, source_target_pairs={{0,8},{8,0},{16,24},{24,16},{32,40},{40,32},{48,56},{56,48},{64,72... | collective-permute-start | bytes 1572872 | tf_op jit(solution)/shard_map/ppermute | solution.py:235
  10.9 20.8 %copy-start = (bf16[2,256,2048]{2,1,0:T(8,128)(2,1)S(1)}, bf16[2,256,2048]{2,1,0:T(8,128)(2,1)}, u32[]{:S(2)}) copy-start(bf16[2,256,2048]{2,1,0:T(8,128)(2,1)} %blocks.5) | copy-start | bytes 6291460
  10.9 20.8 %copy-start.1 = (bf16[2,2048,128]{2,1,0:T(8,128)(2,1)S(1)}, bf16[2,2048,128]{2,1,0:T(8,128)(2,1)}, u32[]{:S(2)}) copy-start(bf16[2,2048,128]{2,1,0:T(8,128)(2,1)} %history.5) | copy-start | bytes 3145732
  10.9 20.8 %collective-permute-start.1 = (bf16[2048,128]{1,0:T(8,128)(2,1)}, bf16[2048,128]{1,0:T(8,128)(2,1)}, u32[]{:S(2)}, u32[]{:S(2)}) collective-permute-start(bf16[2048,128]{1,0:T(8,128)(2,1)} %get-tuple-element.22), channel_id=1, source_target_pairs={{0,8},{8,16},{16,24},{24,32},{32,40},{40,48},{48,56},{56,64},{64,7... | collective-permute-start | bytes 1572872 | tf_op jit(solution)/shard_map/ppermute | solution.py:236
  13.1 0.8 copy-start.6
  17.8 17.4 %all-to-all-start = ((f32[8,48,256]{2,1,0:T(8,128)}), f32[8,48,256]{2,1,0:T(8,128)S(1)}, u32[]{:S(2)}, u32[]{:S(2)}) async-start(f32[8,48,256]{2,1,0:T(8,128)} %get-tuple-element.21), calls=%async_computation | async-start | bytes 786432 | tf_op jit(solution)/shard_map/all_to_all | solution.py:17
  22.4 12.7 %collective-permute-start.2 = (bf16[32,2048]{1,0:T(8,128)(2,1)}, bf16[32,2048]{1,0:T(8,128)(2,1)}, u32[]{:S(2)}, u32[]{:S(2)}) collective-permute-start(bf16[32,2048]{1,0:T(8,128)(2,1)} %get-tuple-element.26), channel_id=1, source_target_pairs={{0,32},{8,40},{1,33},{9,41},{2,34},{10,42},{3,35},{11,43},{4,36},{... | collective-permute-start | bytes 393224 | tf_op jit(solution)/shard_map/ppermute | solution.py:250
  27.9 7.3 %collective-permute-start.3 = (bf16[32,2048]{1,0:T(8,128)(2,1)}, bf16[32,2048]{1,0:T(8,128)(2,1)}, u32[]{:S(2)}, u32[]{:S(2)}) collective-permute-start(bf16[32,2048]{1,0:T(8,128)(2,1)} %get-tuple-element.27), channel_id=1, source_target_pairs={{0,48},{8,56},{1,49},{9,57},{2,50},{10,58},{3,51},{11,59},{4,52},{... | collective-permute-start | bytes 393224 | tf_op jit(solution)/shard_map/ppermute | solution.py:250
  29.8 5.3 %collective-permute-start.4 = (bf16[32,2048]{1,0:T(8,128)(2,1)}, bf16[32,2048]{1,0:T(8,128)(2,1)}, u32[]{:S(2)}, u32[]{:S(2)}) collective-permute-start(bf16[32,2048]{1,0:T(8,128)(2,1)} %get-tuple-element.28), channel_id=1, source_target_pairs={{0,16},{8,24},{1,17},{9,25},{2,18},{10,26},{3,19},{11,27},{4,20},{... | collective-permute-start | bytes 393224 | tf_op jit(solution)/shard_map/ppermute | solution.py:250
  31.7 0.9 copy-start.5
  34.5 0.7 copy-start.2
  35.1 0.9 copy-start.4
  49.8 0.9 copy-start.3

commit v10 on v7

--- a/solution.py
+++ b/solution.py
@@ -1,3 +1,5 @@
+import functools
+
 import numpy as np
 import jax
 import jax.numpy as jnp
@@ -8,6 +10,7 @@
 
 LAG = ("y", "x", "core")
 W = ("x", "core")
+HOLDERS = (0, 6, 2, 1)
 F32 = jnp.float32
 BF16 = jnp.bfloat16
 
@@ -66,16 +69,20 @@
     return jnp.where(lax.axis_index(LAG) == 0, total - field, total).T
 
 
-def last_of(history, out, sems):
-    count = sems.shape[0]
+def last_of(history, out, held, sems):
+    count = sems.shape[1]
     step = out.shape[0] // count
-    loads = []
+    moves = []
     for i in range(count):
         rows = pl.ds(i * step, step)
-        loads.append(pltpu.make_async_copy(history.at[1, rows], out.at[rows], sems.at[i]))
-        loads[-1].start()
-    for load in loads:
+        load = pltpu.make_async_copy(history.at[1, rows], held.at[rows], sems.at[0, i])
+        moves.append((load, pltpu.make_async_copy(held.at[rows], out.at[rows], sems.at[1, i])))
+        load.start()
+    for load, store in moves:
         load.wait()
+        store.start()
+    for _, store in moves:
+        store.wait()
 
 
 def first_sums(blocks, history, excitation, inverse, out, lead, *rest):
@@ -126,11 +133,16 @@
 def second_step(got, blocks, *rest):
     sources, (out, piece, sem) = rest[:-3], rest[-3:]
     sources = (blocks.at[0, : piece.shape[0]], *sources)
-    for k, source in enumerate(sources):
-
-        @pl.when(lax.axis_index("x") == k)
+    w = lax.axis_index(W)
+    for k, source in zip(HOLDERS[:-1], sources):
+
+        @pl.when(w == k)
         def _():
             pltpu.make_async_copy(source, piece, sem).start()
+
+    @pl.when(functools.reduce(jnp.logical_and, [w != k for k in HOLDERS[:-1]]))
+    def _():
+        pltpu.make_async_copy(sources[-1], piece, sem).start()
 
     ny, depth, span = out.shape
     cw = (depth - piece.shape[0]) // 2
@@ -162,8 +174,8 @@
         out[z] = term
     part1[...] = sum_pairs(got3, 0, cw)
     cut = got3.shape[1] - 2 * cw
-    for x in range(first.shape[0] // cut):
-        first[x * cut : (x + 1) * cut] = got3[2 * x, 2 * cw :]
+    for i, w in enumerate(HOLDERS):
+        first[i * cut : (i + 1) * cut] = got3[w, 2 * cw :]
 
 
 def fifth_step(got, part1, first, out, mine):
@@ -193,7 +205,7 @@
     cw = columns // nw
     own = self_inverse.shape[0]
     nlag = ny * nw
-    cut = rows // nx
+    cut = rows // len(HOLDERS)
     span = nw * own
     work = 2 * rows * size * columns * 2
     small = 2 * cw * rows * span
@@ -203,7 +215,7 @@
         (history.shape[1:], BF16),
         0,
         history,
-        scratch=[pltpu.SemaphoreType.DMA((4,))],
+        scratch=[pltpu.VMEM(history.shape[1:], BF16), pltpu.SemaphoreType.DMA((2, 4))],
         held=[pltpu.HBM],
         given=[pltpu.HBM],
         limit=60,
@@ -211,18 +223,17 @@
     before = lax.ppermute(before, LAG, [(i, i + 1) for i in range(nlag - 1)])
     later = call(later_sums, ((columns, rows), F32), work, blocks, before, history)
 
-    outs = [((nw, cw + own, rows), F32), ((columns, rows), F32)] + [((cut, size), BF16)] * (nx - 1)
+    outs = [((nw, cw + own, rows), F32), ((columns, rows), F32)] + [((cut, size), BF16)] * (len(HOLDERS) - 1)
     scratch = [pltpu.VMEM(blocks.shape, BF16), pltpu.VMEM(history.shape, BF16)]
     scratch += [pltpu.VMEM(excitation.shape, F32), pltpu.VMEM((own, rows), F32)]
-    scratch += [pltpu.VMEM(*o) for o in outs[:2]] + [pltpu.SemaphoreType.DMA((8 + nx,))]
+    scratch += [pltpu.VMEM(*o) for o in outs[:2]] + [pltpu.SemaphoreType.DMA((7 + len(HOLDERS),))]
     args = blocks, history, excitation, self_inverse
     held, given = [pltpu.HBM] * len(args), [pltpu.HBM] * len(outs)
     send, lead, *pieces = call(
         first_sums, outs, work, *args, scratch=scratch, held=held, given=given, limit=60
     )
     got1 = swap(send, W)
-    for k in range(1, nx):
-        pieces[k - 1] = lax.ppermute(pieces[k - 1], LAG, [(0, k * nc)])
+    pieces = [lax.ppermute(p, LAG, [(0, w)]) for p, w in zip(pieces, HOLDERS[1:])]
     got1, later = lax.optimization_barrier((got1, later))
     send = call(
         second_step,
@@ -232,7 +243,7 @@
         blocks,
         *pieces,
         scratch=[pltpu.VMEM((cut, size), BF16), pltpu.SemaphoreType.DMA(())],
-        held=[pltpu.VMEM] + [pltpu.HBM] * nx,
+        held=[pltpu.VMEM] + [pltpu.HBM] * len(HOLDERS),
     )
     got2 = swap(send, "y")
     send = call(third_step, ((nw, 2 * cw + cut, rows), BF16), small, got2, later, lead)

time: 120 us -> 105 us (0.88)
  Pallas kernels: 23.3 us -> 9.01 us
  blocking collectives: 75.6 us -> 72.3 us
  waiting for transfers between devices: 1.51 us -> 4 us
    pallas_call x8, Pallas kernels: 23.3 us -> 9.01 us  [call(): pl.pallas_call(body, out_shape=shapes[0] if single else shapes, in_specs=...]
    all_to_all x5, blocking collectives: 75.6 us -> 72.3 us  [swap(): return lax.all_to_all(pieces, axes, 0, 0, tiled=True)]
    ppermute x3, waiting for transfers between devices: 0.01 us -> 2.42 us  [shards(): lax.ppermute(p, LAG, [(0, w)])]
  transfers between devices with their start and end apart: 5 -> 5, of which waited for: 1 -> 2; matrix products, arithmetic and copies ran while one was open for 0% -> 0% of each run, Pallas kernels for 4% -> 5%
where the time goes in v10:
time: 105 us
  blocking collectives  72.3 us (69%)
  starting transfers between devices  16.6 us (16%)
  Pallas kernels  9.01 us (9%)
  waiting for transfers between devices  4 us (4%)
  local copies, waits for them, and re-layouts  1.39 us (1%)
  other arithmetic  1.07 us (1%)
    all_to_all x5, blocking collectives, swap(): return lax.all_to_all(pieces, axes, 0, 0, tiled=True)  72.3 us
    pallas_call x8, Pallas kernels, call(): pl.pallas_call(body, out_shape=shapes[0] if single else shapes, in_specs=...  9.01 us
    all_to_all x1, starting transfers between devices, swap(): return lax.all_to_all(pieces, axes, 0, 0, tiled=True)  7.82 us
    ppermute x1, starting transfers between devices, shards(): before = lax.ppermute(before, LAG, [(i, i + 1) for i in range(nlag - 1)])  4.77 us
    ppermute x3, starting transfers between devices, shards(): lax.ppermute(p, LAG, [(0, w)])  4.02 us
    ppermute x3, waiting for transfers between devices, shards(): lax.ppermute(p, LAG, [(0, w)])  2.42 us
  transfers between devices with their start and end apart: 5, of which 2 were waited for; matrix products, arithmetic and copies ran while one was open for 0% of the time, Pallas kernels for 5%

profile of v10, /device:TPU:1, one launch (start us, length us, event | category | flops | bytes accessed | tf_op | source)
XLA Modules:
  0.0 104.6 jit_solution(15725879440770788674)
XLA Ops:
  0.0 1.8 %shard_map.47 = bf16[2048,128]{1,0:T(8,128)(2,1)} custom-call(bf16[2,2048,128]{2,1,0:T(8,128)(2,1)} %history.5), custom_call_target="tpu_custom_call" | custom-call | bytes 1572864 | tf_op jit(solution)/shard_map/pallas_call | solution.py:31
  1.8 4.8 %collective-permute-start = (bf16[2048,128]{1,0:T(8,128)(2,1)}, bf16[2048,128]{1,0:T(8,128)(2,1)}, u32[]{:S(2)}, u32[]{:S(2)}) collective-permute-start(bf16[2048,128]{1,0:T(8,128)(2,1)} %shard_map.47), channel_id=1, source_target_pairs={{0,8},{8,16},{16,24},{24,32},{32,40},{40,48},{48,56},{56,64},{64,7... | collective-permute-start | bytes 1572872 | tf_op jit(solution)/shard_map/ppermute | solution.py:223
  6.6 3.6 %shard_map.46 = (f32[8,48,256]{2,1,0:T(8,128)}, f32[128,256]{1,0:T(8,128)}, bf16[64,2048]{1,0:T(8,128)(2,1)}, bf16[64,2048]{1,0:T(8,128)(2,1)}, bf16[64,2048]{1,0:T(8,128)(2,1)}) custom-call(bf16[2,256,2048]{2,1,0:T(8,128)(2,1)} %blocks.5, bf16[2,2048,128]{2,1,0:T(8,128)(2,1)} %history.5, f32[2,256,128]{2,1,0:T(8,128)} %excitation.1, f32[32,256]{1,0:T(8,128)} %inverse.1), custom_call_target="tpu_custom_call" | custom-call | flops 268435456 | bytes 4751360 | tf_op jit(solution)/shard_map/pallas_call | solution.py:31
  10.2 7.8 %all-to-all-start = ((f32[8,48,256]{2,1,0:T(8,128)}), f32[8,48,256]{2,1,0:T(8,128)S(1)}, u32[]{:S(2)}, u32[]{:S(2)}) async-start(f32[8,48,256]{2,1,0:T(8,128)} %get-tuple-element.17), calls=%async_computation | async-start | bytes 786432 | tf_op jit(solution)/shard_map/all_to_all | solution.py:19
  18.0 1.4 %collective-permute-start.1 = (bf16[64,2048]{1,0:T(8,128)(2,1)}, bf16[64,2048]{1,0:T(8,128)(2,1)}, u32[]{:S(2)}, u32[]{:S(2)}) collective-permute-start(bf16[64,2048]{1,0:T(8,128)(2,1)} %get-tuple-element.19), channel_id=1, source_target_pairs={{0,48},{1,49},{2,50},{3,51},{4,52},{5,53},{6,54},{7,55}} | collective-permute-start | bytes 786440 | tf_op jit(solution)/shard_map/ppermute | solution.py:236
  19.4 1.4 %collective-permute-start.2 = (bf16[64,2048]{1,0:T(8,128)(2,1)}, bf16[64,2048]{1,0:T(8,128)(2,1)}, u32[]{:S(2)}, u32[]{:S(2)}) collective-permute-start(bf16[64,2048]{1,0:T(8,128)(2,1)} %get-tuple-element.20), channel_id=1, source_target_pairs={{0,16},{1,17},{2,18},{3,19},{4,20},{5,21},{6,22},{7,23}} | collective-permute-start | bytes 786440 | tf_op jit(solution)/shard_map/ppermute | solution.py:236
  20.8 1.3 %collective-permute-start.3 = (bf16[64,2048]{1,0:T(8,128)(2,1)}, bf16[64,2048]{1,0:T(8,128)(2,1)}, u32[]{:S(2)}, u32[]{:S(2)}) collective-permute-start(bf16[64,2048]{1,0:T(8,128)(2,1)} %get-tuple-element.21), channel_id=1, source_target_pairs={{0,8},{1,9},{2,10},{3,11},{4,12},{5,13},{6,14},{7,15}} | collective-permute-start | bytes 786440 | tf_op jit(solution)/shard_map/ppermute | solution.py:236
  22.1 1.8 %shard_map.48.later = f32[128,256]{1,0:T(8,128)S(1)} custom-call(bf16[2,256,2048]{2,1,0:T(8,128)(2,1)S(1)} %copy-done, bf16[2048,128]{1,0:T(8,128)(2,1)} %collective-permute-done.before, bf16[2,2048,128]{2,1,0:T(8,128)(2,1)S(1)} %copy-done.1), custom_call_target="tpu_custom_call" | custom-call | flops 268435456 | bytes 3801088 | tf_op jit(solution)/shard_map/pallas_call | solution.py:31
  23.9 0.6 copy-done.2
  24.6 1.6 %all-to-all-done.got.got1 = f32[8,48,256]{2,1,0:T(8,128)S(1)} async-done(((f32[8,48,256]{2,1,0:T(8,128)}), f32[8,48,256]{2,1,0:T(8,128)S(1)}, u32[]{:S(2)}, u32[]{:S(2)}) %all-to-all-start) | async-done | bytes 393248 | tf_op jit(solution)/shard_map/all_to_all | solution.py:19
  26.1 2.4 %collective-permute-done.3.rest_2_ = bf16[64,2048]{1,0:T(8,128)(2,1)} collective-permute-done((bf16[64,2048]{1,0:T(8,128)(2,1)}, bf16[64,2048]{1,0:T(8,128)(2,1)}, u32[]{:S(2)}, u32[]{:S(2)}) %collective-permute-start.3) | collective-permute-done | bytes 262176 | tf_op jit(solution)/shard_map/ppermute | solution.py:236
  28.6 1.0 shard_map.49
  29.5 15.9 %all_to_all.34.got.got2 = bf16[8,96,256]{2,1,0:T(8,128)(2,1)S(1)} all-to-all(bf16[8,96,256]{2,1,0:T(8,128)(2,1)S(1)} %shard_map.49), channel_id=1, replica_groups=mesh['y'=8,'x'=4,'core'=2,'row'=8] {'y'}, dimensions={0} | all-to-all | bytes 786432 | tf_op jit(solution)/shard_map/all_to_all | solution.py:19
  45.5 12.6 %all_to_all.35.got3 = bf16[8,96,256]{2,1,0:T(8,128)(2,1)S(1)} all-to-all(bf16[8,96,256]{2,1,0:T(8,128)(2,1)S(1)} %shard_map.50), channel_id=1, replica_groups=mesh['y'=8,'x'=4,'core'=2,'row'=8] {'x','core'}, dimensions={0} | all-to-all | bytes 786432 | tf_op jit(solution)/shard_map/all_to_all | solution.py:19
  58.1 0.3 shard_map.51
  58.4 16.3 %all_to_all.36.got = f32[8,16,256]{2,1,0:T(8,128)S(1)} all-to-all(f32[8,16,256]{2,1,0:T(8,128)S(1)} %get-tuple-element.24), channel_id=1, replica_groups=mesh['y'=8,'x'=4,'core'=2,'row'=8] {'row'}, dimensions={0} | all-to-all | bytes 262144 | tf_op jit(solution)/shard_map/all_to_all | solution.py:19
  74.7 0.2 shard_map.52
  74.9 10.4 %all_to_all.37.got = f32[8,16,256]{2,1,0:T(8,128)S(1)} all-to-all(f32[8,16,256]{2,1,0:T(8,128)S(1)} %get-tuple-element.27), channel_id=1, replica_groups=mesh['y'=8,'x'=4,'core'=2,'row'=8] {'y'}, dimensions={0} | all-to-all | bytes 262144 | tf_op jit(solution)/shard_map/all_to_all | solution.py:19
  85.3 0.3 shard_map.53
  85.8 0.2 all_to_all.26
  86.0 17.1 %all_to_all.38 = f32[64,1,576]{2,1,0:T(1,128)S(1)} all-to-all(f32[64,1,576]{2,1,0:T(1,128)S(1)} %all_to_all.26), channel_id=1, replica_groups=mesh['y'=8,'x'=4,'core'=2,'row'=8] {'x','core','row'}, dimensions={0} | all-to-all | bytes 294912 | tf_op jit(solution)/shard_map/all_to_all | solution.py:19
  103.1 0.4 reduce
  103.5 0.2 reshape.20
  103.9 0.6 pad_maximum_fusion
  (21 shorter events, 0.5 us)
Async XLA Ops:
  1.8 20.3 %copy-start = (bf16[2,256,2048]{2,1,0:T(8,128)(2,1)S(1)}, bf16[2,256,2048]{2,1,0:T(8,128)(2,1)}, u32[]{:S(2)}) copy-start(bf16[2,256,2048]{2,1,0:T(8,128)(2,1)} %blocks.5) | copy-start | bytes 6291460
  1.8 20.3 %copy-start.1 = (bf16[2,2048,128]{2,1,0:T(8,128)(2,1)S(1)}, bf16[2,2048,128]{2,1,0:T(8,128)(2,1)}, u32[]{:S(2)}) copy-start(bf16[2,2048,128]{2,1,0:T(8,128)(2,1)} %history.5) | copy-start | bytes 3145732
  1.8 20.2 %collective-permute-start = (bf16[2048,128]{1,0:T(8,128)(2,1)}, bf16[2048,128]{1,0:T(8,128)(2,1)}, u32[]{:S(2)}, u32[]{:S(2)}) collective-permute-start(bf16[2048,128]{1,0:T(8,128)(2,1)} %shard_map.47), channel_id=1, source_target_pairs={{0,8},{8,16},{16,24},{24,32},{32,40},{40,48},{48,56},{56,64},{64,7... | collective-permute-start | bytes 1572872 | tf_op jit(solution)/shard_map/ppermute | solution.py:223
  10.2 15.9 %all-to-all-start = ((f32[8,48,256]{2,1,0:T(8,128)}), f32[8,48,256]{2,1,0:T(8,128)S(1)}, u32[]{:S(2)}, u32[]{:S(2)}) async-start(f32[8,48,256]{2,1,0:T(8,128)} %get-tuple-element.17), calls=%async_computation | async-start | bytes 786432 | tf_op jit(solution)/shard_map/all_to_all | solution.py:19
  18.0 8.1 %collective-permute-start.1 = (bf16[64,2048]{1,0:T(8,128)(2,1)}, bf16[64,2048]{1,0:T(8,128)(2,1)}, u32[]{:S(2)}, u32[]{:S(2)}) collective-permute-start(bf16[64,2048]{1,0:T(8,128)(2,1)} %get-tuple-element.19), channel_id=1, source_target_pairs={{0,48},{1,49},{2,50},{3,51},{4,52},{5,53},{6,54},{7,55}} | collective-permute-start | bytes 786440 | tf_op jit(solution)/shard_map/ppermute | solution.py:236
  19.4 6.7 %collective-permute-start.2 = (bf16[64,2048]{1,0:T(8,128)(2,1)}, bf16[64,2048]{1,0:T(8,128)(2,1)}, u32[]{:S(2)}, u32[]{:S(2)}) collective-permute-start(bf16[64,2048]{1,0:T(8,128)(2,1)} %get-tuple-element.20), channel_id=1, source_target_pairs={{0,16},{1,17},{2,18},{3,19},{4,20},{5,21},{6,22},{7,23}} | collective-permute-start | bytes 786440 | tf_op jit(solution)/shard_map/ppermute | solution.py:236
  20.8 7.8 %collective-permute-start.3 = (bf16[64,2048]{1,0:T(8,128)(2,1)}, bf16[64,2048]{1,0:T(8,128)(2,1)}, u32[]{:S(2)}, u32[]{:S(2)}) collective-permute-start(bf16[64,2048]{1,0:T(8,128)(2,1)} %get-tuple-element.21), channel_id=1, source_target_pairs={{0,8},{1,9},{2,10},{3,11},{4,12},{5,13},{6,14},{7,15}} | collective-permute-start | bytes 786440 | tf_op jit(solution)/shard_map/ppermute | solution.py:236
  23.9 0.7 copy-start.2
  24.6 20.9 %copy-start.4 = (f32[128,256]{1,0:T(8,128)S(1)}, f32[128,256]{1,0:T(8,128)}, u32[]{:S(2)}) copy-start(f32[128,256]{1,0:T(8,128)} %get-tuple-element.23.lead) | copy-start | bytes 393220
  26.1 19.3 %copy-start.3 = (f32[128,256]{1,0:T(8,128)S(1)}, f32[128,256]{1,0:T(8,128)}, u32[]{:S(2)}) copy-start(f32[128,256]{1,0:T(8,128)} %copy-done.2) | copy-start | bytes 393220

commit v11 on v9

--- a/solution.py
+++ b/solution.py
@@ -87,8 +87,8 @@
         store.wait()
 
 
-def first_sums(blocks, history, excitation, inverse, half, out, lead, *rest):
-    pieces, (b, h, e, own, o, f, g, sems) = rest[:-8], rest[-8:]
+def first_sums(blocks, history, excitation, inverse, half, out, field, *rest):
+    pieces, (b, h, e, own, turned, o, f, g, sems) = rest[:-9], rest[-9:]
     cut = pieces[0].shape[0]
     loads = [
         pltpu.make_async_copy(history.at[0], h.at[0], sems.at[0]),
@@ -126,8 +126,9 @@
         o[w, cw:] = own[...]
     stores = [pltpu.make_async_copy(o, out, sems.at[7])]
     stores[-1].start()
-    f[...] = less_field(jnp.zeros_like(e[1]), e[1])
-    stores.append(pltpu.make_async_copy(f, lead, sems.at[8]))
+    turned[...] = e[1].T
+    f[...] = turned[pl.ds(pl.multiple_of(lax.axis_index(W) * cw, cw), cw)]
+    stores.append(pltpu.make_async_copy(f, field, sems.at[8]))
     stores[-1].start()
     for k, piece in enumerate(pieces):
         rows = g.at[k * cut : (k + 1) * cut]
@@ -136,8 +137,8 @@
         store.wait()
 
 
-def later_sums(blocks, before, history, lead, out):
-    out[...] = (mm(blocks[1], history[0]) + mm(blocks[0], before[...])).T + lead[...]
+def later_sums(blocks, before, history, out):
+    out[...] = (mm(blocks[1], history[0]) + mm(blocks[0], before[...])).T
 
 
 def second_step(got, *rest):
@@ -196,10 +197,11 @@
     mine[...] = share
 
 
-def sixth_step(got1, got, mine, out):
+def sixth_step(got1, got, field, mine, out):
     cw = got.shape[1]
     inverse = got1[:, cw:].reshape(-1, got.shape[2])
-    out[:cw] = -mm_t(sum_first(got, 0, cw), inverse, lax.Precision.HIGHEST)
+    resid = field[...] - sum_first(got, 0, cw)
+    out[:cw] = mm_t(resid, inverse, lax.Precision.HIGHEST)
     out[cw:] = mine[...]
 
 
@@ -235,20 +237,22 @@
     half = lax.ppermute(half, LAG, [(i, i ^ 1) for i in range(nlag)])
     before = lax.ppermute(before, LAG, [(i, i + 1) for i in range(nlag - 1)])
 
-    outs = [((nw, cw + own, rows), F32), ((columns, rows), F32)] + [((cut, size), BF16)] * nx
+    outs = [((nw, cw + own, rows), F32), ((cw, rows), F32)] + [((cut, size), BF16)] * nx
     scratch = [pltpu.VMEM(blocks.shape, BF16), pltpu.VMEM(history.shape, BF16)]
     scratch += [pltpu.VMEM(excitation.shape, F32), pltpu.VMEM((own, rows), F32)]
+    scratch += [pltpu.VMEM((columns, rows), F32)]
     scratch += [pltpu.VMEM(*o) for o in outs[:2]] + [pltpu.VMEM(part, BF16)]
     scratch += [pltpu.SemaphoreType.DMA((9 + nx,))]
     args = blocks, history, excitation, self_inverse, half
     held, given = [pltpu.HBM] * len(args), [pltpu.HBM] * len(outs)
-    send, lead, *pieces = call(
+    send, field, *pieces = call(
         first_sums, outs, work, *args, scratch=scratch, held=held, given=given, limit=60
     )
     got1 = swap(send, W)
     routes = {k: [(c, k * nc + c) for c in range(nc)] for k in ORDER}
     sent = [lax.ppermute(pieces[k], LAG, routes[k]) for k in ORDER]
-    later = call(later_sums, ((columns, rows), F32), work, blocks, before, history, lead)
+    got1, before = lax.optimization_barrier((got1, before))
+    later = call(later_sums, ((columns, rows), F32), work, blocks, before, history)
     got1, later = lax.optimization_barrier((got1, later))
     send = call(
         second_step,
@@ -259,6 +263,7 @@
         *sent,
         scratch=[pltpu.VMEM((cut, size), BF16), pltpu.SemaphoreType.DMA(())],
         held=[pltpu.VMEM] + [pltpu.HBM] * nx,
+        limit=24,
     )
     got2 = swap(send, "y")
     send = call(third_step, ((nw, 2 * cw + cut, rows), BF16), small, got2, later)
@@ -270,7 +275,7 @@
     outs = [((ny, cw, rows), F32), ((cz, span), F32)]
     send, mine0 = call(fifth_step, outs, small, got4, part1, first)
     got5 = swap(send, "y")
-    both = call(sixth_step, ((cw + cz, span), F32), small, got1, got5, mine0)
+    both = call(sixth_step, ((cw + cz, span), F32), small, got1, got5, field, mine0)
     both = both.reshape(cw + cz, nw, own).transpose(1, 0, 2).reshape(nw, 1, (cw + cz) * own)
     both = jnp.broadcast_to(both, (nw, nz, (cw + cz) * own)).reshape(nw * nz, (cw + cz) * own)
     got = swap(both, W + ("row",)).reshape(nw, nz, cw + cz, own)

time: 107 us -> 105 us (0.981)
  local copies, waits for them, and re-layouts: 4.9 us -> 1.58 us
  blocking collectives: 66.1 us -> 68 us
    unnamed x14 -> x10, local copies, waits for them, and re-layouts: 4.17 us -> 0.85 us
    all_to_all x5, blocking collectives: 66.1 us -> 68 us  [swap(): return lax.all_to_all(pieces, axes, 0, 0, tiled=True)]
  transfers between devices with their start and end apart: 6 -> 6, of which waited for: 0 -> 1; matrix products, arithmetic and copies ran while one was open for 0% -> 0% of each run, Pallas kernels for 5% -> 5%
where the time goes in v11:
time: 105 us
  blocking collectives  68 us (65%)
  starting transfers between devices  25 us (24%)
  Pallas kernels  8.68 us (8%)
  local copies, waits for them, and re-layouts  1.58 us (2%)
  other arithmetic  1.07 us (1%)
    all_to_all x5, blocking collectives, swap(): return lax.all_to_all(pieces, axes, 0, 0, tiled=True)  68 us
    ppermute x3, starting transfers between devices, shards(): sent = [lax.ppermute(pieces[k], LAG, routes[k]) for k in ORDER]  9.34 us
    ppermute x1, starting transfers between devices, shards(): half = lax.ppermute(half, LAG, [(i, i ^ 1) for i in range(nlag)])  8.79 us
    pallas_call x8, Pallas kernels, call(): pl.pallas_call(body, out_shape=shapes[0] if single else shapes, in_specs=...  8.68 us
    all_to_all x1, starting transfers between devices, swap(): return lax.all_to_all(pieces, axes, 0, 0, tiled=True)  4.65 us
    ppermute x1, starting transfers between devices, shards(): before = lax.ppermute(before, LAG, [(i, i + 1) for i in range(nlag - 1)])  2.18 us
  transfers between devices with their start and end apart: 6, of which 1 were waited for; matrix products, arithmetic and copies ran while one was open for 0% of the time, Pallas kernels for 5%

profile of v11, /device:TPU:1, one launch (start us, length us, event | category | flops | bytes accessed | tf_op | source)
XLA Modules:
  0.0 104.8 jit_solution(4121590036115423234)
XLA Ops:
  0.0 2.1 %shard_map.46 = (bf16[2048,128]{1,0:T(8,128)(2,1)}, bf16[128,2048]{1,0:T(8,128)(2,1)}) custom-call(bf16[2,2048,128]{2,1,0:T(8,128)(2,1)} %history.5, bf16[2,256,2048]{2,1,0:T(8,128)(2,1)} %blocks.5), custom_call_target="tpu_custom_call" | custom-call | bytes 4194304 | tf_op jit(solution)/shard_map/pallas_call | solution.py:29
  2.1 8.8 %collective-permute-start = (bf16[128,2048]{1,0:T(8,128)(2,1)}, bf16[128,2048]{1,0:T(8,128)(2,1)S(1)}, u32[]{:S(2)}, u32[]{:S(2)}) collective-permute-start(bf16[128,2048]{1,0:T(8,128)(2,1)} %get-tuple-element.22), channel_id=1, source_target_pairs={{0,8},{8,0},{16,24},{24,16},{32,40},{40,32},{48,56},{56,48},{64,72... | collective-permute-start | bytes 1572872 | tf_op jit(solution)/shard_map/ppermute | solution.py:237
  10.9 2.2 %collective-permute-start.1 = (bf16[2048,128]{1,0:T(8,128)(2,1)}, bf16[2048,128]{1,0:T(8,128)(2,1)}, u32[]{:S(2)}, u32[]{:S(2)}) collective-permute-start(bf16[2048,128]{1,0:T(8,128)(2,1)} %get-tuple-element.24), channel_id=1, source_target_pairs={{0,8},{8,16},{16,24},{24,32},{32,40},{40,48},{48,56},{56,64},{64,7... | collective-permute-start | bytes 1572872 | tf_op jit(solution)/shard_map/ppermute | solution.py:238
  13.1 0.8 copy-done.4
  13.9 3.8 %shard_map.47 = (f32[8,48,256]{2,1,0:T(8,128)}, f32[16,256]{1,0:T(8,128)}, bf16[32,2048]{1,0:T(8,128)(2,1)}, bf16[32,2048]{1,0:T(8,128)(2,1)}, bf16[32,2048]{1,0:T(8,128)(2,1)}, /*index=5*/bf16[32,2048]{1,0:T(8,128)(2,1)}) custom-call(bf16[2,256,2048]{2,1,0:T(8,128)(2,1)} %blocks.5, bf16[2,2048,128]{2,1,0:T(8,128)(2,1)} %history.5, ...), custom_call_target="tpu_custom_call" | custom-call | flops 268435456 | bytes 4898816 | tf_op jit(solution)/shard_map/pallas_call | solution.py:29
  17.7 4.6 %all-to-all-start = ((f32[8,48,256]{2,1,0:T(8,128)}), f32[8,48,256]{2,1,0:T(8,128)S(1)}, u32[]{:S(2)}, u32[]{:S(2)}) async-start(f32[8,48,256]{2,1,0:T(8,128)} %get-tuple-element.23), calls=%async_computation | async-start | bytes 786432 | tf_op jit(solution)/shard_map/all_to_all | solution.py:17
  22.4 5.5 %collective-permute-start.2 = (bf16[32,2048]{1,0:T(8,128)(2,1)}, bf16[32,2048]{1,0:T(8,128)(2,1)}, u32[]{:S(2)}, u32[]{:S(2)}) collective-permute-start(bf16[32,2048]{1,0:T(8,128)(2,1)} %get-tuple-element.29), channel_id=1, source_target_pairs={{0,32},{8,40},{1,33},{9,41},{2,34},{10,42},{3,35},{11,43},{4,36},{... | collective-permute-start | bytes 393224 | tf_op jit(solution)/shard_map/ppermute | solution.py:253
  27.8 2.0 %collective-permute-start.3 = (bf16[32,2048]{1,0:T(8,128)(2,1)}, bf16[32,2048]{1,0:T(8,128)(2,1)}, u32[]{:S(2)}, u32[]{:S(2)}) collective-permute-start(bf16[32,2048]{1,0:T(8,128)(2,1)} %get-tuple-element.30), channel_id=1, source_target_pairs={{0,48},{8,56},{1,49},{9,57},{2,50},{10,58},{3,51},{11,59},{4,52},{... | collective-permute-start | bytes 393224 | tf_op jit(solution)/shard_map/ppermute | solution.py:253
  29.8 1.9 %collective-permute-start.4 = (bf16[32,2048]{1,0:T(8,128)(2,1)}, bf16[32,2048]{1,0:T(8,128)(2,1)}, u32[]{:S(2)}, u32[]{:S(2)}) collective-permute-start(bf16[32,2048]{1,0:T(8,128)(2,1)} %get-tuple-element.31), channel_id=1, source_target_pairs={{0,16},{8,24},{1,17},{9,25},{2,18},{10,26},{3,19},{11,27},{4,20},{... | collective-permute-start | bytes 393224 | tf_op jit(solution)/shard_map/ppermute | solution.py:253
  31.7 1.8 %shard_map.48.later = f32[128,256]{1,0:T(8,128)S(1)} custom-call(bf16[2,256,2048]{2,1,0:T(8,128)(2,1)S(1)} %copy-done, bf16[2048,128]{1,0:T(8,128)(2,1)} %collective-permute-done.1.before, bf16[2,2048,128]{2,1,0:T(8,128)(2,1)S(1)} %copy-done.1), custom_call_target="tpu_custom_call" | custom-call | flops 268435456 | bytes 3801088 | tf_op jit(solution)/shard_map/pallas_call | solution.py:29
  33.6 0.3 collective-permute-done.4.rest_3_
  33.9 0.2 shard_map.49
  34.1 12.5 %all_to_all.34.got.got2 = bf16[8,64,256]{2,1,0:T(8,128)(2,1)S(1)} all-to-all(bf16[8,64,256]{2,1,0:T(8,128)(2,1)S(1)} %shard_map.49), channel_id=1, replica_groups=mesh['y'=8,'x'=4,'core'=2,'row'=8] {'y'}, dimensions={0} | all-to-all | bytes 524288 | tf_op jit(solution)/shard_map/all_to_all | solution.py:17
  46.7 13.5 %all_to_all.35.got3 = bf16[8,64,256]{2,1,0:T(8,128)(2,1)S(1)} all-to-all(bf16[8,64,256]{2,1,0:T(8,128)(2,1)S(1)} %shard_map.50), channel_id=1, replica_groups=mesh['y'=8,'x'=4,'core'=2,'row'=8] {'x','core'}, dimensions={0} | all-to-all | bytes 524288 | tf_op jit(solution)/shard_map/all_to_all | solution.py:17
  60.1 0.3 shard_map.51
  60.5 14.4 %all_to_all.36.got = f32[8,16,256]{2,1,0:T(8,128)S(1)} all-to-all(f32[8,16,256]{2,1,0:T(8,128)S(1)} %get-tuple-element.33), channel_id=1, replica_groups=mesh['y'=8,'x'=4,'core'=2,'row'=8] {'row'}, dimensions={0} | all-to-all | bytes 262144 | tf_op jit(solution)/shard_map/all_to_all | solution.py:17
  74.9 0.2 shard_map.52
  75.1 10.4 %all_to_all.37.got = f32[8,16,256]{2,1,0:T(8,128)S(1)} all-to-all(f32[8,16,256]{2,1,0:T(8,128)S(1)} %get-tuple-element.36), channel_id=1, replica_groups=mesh['y'=8,'x'=4,'core'=2,'row'=8] {'y'}, dimensions={0} | all-to-all | bytes 262144 | tf_op jit(solution)/shard_map/all_to_all | solution.py:17
  85.5 0.3 shard_map.53
  86.1 0.2 all_to_all.26
  86.2 17.1 %all_to_all.38 = f32[64,1,576]{2,1,0:T(1,128)S(1)} all-to-all(f32[64,1,576]{2,1,0:T(1,128)S(1)} %all_to_all.26), channel_id=1, replica_groups=mesh['y'=8,'x'=4,'core'=2,'row'=8] {'x','core','row'}, dimensions={0} | all-to-all | bytes 294912 | tf_op jit(solution)/shard_map/all_to_all | solution.py:17
  103.3 0.4 reduce
  103.7 0.2 reshape.20
  104.1 0.6 pad_maximum_fusion
  (23 shorter events, 0.5 us)
Async XLA Ops:
  2.1 11.0 %collective-permute-start = (bf16[128,2048]{1,0:T(8,128)(2,1)}, bf16[128,2048]{1,0:T(8,128)(2,1)S(1)}, u32[]{:S(2)}, u32[]{:S(2)}) collective-permute-start(bf16[128,2048]{1,0:T(8,128)(2,1)} %get-tuple-element.22), channel_id=1, source_target_pairs={{0,8},{8,0},{16,24},{24,16},{32,40},{40,32},{48,56},{56,48},{64,72... | collective-permute-start | bytes 1572872 | tf_op jit(solution)/shard_map/ppermute | solution.py:237
  10.9 20.8 %copy-start = (bf16[2,256,2048]{2,1,0:T(8,128)(2,1)S(1)}, bf16[2,256,2048]{2,1,0:T(8,128)(2,1)}, u32[]{:S(2)}) copy-start(bf16[2,256,2048]{2,1,0:T(8,128)(2,1)} %blocks.5) | copy-start | bytes 6291460
  10.9 20.8 %copy-start.1 = (bf16[2,2048,128]{2,1,0:T(8,128)(2,1)S(1)}, bf16[2,2048,128]{2,1,0:T(8,128)(2,1)}, u32[]{:S(2)}) copy-start(bf16[2,2048,128]{2,1,0:T(8,128)(2,1)} %history.5) | copy-start | bytes 3145732
  10.9 20.8 %collective-permute-start.1 = (bf16[2048,128]{1,0:T(8,128)(2,1)}, bf16[2048,128]{1,0:T(8,128)(2,1)}, u32[]{:S(2)}, u32[]{:S(2)}) collective-permute-start(bf16[2048,128]{1,0:T(8,128)(2,1)} %get-tuple-element.24), channel_id=1, source_target_pairs={{0,8},{8,16},{16,24},{24,32},{32,40},{40,48},{48,56},{56,64},{64,7... | collective-permute-start | bytes 1572872 | tf_op jit(solution)/shard_map/ppermute | solution.py:238
  13.1 0.8 copy-start.4
  17.7 14.0 %all-to-all-start = ((f32[8,48,256]{2,1,0:T(8,128)}), f32[8,48,256]{2,1,0:T(8,128)S(1)}, u32[]{:S(2)}, u32[]{:S(2)}) async-start(f32[8,48,256]{2,1,0:T(8,128)} %get-tuple-element.23), calls=%async_computation | async-start | bytes 786432 | tf_op jit(solution)/shard_map/all_to_all | solution.py:17
  22.4 11.2 %collective-permute-start.2 = (bf16[32,2048]{1,0:T(8,128)(2,1)}, bf16[32,2048]{1,0:T(8,128)(2,1)}, u32[]{:S(2)}, u32[]{:S(2)}) collective-permute-start(bf16[32,2048]{1,0:T(8,128)(2,1)} %get-tuple-element.29), channel_id=1, source_target_pairs={{0,32},{8,40},{1,33},{9,41},{2,34},{10,42},{3,35},{11,43},{4,36},{... | collective-permute-start | bytes 393224 | tf_op jit(solution)/shard_map/ppermute | solution.py:253
  27.8 5.8 %collective-permute-start.3 = (bf16[32,2048]{1,0:T(8,128)(2,1)}, bf16[32,2048]{1,0:T(8,128)(2,1)}, u32[]{:S(2)}, u32[]{:S(2)}) collective-permute-start(bf16[32,2048]{1,0:T(8,128)(2,1)} %get-tuple-element.30), channel_id=1, source_target_pairs={{0,48},{8,56},{1,49},{9,57},{2,50},{10,58},{3,51},{11,59},{4,52},{... | collective-permute-start | bytes 393224 | tf_op jit(solution)/shard_map/ppermute | solution.py:253
  29.8 4.1 %collective-permute-start.4 = (bf16[32,2048]{1,0:T(8,128)(2,1)}, bf16[32,2048]{1,0:T(8,128)(2,1)}, u32[]{:S(2)}, u32[]{:S(2)}) collective-permute-start(bf16[32,2048]{1,0:T(8,128)(2,1)} %get-tuple-element.31), channel_id=1, source_target_pairs={{0,16},{8,24},{1,17},{9,25},{2,18},{10,26},{3,19},{11,27},{4,20},{... | collective-permute-start | bytes 393224 | tf_op jit(solution)/shard_map/ppermute | solution.py:253
  31.7 2.2 %copy-start.2 = (bf16[32,2048]{1,0:T(8,128)(2,1)S(1)}, bf16[32,2048]{1,0:T(8,128)(2,1)}, u32[]{:S(2)}) copy-start(bf16[32,2048]{1,0:T(8,128)(2,1)} %get-tuple-element.28.rest_0_) | copy-start | bytes 393220
  33.9 51.6 %copy-start.3 = (f32[16,256]{1,0:T(8,128)S(1)}, f32[16,256]{1,0:T(8,128)}, u32[]{:S(2)}) copy-start(f32[16,256]{1,0:T(8,128)} %get-tuple-element.37.field) | copy-start | bytes 49156

commit v12 on v10

--- a/solution.py
+++ b/solution.py
@@ -69,31 +69,15 @@
     return jnp.where(lax.axis_index(LAG) == 0, total - field, total).T
 
 
-def last_of(history, out, held, sems):
-    count = sems.shape[1]
-    step = out.shape[0] // count
-    moves = []
-    for i in range(count):
-        rows = pl.ds(i * step, step)
-        load = pltpu.make_async_copy(history.at[1, rows], held.at[rows], sems.at[0, i])
-        moves.append((load, pltpu.make_async_copy(held.at[rows], out.at[rows], sems.at[1, i])))
-        load.start()
-    for load, store in moves:
-        load.wait()
-        store.start()
-    for _, store in moves:
-        store.wait()
-
-
-def first_sums(blocks, history, excitation, inverse, out, lead, *rest):
+def first_sums(blocks, history, excitation, inverse, out, lead, last, *rest):
     pieces, (b, h, e, own, o, f, sems) = rest[:-7], rest[-7:]
     cut = pieces[0].shape[0]
     loads = [
-        pltpu.make_async_copy(history.at[0], h.at[0], sems.at[0]),
-        pltpu.make_async_copy(blocks.at[0], b.at[0], sems.at[1]),
-        pltpu.make_async_copy(history.at[1], h.at[1], sems.at[2]),
-        pltpu.make_async_copy(blocks.at[1], b.at[1], sems.at[3]),
         pltpu.make_async_copy(inverse, own, sems.at[4]),
+        pltpu.make_async_copy(history.at[1], h.at[1], sems.at[0]),
+        pltpu.make_async_copy(blocks.at[1], b.at[1], sems.at[1]),
+        pltpu.make_async_copy(history.at[0], h.at[0], sems.at[2]),
+        pltpu.make_async_copy(blocks.at[0], b.at[0], sems.at[3]),
         pltpu.make_async_copy(excitation, e, sems.at[5]),
     ]
     for load in loads:
@@ -101,29 +85,44 @@
     nw, depth, _ = out.shape
     cw = depth - own.shape[0]
     loads[0].wait()
+    for w in range(nw):
+        o[w, cw:] = own[...]
+    gathered = pl.ds(cw, own.shape[0])
+    stores = [pltpu.make_async_copy(o.at[:, gathered], out.at[:, gathered], sems.at[6])]
+    stores[-1].start()
     loads[1].wait()
-    stores = []
-    for k, piece in enumerate(pieces):
-        rows = b.at[0, (k + 1) * cut : (k + 2) * cut]
-        stores.append(pltpu.make_async_copy(rows, piece, sems.at[8 + k]))
-        stores[-1].start()
-    total = mm(b[0], h[0])
+    stores.append(pltpu.make_async_copy(h.at[1], last, sems.at[0]))
+    stores[-1].start()
     loads[2].wait()
+    total = mm(b[1], h[1])
     loads[3].wait()
-    total = total + mm(b[1], h[1])
     loads[4].wait()
+
+    @pl.when(lax.axis_index(LAG) == 0)
+    def _():
+        for k, piece in enumerate(pieces):
+            rows = b.at[0, (k + 1) * cut : (k + 2) * cut]
+            pltpu.make_async_copy(rows, piece, sems.at[8 + k]).start()
+
+    total = total + mm(b[0], h[0])
     loads[5].wait()
     total = less_field(total, e[0])
     for w in range(nw):
         o[w, :cw] = total[w * cw : (w + 1) * cw]
-        o[w, cw:] = own[...]
-    stores.append(pltpu.make_async_copy(o, out, sems.at[6]))
+    summed = pl.ds(0, cw)
+    stores.append(pltpu.make_async_copy(o.at[:, summed], out.at[:, summed], sems.at[4]))
     stores[-1].start()
     f[...] = less_field(jnp.zeros_like(e[1]), e[1])
     stores.append(pltpu.make_async_copy(f, lead, sems.at[7]))
     stores[-1].start()
     for store in stores:
         store.wait()
+
+    @pl.when(lax.axis_index(LAG) == 0)
+    def _():
+        for k, piece in enumerate(pieces):
+            rows = b.at[0, (k + 1) * cut : (k + 2) * cut]
+            pltpu.make_async_copy(rows, piece, sems.at[8 + k]).wait()
 
 
 def later_sums(blocks, before, history, out):
@@ -210,30 +209,21 @@
     work = 2 * rows * size * columns * 2
     small = 2 * cw * rows * span
 
-    before = call(
-        last_of,
-        (history.shape[1:], BF16),
-        0,
-        history,
-        scratch=[pltpu.VMEM(history.shape[1:], BF16), pltpu.SemaphoreType.DMA((2, 4))],
-        held=[pltpu.HBM],
-        given=[pltpu.HBM],
-        limit=60,
-    )
-    before = lax.ppermute(before, LAG, [(i, i + 1) for i in range(nlag - 1)])
-    later = call(later_sums, ((columns, rows), F32), work, blocks, before, history)
-
-    outs = [((nw, cw + own, rows), F32), ((columns, rows), F32)] + [((cut, size), BF16)] * (len(HOLDERS) - 1)
+
+    outs = [((nw, cw + own, rows), F32), ((columns, rows), F32), (history.shape[1:], BF16)]
+    outs += [((cut, size), BF16)] * (len(HOLDERS) - 1)
     scratch = [pltpu.VMEM(blocks.shape, BF16), pltpu.VMEM(history.shape, BF16)]
     scratch += [pltpu.VMEM(excitation.shape, F32), pltpu.VMEM((own, rows), F32)]
     scratch += [pltpu.VMEM(*o) for o in outs[:2]] + [pltpu.SemaphoreType.DMA((7 + len(HOLDERS),))]
     args = blocks, history, excitation, self_inverse
     held, given = [pltpu.HBM] * len(args), [pltpu.HBM] * len(outs)
-    send, lead, *pieces = call(
+    send, lead, last, *pieces = call(
         first_sums, outs, work, *args, scratch=scratch, held=held, given=given, limit=60
     )
+    before = lax.ppermute(last, LAG, [(i, i + 1) for i in range(nlag - 1)])
     got1 = swap(send, W)
     pieces = [lax.ppermute(p, LAG, [(0, w)]) for p, w in zip(pieces, HOLDERS[1:])]
+    later = call(later_sums, ((columns, rows), F32), work, blocks, before, history)
     got1, later = lax.optimization_barrier((got1, later))
     send = call(
         second_step,

time: 105 us -> 104 us (level)
  Pallas kernels: 9.01 us -> 7.33 us
  blocking collectives: 72.3 us -> 73.5 us
    pallas_call x8 -> x7, Pallas kernels: 9.01 us -> 7.33 us  [call(): pl.pallas_call(body, out_shape=shapes[0] if single else shapes, in_specs=...]
    all_to_all x5, blocking collectives: 72.3 us -> 73.5 us  [swap(): return lax.all_to_all(pieces, axes, 0, 0, tiled=True)]
  transfers between devices with their start and end apart: 5 -> 5, of which waited for: 2 -> 2; matrix products, arithmetic and copies ran while one was open for 0% -> 0% of each run, Pallas kernels for 5% -> 2%
where the time goes in v12:
time: 104 us
  blocking collectives  73.5 us (71%)
  starting transfers between devices  16.3 us (16%)
  Pallas kernels  7.33 us (7%)
  waiting for transfers between devices  4 us (4%)
  local copies, waits for them, and re-layouts  1.39 us (1%)
  other arithmetic  1.07 us (1%)
    all_to_all x5, blocking collectives, swap(): return lax.all_to_all(pieces, axes, 0, 0, tiled=True)  73.5 us
    all_to_all x1, starting transfers between devices, swap(): return lax.all_to_all(pieces, axes, 0, 0, tiled=True)  7.81 us
    pallas_call x7, Pallas kernels, call(): pl.pallas_call(body, out_shape=shapes[0] if single else shapes, in_specs=...  7.33 us
    ppermute x1, starting transfers between devices, shards(): before = lax.ppermute(last, LAG, [(i, i + 1) for i in range(nlag - 1)])  4.51 us
    ppermute x3, starting transfers between devices, shards(): lax.ppermute(p, LAG, [(0, w)])  4.02 us
    ppermute x3, waiting for transfers between devices, shards(): lax.ppermute(p, LAG, [(0, w)])  2.42 us
  transfers between devices with their start and end apart: 5, of which 2 were waited for; matrix products, arithmetic and copies ran while one was open for 0% of the time, Pallas kernels for 2%

profile of v12, /device:TPU:1, one launch (start us, length us, event | category | flops | bytes accessed | tf_op | source)
XLA Modules:
  0.0 103.8 jit_solution(6567749559605306814)
XLA Ops:
  0.0 3.7 %shard_map.46 = (f32[8,48,256]{2,1,0:T(8,128)}, f32[128,256]{1,0:T(8,128)}, bf16[2048,128]{1,0:T(8,128)(2,1)}, bf16[64,2048]{1,0:T(8,128)(2,1)}, bf16[64,2048]{1,0:T(8,128)(2,1)}, /*index=5*/bf16[64,2048]{1,0:T(8,128)(2,1)}) custom-call(bf16[2,256,2048]{2,1,0:T(8,128)(2,1)} %blocks.5, bf16[2,2048,128]{2,1,0:T(8,128)(2,1)} %history.3, ...), custom_call_target="tpu_custom_call" | custom-call | flops 268435456 | bytes 5275648 | tf_op jit(solution)/shard_map/pallas_call | solution.py:31
  3.7 4.5 %collective-permute-start = (bf16[2048,128]{1,0:T(8,128)(2,1)}, bf16[2048,128]{1,0:T(8,128)(2,1)}, u32[]{:S(2)}, u32[]{:S(2)}) collective-permute-start(bf16[2048,128]{1,0:T(8,128)(2,1)} %get-tuple-element.19), channel_id=1, source_target_pairs={{0,8},{8,16},{16,24},{24,32},{32,40},{40,48},{48,56},{56,64},{64,7... | collective-permute-start | bytes 1572872 | tf_op jit(solution)/shard_map/ppermute | solution.py:223
  8.2 7.8 %all-to-all-start = ((f32[8,48,256]{2,1,0:T(8,128)}), f32[8,48,256]{2,1,0:T(8,128)S(1)}, u32[]{:S(2)}, u32[]{:S(2)}) async-start(f32[8,48,256]{2,1,0:T(8,128)} %get-tuple-element.18), calls=%async_computation | async-start | bytes 786432 | tf_op jit(solution)/shard_map/all_to_all | solution.py:19
  16.1 1.4 %collective-permute-start.1 = (bf16[64,2048]{1,0:T(8,128)(2,1)}, bf16[64,2048]{1,0:T(8,128)(2,1)}, u32[]{:S(2)}, u32[]{:S(2)}) collective-permute-start(bf16[64,2048]{1,0:T(8,128)(2,1)} %get-tuple-element.21), channel_id=1, source_target_pairs={{0,48},{1,49},{2,50},{3,51},{4,52},{5,53},{6,54},{7,55}} | collective-permute-start | bytes 786440 | tf_op jit(solution)/shard_map/ppermute | solution.py:225
  17.4 1.4 %collective-permute-start.2 = (bf16[64,2048]{1,0:T(8,128)(2,1)}, bf16[64,2048]{1,0:T(8,128)(2,1)}, u32[]{:S(2)}, u32[]{:S(2)}) collective-permute-start(bf16[64,2048]{1,0:T(8,128)(2,1)} %get-tuple-element.22), channel_id=1, source_target_pairs={{0,16},{1,17},{2,18},{3,19},{4,20},{5,21},{6,22},{7,23}} | collective-permute-start | bytes 786440 | tf_op jit(solution)/shard_map/ppermute | solution.py:225
  18.8 1.3 %collective-permute-start.3 = (bf16[64,2048]{1,0:T(8,128)(2,1)}, bf16[64,2048]{1,0:T(8,128)(2,1)}, u32[]{:S(2)}, u32[]{:S(2)}) collective-permute-start(bf16[64,2048]{1,0:T(8,128)(2,1)} %get-tuple-element.23), channel_id=1, source_target_pairs={{0,8},{1,9},{2,10},{3,11},{4,12},{5,13},{6,14},{7,15}} | collective-permute-start | bytes 786440 | tf_op jit(solution)/shard_map/ppermute | solution.py:225
  20.1 1.8 %shard_map.47.later = f32[128,256]{1,0:T(8,128)S(1)} custom-call(bf16[2,256,2048]{2,1,0:T(8,128)(2,1)S(1)} %copy-done, bf16[2048,128]{1,0:T(8,128)(2,1)} %collective-permute-done.before, bf16[2,2048,128]{2,1,0:T(8,128)(2,1)S(1)} %copy-done.1), custom_call_target="tpu_custom_call" | custom-call | flops 268435456 | bytes 3801088 | tf_op jit(solution)/shard_map/pallas_call | solution.py:31
  21.9 0.6 copy-done.2
  22.6 1.6 %all-to-all-done.got.got1 = f32[8,48,256]{2,1,0:T(8,128)S(1)} async-done(((f32[8,48,256]{2,1,0:T(8,128)}), f32[8,48,256]{2,1,0:T(8,128)S(1)}, u32[]{:S(2)}, u32[]{:S(2)}) %all-to-all-start) | async-done | bytes 393248 | tf_op jit(solution)/shard_map/all_to_all | solution.py:19
  24.2 2.4 %collective-permute-done.3.rest_2_ = bf16[64,2048]{1,0:T(8,128)(2,1)} collective-permute-done((bf16[64,2048]{1,0:T(8,128)(2,1)}, bf16[64,2048]{1,0:T(8,128)(2,1)}, u32[]{:S(2)}, u32[]{:S(2)}) %collective-permute-start.3) | collective-permute-done | bytes 262176 | tf_op jit(solution)/shard_map/ppermute | solution.py:225
  26.6 1.0 shard_map.48
  27.6 15.9 %all_to_all.34.got.got2 = bf16[8,96,256]{2,1,0:T(8,128)(2,1)S(1)} all-to-all(bf16[8,96,256]{2,1,0:T(8,128)(2,1)S(1)} %shard_map.48), channel_id=1, replica_groups=mesh['y'=8,'x'=4,'core'=2,'row'=8] {'y'}, dimensions={0} | all-to-all | bytes 786432 | tf_op jit(solution)/shard_map/all_to_all | solution.py:19
  43.5 12.6 %all_to_all.35.got3 = bf16[8,96,256]{2,1,0:T(8,128)(2,1)S(1)} all-to-all(bf16[8,96,256]{2,1,0:T(8,128)(2,1)S(1)} %shard_map.49), channel_id=1, replica_groups=mesh['y'=8,'x'=4,'core'=2,'row'=8] {'x','core'}, dimensions={0} | all-to-all | bytes 786432 | tf_op jit(solution)/shard_map/all_to_all | solution.py:19
  56.1 0.3 shard_map.50
  56.4 17.5 %all_to_all.36.got = f32[8,16,256]{2,1,0:T(8,128)S(1)} all-to-all(f32[8,16,256]{2,1,0:T(8,128)S(1)} %get-tuple-element.26), channel_id=1, replica_groups=mesh['y'=8,'x'=4,'core'=2,'row'=8] {'row'}, dimensions={0} | all-to-all | bytes 262144 | tf_op jit(solution)/shard_map/all_to_all | solution.py:19
  73.9 0.2 shard_map.51
  74.1 10.4 %all_to_all.37.got = f32[8,16,256]{2,1,0:T(8,128)S(1)} all-to-all(f32[8,16,256]{2,1,0:T(8,128)S(1)} %get-tuple-element.29), channel_id=1, replica_groups=mesh['y'=8,'x'=4,'core'=2,'row'=8] {'y'}, dimensions={0} | all-to-all | bytes 262144 | tf_op jit(solution)/shard_map/all_to_all | solution.py:19
  84.5 0.3 shard_map.52
  84.8 0.1 reshape.19
  85.1 0.2 all_to_all.26
  85.2 17.1 %all_to_all.38 = f32[64,1,576]{2,1,0:T(1,128)S(1)} all-to-all(f32[64,1,576]{2,1,0:T(1,128)S(1)} %all_to_all.26), channel_id=1, replica_groups=mesh['y'=8,'x'=4,'core'=2,'row'=8] {'x','core','row'}, dimensions={0} | all-to-all | bytes 294912 | tf_op jit(solution)/shard_map/all_to_all | solution.py:19
  102.4 0.4 reduce
  102.7 0.2 reshape.20
  103.1 0.6 pad_maximum_fusion
  (20 shorter events, 0.4 us)
Async XLA Ops:
  0.0 20.1 %copy-start = (bf16[2,256,2048]{2,1,0:T(8,128)(2,1)S(1)}, bf16[2,256,2048]{2,1,0:T(8,128)(2,1)}, u32[]{:S(2)}) copy-start(bf16[2,256,2048]{2,1,0:T(8,128)(2,1)} %blocks.5) | copy-start | bytes 6291460
  0.0 20.1 %copy-start.1 = (bf16[2,2048,128]{2,1,0:T(8,128)(2,1)S(1)}, bf16[2,2048,128]{2,1,0:T(8,128)(2,1)}, u32[]{:S(2)}) copy-start(bf16[2,2048,128]{2,1,0:T(8,128)(2,1)} %history.3) | copy-start | bytes 3145732
  3.7 16.4 %collective-permute-start = (bf16[2048,128]{1,0:T(8,128)(2,1)}, bf16[2048,128]{1,0:T(8,128)(2,1)}, u32[]{:S(2)}, u32[]{:S(2)}) collective-permute-start(bf16[2048,128]{1,0:T(8,128)(2,1)} %get-tuple-element.19), channel_id=1, source_target_pairs={{0,8},{8,16},{16,24},{24,32},{32,40},{40,48},{48,56},{56,64},{64,7... | collective-permute-start | bytes 1572872 | tf_op jit(solution)/shard_map/ppermute | solution.py:223
  8.2 15.9 %all-to-all-start = ((f32[8,48,256]{2,1,0:T(8,128)}), f32[8,48,256]{2,1,0:T(8,128)S(1)}, u32[]{:S(2)}, u32[]{:S(2)}) async-start(f32[8,48,256]{2,1,0:T(8,128)} %get-tuple-element.18), calls=%async_computation | async-start | bytes 786432 | tf_op jit(solution)/shard_map/all_to_all | solution.py:19
  16.1 8.1 %collective-permute-start.1 = (bf16[64,2048]{1,0:T(8,128)(2,1)}, bf16[64,2048]{1,0:T(8,128)(2,1)}, u32[]{:S(2)}, u32[]{:S(2)}) collective-permute-start(bf16[64,2048]{1,0:T(8,128)(2,1)} %get-tuple-element.21), channel_id=1, source_target_pairs={{0,48},{1,49},{2,50},{3,51},{4,52},{5,53},{6,54},{7,55}} | collective-permute-start | bytes 786440 | tf_op jit(solution)/shard_map/ppermute | solution.py:225
  17.4 6.7 %collective-permute-start.2 = (bf16[64,2048]{1,0:T(8,128)(2,1)}, bf16[64,2048]{1,0:T(8,128)(2,1)}, u32[]{:S(2)}, u32[]{:S(2)}) collective-permute-start(bf16[64,2048]{1,0:T(8,128)(2,1)} %get-tuple-element.22), channel_id=1, source_target_pairs={{0,16},{1,17},{2,18},{3,19},{4,20},{5,21},{6,22},{7,23}} | collective-permute-start | bytes 786440 | tf_op jit(solution)/shard_map/ppermute | solution.py:225
  18.8 7.8 %collective-permute-start.3 = (bf16[64,2048]{1,0:T(8,128)(2,1)}, bf16[64,2048]{1,0:T(8,128)(2,1)}, u32[]{:S(2)}, u32[]{:S(2)}) collective-permute-start(bf16[64,2048]{1,0:T(8,128)(2,1)} %get-tuple-element.23), channel_id=1, source_target_pairs={{0,8},{1,9},{2,10},{3,11},{4,12},{5,13},{6,14},{7,15}} | collective-permute-start | bytes 786440 | tf_op jit(solution)/shard_map/ppermute | solution.py:225
  21.9 0.7 copy-start.2
  22.6 20.9 %copy-start.4 = (f32[128,256]{1,0:T(8,128)S(1)}, f32[128,256]{1,0:T(8,128)}, u32[]{:S(2)}) copy-start(f32[128,256]{1,0:T(8,128)} %get-tuple-element.25.lead) | copy-start | bytes 393220
  24.1 19.3 %copy-start.3 = (f32[128,256]{1,0:T(8,128)S(1)}, f32[128,256]{1,0:T(8,128)}, u32[]{:S(2)}) copy-start(f32[128,256]{1,0:T(8,128)} %copy-done.2) | copy-start | bytes 393220

commit v13 on v12

--- a/solution.py
+++ b/solution.py
@@ -223,6 +223,7 @@
     before = lax.ppermute(last, LAG, [(i, i + 1) for i in range(nlag - 1)])
     got1 = swap(send, W)
     pieces = [lax.ppermute(p, LAG, [(0, w)]) for p, w in zip(pieces, HOLDERS[1:])]
+    got1, before = lax.optimization_barrier((got1, before))
     later = call(later_sums, ((columns, rows), F32), work, blocks, before, history)
     got1, later = lax.optimization_barrier((got1, later))
     send = call(

time: 104 us -> 106 us (1.019)
  blocking collectives: 73.5 us -> 75.4 us
    all_to_all x1, waiting for transfers between devices: 1.57 us -> 4.07 us  [swap(): return lax.all_to_all(pieces, axes, 0, 0, tiled=True)]
    all_to_all x5, blocking collectives: 73.5 us -> 75.4 us  [swap(): return lax.all_to_all(pieces, axes, 0, 0, tiled=True)]
    ppermute x3, waiting for transfers between devices: 2.42 us -> 0.58 us  [shards(): lax.ppermute(p, LAG, [(0, w)])]
where the time goes in v13:
time: 106 us
  blocking collectives  75.4 us (71%)
  starting transfers between devices  16.3 us (15%)
  Pallas kernels  7.35 us (7%)
  waiting for transfers between devices  4.66 us (4%)
  other arithmetic  1.07 us (1%)
    all_to_all x5, blocking collectives, swap(): return lax.all_to_all(pieces, axes, 0, 0, tiled=True)  75.4 us
    all_to_all x1, starting transfers between devices, swap(): return lax.all_to_all(pieces, axes, 0, 0, tiled=True)  7.81 us
    pallas_call x7, Pallas kernels, call(): pl.pallas_call(body, out_shape=shapes[0] if single else shapes, in_specs=...  7.35 us
    ppermute x1, starting transfers between devices, shards(): before = lax.ppermute(last, LAG, [(i, i + 1) for i in range(nlag - 1)])  4.51 us
    all_to_all x1, waiting for transfers between devices, swap(): return lax.all_to_all(pieces, axes, 0, 0, tiled=True)  4.07 us
    ppermute x3, starting transfers between devices, shards(): lax.ppermute(p, LAG, [(0, w)])  4.01 us
  transfers between devices with their start and end apart: 5, of which 2 were waited for; matrix products, arithmetic and copies ran while one was open for 0% of the time, Pallas kernels for 2%

profile of v13, /device:TPU:1, one launch (start us, length us, event | category | flops | bytes accessed | tf_op | source)
XLA Modules:
  0.0 105.6 jit_solution(8057994379553504422)
XLA Ops:
  0.0 3.7 %shard_map.46 = (f32[8,48,256]{2,1,0:T(8,128)}, f32[128,256]{1,0:T(8,128)}, bf16[2048,128]{1,0:T(8,128)(2,1)}, bf16[64,2048]{1,0:T(8,128)(2,1)}, bf16[64,2048]{1,0:T(8,128)(2,1)}, /*index=5*/bf16[64,2048]{1,0:T(8,128)(2,1)}) custom-call(bf16[2,256,2048]{2,1,0:T(8,128)(2,1)} %blocks.5, bf16[2,2048,128]{2,1,0:T(8,128)(2,1)} %history.3, ...), custom_call_target="tpu_custom_call" | custom-call | flops 268435456 | bytes 5275648 | tf_op jit(solution)/shard_map/pallas_call | solution.py:31
  3.7 4.5 %collective-permute-start = (bf16[2048,128]{1,0:T(8,128)(2,1)}, bf16[2048,128]{1,0:T(8,128)(2,1)}, u32[]{:S(2)}, u32[]{:S(2)}) collective-permute-start(bf16[2048,128]{1,0:T(8,128)(2,1)} %get-tuple-element.21), channel_id=1, source_target_pairs={{0,8},{8,16},{16,24},{24,32},{32,40},{40,48},{48,56},{56,64},{64,7... | collective-permute-start | bytes 1572872 | tf_op jit(solution)/shard_map/ppermute | solution.py:223
  8.3 7.8 %all-to-all-start = ((f32[8,48,256]{2,1,0:T(8,128)}), f32[8,48,256]{2,1,0:T(8,128)S(1)}, u32[]{:S(2)}, u32[]{:S(2)}) async-start(f32[8,48,256]{2,1,0:T(8,128)} %get-tuple-element.20), calls=%async_computation | async-start | bytes 786432 | tf_op jit(solution)/shard_map/all_to_all | solution.py:19
  16.1 1.4 %collective-permute-start.1 = (bf16[64,2048]{1,0:T(8,128)(2,1)}, bf16[64,2048]{1,0:T(8,128)(2,1)}, u32[]{:S(2)}, u32[]{:S(2)}) collective-permute-start(bf16[64,2048]{1,0:T(8,128)(2,1)} %get-tuple-element.25), channel_id=1, source_target_pairs={{0,48},{1,49},{2,50},{3,51},{4,52},{5,53},{6,54},{7,55}} | collective-permute-start | bytes 786440 | tf_op jit(solution)/shard_map/ppermute | solution.py:225
  17.4 1.4 %collective-permute-start.2 = (bf16[64,2048]{1,0:T(8,128)(2,1)}, bf16[64,2048]{1,0:T(8,128)(2,1)}, u32[]{:S(2)}, u32[]{:S(2)}) collective-permute-start(bf16[64,2048]{1,0:T(8,128)(2,1)} %get-tuple-element.26), channel_id=1, source_target_pairs={{0,16},{1,17},{2,18},{3,19},{4,20},{5,21},{6,22},{7,23}} | collective-permute-start | bytes 786440 | tf_op jit(solution)/shard_map/ppermute | solution.py:225
  18.8 1.3 %collective-permute-start.3 = (bf16[64,2048]{1,0:T(8,128)(2,1)}, bf16[64,2048]{1,0:T(8,128)(2,1)}, u32[]{:S(2)}, u32[]{:S(2)}) collective-permute-start(bf16[64,2048]{1,0:T(8,128)(2,1)} %get-tuple-element.27), channel_id=1, source_target_pairs={{0,8},{1,9},{2,10},{3,11},{4,12},{5,13},{6,14},{7,15}} | collective-permute-start | bytes 786440 | tf_op jit(solution)/shard_map/ppermute | solution.py:225
  20.1 4.1 %all-to-all-done.got.got1 = f32[8,48,256]{2,1,0:T(8,128)S(1)} async-done(((f32[8,48,256]{2,1,0:T(8,128)}), f32[8,48,256]{2,1,0:T(8,128)S(1)}, u32[]{:S(2)}, u32[]{:S(2)}) %all-to-all-start) | async-done | bytes 393248 | tf_op jit(solution)/shard_map/all_to_all | solution.py:19
  24.2 1.8 %shard_map.47.later = f32[128,256]{1,0:T(8,128)S(1)} custom-call(bf16[2,256,2048]{2,1,0:T(8,128)(2,1)S(1)} %copy-done, bf16[2048,128]{1,0:T(8,128)(2,1)} %collective-permute-done.before, bf16[2,2048,128]{2,1,0:T(8,128)(2,1)S(1)} %copy-done.1), custom_call_target="tpu_custom_call" | custom-call | flops 268435456 | bytes 3801088 | tf_op jit(solution)/shard_map/pallas_call | solution.py:31
  26.0 0.6 collective-permute-done.3.rest_2_
  26.6 1.0 shard_map.48
  27.6 17.6 %all_to_all.34.got.got2 = bf16[8,96,256]{2,1,0:T(8,128)(2,1)S(1)} all-to-all(bf16[8,96,256]{2,1,0:T(8,128)(2,1)S(1)} %shard_map.48), channel_id=1, replica_groups=mesh['y'=8,'x'=4,'core'=2,'row'=8] {'y'}, dimensions={0} | all-to-all | bytes 786432 | tf_op jit(solution)/shard_map/all_to_all | solution.py:19
  45.2 12.6 %all_to_all.35.got3 = bf16[8,96,256]{2,1,0:T(8,128)(2,1)S(1)} all-to-all(bf16[8,96,256]{2,1,0:T(8,128)(2,1)S(1)} %shard_map.49), channel_id=1, replica_groups=mesh['y'=8,'x'=4,'core'=2,'row'=8] {'x','core'}, dimensions={0} | all-to-all | bytes 786432 | tf_op jit(solution)/shard_map/all_to_all | solution.py:19
  57.7 0.3 shard_map.50
  58.1 17.7 %all_to_all.36.got = f32[8,16,256]{2,1,0:T(8,128)S(1)} all-to-all(f32[8,16,256]{2,1,0:T(8,128)S(1)} %get-tuple-element.30), channel_id=1, replica_groups=mesh['y'=8,'x'=4,'core'=2,'row'=8] {'row'}, dimensions={0} | all-to-all | bytes 262144 | tf_op jit(solution)/shard_map/all_to_all | solution.py:19
  75.8 0.2 shard_map.51
  76.0 10.4 %all_to_all.37.got = f32[8,16,256]{2,1,0:T(8,128)S(1)} all-to-all(f32[8,16,256]{2,1,0:T(8,128)S(1)} %get-tuple-element.33), channel_id=1, replica_groups=mesh['y'=8,'x'=4,'core'=2,'row'=8] {'y'}, dimensions={0} | all-to-all | bytes 262144 | tf_op jit(solution)/shard_map/all_to_all | solution.py:19
  86.4 0.3 shard_map.52
  86.7 0.1 reshape.19
  86.8 0.1 broadcast_in_dim.7
  86.9 0.2 all_to_all.26
  87.1 17.1 %all_to_all.38 = f32[64,1,576]{2,1,0:T(1,128)S(1)} all-to-all(f32[64,1,576]{2,1,0:T(1,128)S(1)} %all_to_all.26), channel_id=1, replica_groups=mesh['y'=8,'x'=4,'core'=2,'row'=8] {'x','core','row'}, dimensions={0} | all-to-all | bytes 294912 | tf_op jit(solution)/shard_map/all_to_all | solution.py:19
  104.2 0.4 reduce
  104.6 0.2 reshape.20
  105.0 0.6 pad_maximum_fusion
  (16 shorter events, 0.3 us)
Async XLA Ops:
  0.0 24.2 %copy-start = (bf16[2,256,2048]{2,1,0:T(8,128)(2,1)S(1)}, bf16[2,256,2048]{2,1,0:T(8,128)(2,1)}, u32[]{:S(2)}) copy-start(bf16[2,256,2048]{2,1,0:T(8,128)(2,1)} %blocks.5) | copy-start | bytes 6291460
  0.0 24.2 %copy-start.1 = (bf16[2,2048,128]{2,1,0:T(8,128)(2,1)S(1)}, bf16[2,2048,128]{2,1,0:T(8,128)(2,1)}, u32[]{:S(2)}) copy-start(bf16[2,2048,128]{2,1,0:T(8,128)(2,1)} %history.3) | copy-start | bytes 3145732
  3.7 20.4 %collective-permute-start = (bf16[2048,128]{1,0:T(8,128)(2,1)}, bf16[2048,128]{1,0:T(8,128)(2,1)}, u32[]{:S(2)}, u32[]{:S(2)}) collective-permute-start(bf16[2048,128]{1,0:T(8,128)(2,1)} %get-tuple-element.21), channel_id=1, source_target_pairs={{0,8},{8,16},{16,24},{24,32},{32,40},{40,48},{48,56},{56,64},{64,7... | collective-permute-start | bytes 1572872 | tf_op jit(solution)/shard_map/ppermute | solution.py:223
  8.3 15.9 %all-to-all-start = ((f32[8,48,256]{2,1,0:T(8,128)}), f32[8,48,256]{2,1,0:T(8,128)S(1)}, u32[]{:S(2)}, u32[]{:S(2)}) async-start(f32[8,48,256]{2,1,0:T(8,128)} %get-tuple-element.20), calls=%async_computation | async-start | bytes 786432 | tf_op jit(solution)/shard_map/all_to_all | solution.py:19
  16.1 9.9 %collective-permute-start.1 = (bf16[64,2048]{1,0:T(8,128)(2,1)}, bf16[64,2048]{1,0:T(8,128)(2,1)}, u32[]{:S(2)}, u32[]{:S(2)}) collective-permute-start(bf16[64,2048]{1,0:T(8,128)(2,1)} %get-tuple-element.25), channel_id=1, source_target_pairs={{0,48},{1,49},{2,50},{3,51},{4,52},{5,53},{6,54},{7,55}} | collective-permute-start | bytes 786440 | tf_op jit(solution)/shard_map/ppermute | solution.py:225
  17.4 8.6 %collective-permute-start.2 = (bf16[64,2048]{1,0:T(8,128)(2,1)}, bf16[64,2048]{1,0:T(8,128)(2,1)}, u32[]{:S(2)}, u32[]{:S(2)}) collective-permute-start(bf16[64,2048]{1,0:T(8,128)(2,1)} %get-tuple-element.26), channel_id=1, source_target_pairs={{0,16},{1,17},{2,18},{3,19},{4,20},{5,21},{6,22},{7,23}} | collective-permute-start | bytes 786440 | tf_op jit(solution)/shard_map/ppermute | solution.py:225
  18.8 7.8 %collective-permute-start.3 = (bf16[64,2048]{1,0:T(8,128)(2,1)}, bf16[64,2048]{1,0:T(8,128)(2,1)}, u32[]{:S(2)}, u32[]{:S(2)}) collective-permute-start(bf16[64,2048]{1,0:T(8,128)(2,1)} %get-tuple-element.27), channel_id=1, source_target_pairs={{0,8},{1,9},{2,10},{3,11},{4,12},{5,13},{6,14},{7,15}} | collective-permute-start | bytes 786440 | tf_op jit(solution)/shard_map/ppermute | solution.py:225
  26.0 19.2 %copy-start.2 = (f32[128,256]{1,0:T(8,128)S(1)}, f32[128,256]{1,0:T(8,128)}, u32[]{:S(2)}) copy-start(f32[128,256]{1,0:T(8,128)} %get-tuple-element.29.lead) | copy-start | bytes 393220

commit v14 on v12

--- a/solution.py
+++ b/solution.py
@@ -10,7 +10,7 @@
 
 LAG = ("y", "x", "core")
 W = ("x", "core")
-HOLDERS = (0, 6, 2, 1)
+HOLDERS = (0, 1, 6, 2)
 F32 = jnp.float32
 BF16 = jnp.bfloat16
 

time: 104 us -> 104 us (level)
  waiting for transfers between devices: 4 us -> 1.58 us
  blocking collectives: 73.5 us -> 75.9 us
    ppermute x3, waiting for transfers between devices: 2.42 us -> 0.01 us  [shards(): lax.ppermute(p, LAG, [(0, w)])]
    all_to_all x5, blocking collectives: 73.5 us -> 75.9 us  [swap(): return lax.all_to_all(pieces, axes, 0, 0, tiled=True)]
  transfers between devices with their start and end apart: 5 -> 5, of which waited for: 2 -> 1; matrix products, arithmetic and copies ran while one was open for 0% -> 0% of each run, Pallas kernels for 2% -> 2%
where the time goes in v14:
time: 104 us
  blocking collectives  75.9 us (73%)
  starting transfers between devices  16.4 us (16%)
  Pallas kernels  7.37 us (7%)
  waiting for transfers between devices  1.58 us (2%)
  local copies, waits for them, and re-layouts  1.39 us (1%)
  other arithmetic  1.07 us (1%)
    all_to_all x5, blocking collectives, swap(): return lax.all_to_all(pieces, axes, 0, 0, tiled=True)  75.9 us
    all_to_all x1, starting transfers between devices, swap(): return lax.all_to_all(pieces, axes, 0, 0, tiled=True)  7.81 us
    pallas_call x7, Pallas kernels, call(): pl.pallas_call(body, out_shape=shapes[0] if single else shapes, in_specs=...  7.37 us
    ppermute x1, starting transfers between devices, shards(): before = lax.ppermute(last, LAG, [(i, i + 1) for i in range(nlag - 1)])  4.51 us
    ppermute x3, starting transfers between devices, shards(): lax.ppermute(p, LAG, [(0, w)])  4.05 us
  transfers between devices with their start and end apart: 5, of which 1 were waited for; matrix products, arithmetic and copies ran while one was open for 0% of the time, Pallas kernels for 2%

profile of v14, /device:TPU:1, one launch (start us, length us, event | category | flops | bytes accessed | tf_op | source)
XLA Modules:
  0.0 103.8 jit_solution(3231957135781400732)
XLA Ops:
  0.0 3.7 %shard_map.46 = (f32[8,48,256]{2,1,0:T(8,128)}, f32[128,256]{1,0:T(8,128)}, bf16[2048,128]{1,0:T(8,128)(2,1)}, bf16[64,2048]{1,0:T(8,128)(2,1)}, bf16[64,2048]{1,0:T(8,128)(2,1)}, /*index=5*/bf16[64,2048]{1,0:T(8,128)(2,1)}) custom-call(bf16[2,256,2048]{2,1,0:T(8,128)(2,1)} %blocks.5, bf16[2,2048,128]{2,1,0:T(8,128)(2,1)} %history.3, ...), custom_call_target="tpu_custom_call" | custom-call | flops 268435456 | bytes 5275648 | tf_op jit(solution)/shard_map/pallas_call | solution.py:31
  3.7 4.5 %collective-permute-start = (bf16[2048,128]{1,0:T(8,128)(2,1)}, bf16[2048,128]{1,0:T(8,128)(2,1)}, u32[]{:S(2)}, u32[]{:S(2)}) collective-permute-start(bf16[2048,128]{1,0:T(8,128)(2,1)} %get-tuple-element.19), channel_id=1, source_target_pairs={{0,8},{8,16},{16,24},{24,32},{32,40},{40,48},{48,56},{56,64},{64,7... | collective-permute-start | bytes 1572872 | tf_op jit(solution)/shard_map/ppermute | solution.py:223
  8.2 7.8 %all-to-all-start = ((f32[8,48,256]{2,1,0:T(8,128)}), f32[8,48,256]{2,1,0:T(8,128)S(1)}, u32[]{:S(2)}, u32[]{:S(2)}) async-start(f32[8,48,256]{2,1,0:T(8,128)} %get-tuple-element.18), calls=%async_computation | async-start | bytes 786432 | tf_op jit(solution)/shard_map/all_to_all | solution.py:19
  16.1 1.3 %collective-permute-start.1 = (bf16[64,2048]{1,0:T(8,128)(2,1)}, bf16[64,2048]{1,0:T(8,128)(2,1)}, u32[]{:S(2)}, u32[]{:S(2)}) collective-permute-start(bf16[64,2048]{1,0:T(8,128)(2,1)} %get-tuple-element.21), channel_id=1, source_target_pairs={{0,8},{1,9},{2,10},{3,11},{4,12},{5,13},{6,14},{7,15}} | collective-permute-start | bytes 786440 | tf_op jit(solution)/shard_map/ppermute | solution.py:225
  17.3 1.4 %collective-permute-start.2 = (bf16[64,2048]{1,0:T(8,128)(2,1)}, bf16[64,2048]{1,0:T(8,128)(2,1)}, u32[]{:S(2)}, u32[]{:S(2)}) collective-permute-start(bf16[64,2048]{1,0:T(8,128)(2,1)} %get-tuple-element.22), channel_id=1, source_target_pairs={{0,48},{1,49},{2,50},{3,51},{4,52},{5,53},{6,54},{7,55}} | collective-permute-start | bytes 786440 | tf_op jit(solution)/shard_map/ppermute | solution.py:225
  18.7 1.4 %collective-permute-start.3 = (bf16[64,2048]{1,0:T(8,128)(2,1)}, bf16[64,2048]{1,0:T(8,128)(2,1)}, u32[]{:S(2)}, u32[]{:S(2)}) collective-permute-start(bf16[64,2048]{1,0:T(8,128)(2,1)} %get-tuple-element.23), channel_id=1, source_target_pairs={{0,16},{1,17},{2,18},{3,19},{4,20},{5,21},{6,22},{7,23}} | collective-permute-start | bytes 786440 | tf_op jit(solution)/shard_map/ppermute | solution.py:225
  20.1 1.8 %shard_map.47.later = f32[128,256]{1,0:T(8,128)S(1)} custom-call(bf16[2,256,2048]{2,1,0:T(8,128)(2,1)S(1)} %copy-done, bf16[2048,128]{1,0:T(8,128)(2,1)} %collective-permute-done.before, bf16[2,2048,128]{2,1,0:T(8,128)(2,1)S(1)} %copy-done.1), custom_call_target="tpu_custom_call" | custom-call | flops 268435456 | bytes 3801088 | tf_op jit(solution)/shard_map/pallas_call | solution.py:31
  21.9 0.6 copy-done.2
  22.6 1.6 %all-to-all-done.got.got1 = f32[8,48,256]{2,1,0:T(8,128)S(1)} async-done(((f32[8,48,256]{2,1,0:T(8,128)}), f32[8,48,256]{2,1,0:T(8,128)S(1)}, u32[]{:S(2)}, u32[]{:S(2)}) %all-to-all-start) | async-done | bytes 393248 | tf_op jit(solution)/shard_map/all_to_all | solution.py:19
  24.2 1.0 shard_map.48
  25.2 17.6 %all_to_all.34.got.got2 = bf16[8,96,256]{2,1,0:T(8,128)(2,1)S(1)} all-to-all(bf16[8,96,256]{2,1,0:T(8,128)(2,1)S(1)} %shard_map.48), channel_id=1, replica_groups=mesh['y'=8,'x'=4,'core'=2,'row'=8] {'y'}, dimensions={0} | all-to-all | bytes 786432 | tf_op jit(solution)/shard_map/all_to_all | solution.py:19
  42.9 13.0 %all_to_all.35.got3 = bf16[8,96,256]{2,1,0:T(8,128)(2,1)S(1)} all-to-all(bf16[8,96,256]{2,1,0:T(8,128)(2,1)S(1)} %shard_map.49), channel_id=1, replica_groups=mesh['y'=8,'x'=4,'core'=2,'row'=8] {'x','core'}, dimensions={0} | all-to-all | bytes 786432 | tf_op jit(solution)/shard_map/all_to_all | solution.py:19
  55.9 0.3 shard_map.50
  56.2 17.7 %all_to_all.36.got = f32[8,16,256]{2,1,0:T(8,128)S(1)} all-to-all(f32[8,16,256]{2,1,0:T(8,128)S(1)} %get-tuple-element.26), channel_id=1, replica_groups=mesh['y'=8,'x'=4,'core'=2,'row'=8] {'row'}, dimensions={0} | all-to-all | bytes 262144 | tf_op jit(solution)/shard_map/all_to_all | solution.py:19
  73.9 0.2 shard_map.51
  74.1 10.4 %all_to_all.37.got = f32[8,16,256]{2,1,0:T(8,128)S(1)} all-to-all(f32[8,16,256]{2,1,0:T(8,128)S(1)} %get-tuple-element.29), channel_id=1, replica_groups=mesh['y'=8,'x'=4,'core'=2,'row'=8] {'y'}, dimensions={0} | all-to-all | bytes 262144 | tf_op jit(solution)/shard_map/all_to_all | solution.py:19
  84.5 0.3 shard_map.52
  84.8 0.1 reshape.19
  85.0 0.1 broadcast_in_dim.7
  85.1 0.2 all_to_all.26
  85.2 17.1 %all_to_all.38 = f32[64,1,576]{2,1,0:T(1,128)S(1)} all-to-all(f32[64,1,576]{2,1,0:T(1,128)S(1)} %all_to_all.26), channel_id=1, replica_groups=mesh['y'=8,'x'=4,'core'=2,'row'=8] {'x','core','row'}, dimensions={0} | all-to-all | bytes 294912 | tf_op jit(solution)/shard_map/all_to_all | solution.py:19
  102.3 0.4 reduce
  102.7 0.2 reshape.20
  103.1 0.6 pad_maximum_fusion
  (20 shorter events, 0.3 us)
Async XLA Ops:
  0.0 20.1 %copy-start = (bf16[2,256,2048]{2,1,0:T(8,128)(2,1)S(1)}, bf16[2,256,2048]{2,1,0:T(8,128)(2,1)}, u32[]{:S(2)}) copy-start(bf16[2,256,2048]{2,1,0:T(8,128)(2,1)} %blocks.5) | copy-start | bytes 6291460
  0.0 20.1 %copy-start.1 = (bf16[2,2048,128]{2,1,0:T(8,128)(2,1)S(1)}, bf16[2,2048,128]{2,1,0:T(8,128)(2,1)}, u32[]{:S(2)}) copy-start(bf16[2,2048,128]{2,1,0:T(8,128)(2,1)} %history.3) | copy-start | bytes 3145732
  3.7 16.4 %collective-permute-start = (bf16[2048,128]{1,0:T(8,128)(2,1)}, bf16[2048,128]{1,0:T(8,128)(2,1)}, u32[]{:S(2)}, u32[]{:S(2)}) collective-permute-start(bf16[2048,128]{1,0:T(8,128)(2,1)} %get-tuple-element.19), channel_id=1, source_target_pairs={{0,8},{8,16},{16,24},{24,32},{32,40},{40,48},{48,56},{56,64},{64,7... | collective-permute-start | bytes 1572872 | tf_op jit(solution)/shard_map/ppermute | solution.py:223
  8.2 15.9 %all-to-all-start = ((f32[8,48,256]{2,1,0:T(8,128)}), f32[8,48,256]{2,1,0:T(8,128)S(1)}, u32[]{:S(2)}, u32[]{:S(2)}) async-start(f32[8,48,256]{2,1,0:T(8,128)} %get-tuple-element.18), calls=%async_computation | async-start | bytes 786432 | tf_op jit(solution)/shard_map/all_to_all | solution.py:19
  16.1 8.1 %collective-permute-start.1 = (bf16[64,2048]{1,0:T(8,128)(2,1)}, bf16[64,2048]{1,0:T(8,128)(2,1)}, u32[]{:S(2)}, u32[]{:S(2)}) collective-permute-start(bf16[64,2048]{1,0:T(8,128)(2,1)} %get-tuple-element.21), channel_id=1, source_target_pairs={{0,8},{1,9},{2,10},{3,11},{4,12},{5,13},{6,14},{7,15}} | collective-permute-start | bytes 786440 | tf_op jit(solution)/shard_map/ppermute | solution.py:225
  17.3 6.8 %collective-permute-start.2 = (bf16[64,2048]{1,0:T(8,128)(2,1)}, bf16[64,2048]{1,0:T(8,128)(2,1)}, u32[]{:S(2)}, u32[]{:S(2)}) collective-permute-start(bf16[64,2048]{1,0:T(8,128)(2,1)} %get-tuple-element.22), channel_id=1, source_target_pairs={{0,48},{1,49},{2,50},{3,51},{4,52},{5,53},{6,54},{7,55}} | collective-permute-start | bytes 786440 | tf_op jit(solution)/shard_map/ppermute | solution.py:225
  18.7 5.4 %collective-permute-start.3 = (bf16[64,2048]{1,0:T(8,128)(2,1)}, bf16[64,2048]{1,0:T(8,128)(2,1)}, u32[]{:S(2)}, u32[]{:S(2)}) collective-permute-start(bf16[64,2048]{1,0:T(8,128)(2,1)} %get-tuple-element.23), channel_id=1, source_target_pairs={{0,16},{1,17},{2,18},{3,19},{4,20},{5,21},{6,22},{7,23}} | collective-permute-start | bytes 786440 | tf_op jit(solution)/shard_map/ppermute | solution.py:225
  21.9 0.7 copy-start.2
  22.6 20.3 %copy-start.4 = (f32[128,256]{1,0:T(8,128)S(1)}, f32[128,256]{1,0:T(8,128)}, u32[]{:S(2)}) copy-start(f32[128,256]{1,0:T(8,128)} %get-tuple-element.25.lead) | copy-start | bytes 393220
  24.1 18.7 %copy-start.3 = (f32[128,256]{1,0:T(8,128)S(1)}, f32[128,256]{1,0:T(8,128)}, u32[]{:S(2)}) copy-start(f32[128,256]{1,0:T(8,128)} %copy-done.2) | copy-start | bytes 393220
